TPU v7x, 512 devices: a whole 4x8x8 slice. The times are simulated.
512 devices in a mesh: dom: 64 (over z, x, core), band: 8 (over y).
Axes of the slice: x: 4, y: 8, z: 8, core: 2. Of those that a mesh axis runs over, the one named last changes fastest.
Arguments:
- orbitals: float32 [256, 64, 6, 512], P('band', 'dom'), may hold values from -6 to 6
- potential: float32 [64, 6, 512], P('dom'), may hold values from -1 to 1
- proj_shape: float32 [64, 64, 6, 512], P(None, 'dom'), may hold values from -4 to 4
- proj_strength: float32 [64], replicated, may hold values from -6 to -2
- atom_z: int32 [64], replicated, may hold values from 0 to 38
- atom_x: int32 [64], replicated, may hold values from 0 to 54
- atom_y: int32 [64], replicated, may hold values from 0 to 54
Outputs:
- rotated: float32 [256, 64, 6, 512], P('band', 'dom')
- projected: float32 [256, 256], P('band')
All inputs are finite; a program needn't handle non-finite values.
Results may differ from a plain program's by a relative error of at most 0.0003.
Values sent between devices are 32-bit elements; how exact they have to be, the bound alone decides.
No kernel may reach another device: no remote copies, remote signals or barrier semaphores. Data moves between devices by JAX's collectives and lax.ppermute only.
A program may use at most 64 MiB of HBM per device.

v0:
```python
import jax
import jax.numpy as jnp
from jax import lax
from jax.sharding import PartitionSpec as P

XBLOCKS = 8
NY = 64
DEGREE = 4
SPAN = 10
PROJ_CELLS = 1000


COEFFS = [
    -5369.0 / 1800.0,
    12.0 / 7.0,
    -15.0 / 56.0,
    10.0 / 189.0,
    -1.0 / 112.0,
    2.0 / 1925.0,
    -1.0 / 16632.0,
]
CENTER_VALUE = 9.5
HALF_WIDTH = 6.5


def from_behind(shard, axis, by):
    peers = lax.axis_size(axis)
    pairs = [(i, i + by) for i in range(peers) if 0 <= i + by < peers]
    return lax.ppermute(shard, axis, pairs)


def extend_planes(values):
    below = from_behind(values, "dom", XBLOCKS)
    above = from_behind(values, "dom", -XBLOCKS)
    return jnp.concatenate([below, values, above], axis=1)


def extend_rows(values):
    row_cells = 6 * NY
    x_block = lax.axis_index("dom") % XBLOCKS
    before = from_behind(values[:, :, -row_cells:], "dom", 1)
    after = from_behind(values[:, :, :row_cells], "dom", -1)
    before = jnp.where(x_block > 0, before, 0.0)
    after = jnp.where(x_block < XBLOCKS - 1, after, 0.0)
    return jnp.concatenate([before, values, after], axis=2)


def local_part(values, planes_ext, rows_ext, potential):
    depth = values.shape[1]
    width = values.shape[2]
    widened = jnp.pad(values, ((0, 0), (0, 0), (6, 6)))
    column = jnp.arange(width) % NY
    summed = 3.0 * COEFFS[0] * values
    for offset in range(1, 7):
        along_z = (
            planes_ext[:, 6 + offset : 6 + offset + depth]
            + planes_ext[:, 6 - offset : 6 - offset + depth]
        )
        along_x = (
            rows_ext[:, :, (6 + offset) * NY : (6 + offset) * NY + width]
            + rows_ext[:, :, (6 - offset) * NY : (6 - offset) * NY + width]
        )
        upward = jnp.where(
            column + offset < NY, widened[:, :, 6 + offset : 6 + offset + width], 0.0
        )
        downward = jnp.where(
            column - offset >= 0, widened[:, :, 6 - offset : 6 - offset + width], 0.0
        )
        summed = summed + COEFFS[offset] * (along_z + along_x + upward + downward)
    return -0.5 * summed + potential[None] * values


def hamiltonian_apply(values, potential, projector, scaled_strength):
    planes_ext = extend_planes(values)
    rows_ext = extend_rows(values)
    result = local_part(values, planes_ext, rows_ext, potential)
    correlations = jnp.einsum("azc,bzc->ab", projector, values, precision=lax.Precision.HIGHEST)
    correlations = lax.psum(correlations, "dom")
    return result + jnp.einsum(
        "ab,azc->bzc",
        correlations * scaled_strength[:, None],
        projector,
        precision=lax.Precision.HIGHEST,
    )


def on_device(orbitals, potential, proj_shape, proj_strength, atom_z, atom_x, atom_y):
    start_values = orbitals[:, 0]
    field_potential = potential[0]
    shapes = proj_shape[:, 0]
    block_bands = start_values.shape[0]
    depth = start_values.shape[1]
    width = start_values.shape[2]
    total_bands = block_bands * lax.axis_size("band")
    ncells_all = lax.axis_size("dom") * depth * width
    position = lax.axis_index("dom")
    flat_cell = jnp.arange(width)
    z_cell = position // XBLOCKS * depth + jnp.arange(depth)
    x_cell = position % XBLOCKS * (width // NY) + flat_cell // NY
    y_cell = flat_cell % NY
    in_z = (z_cell[None, :] >= atom_z[:, None]) & (z_cell[None, :] < atom_z[:, None] + SPAN)
    in_x = (x_cell[None, :] >= atom_x[:, None]) & (x_cell[None, :] < atom_x[:, None] + SPAN)
    in_y = (y_cell[None, :] >= atom_y[:, None]) & (y_cell[None, :] < atom_y[:, None] + SPAN)
    inside = in_z[:, :, None] & (in_x & in_y)[:, None, :]
    projector = jnp.where(inside, shapes, 0.0)
    scaled_strength = proj_strength / PROJ_CELLS
    previous = start_values
    current = (
        hamiltonian_apply(previous, field_potential, projector, scaled_strength)
        - CENTER_VALUE * previous
    ) / HALF_WIDTH
    for repeat in range(DEGREE - 1):
        following = (
            2.0
            * (
                hamiltonian_apply(current, field_potential, projector, scaled_strength)
                - CENTER_VALUE * current
            )
            / HALF_WIDTH
            - previous
        )
        previous = current
        current = following
    image = hamiltonian_apply(current, field_potential, projector, scaled_strength)
    all_filtered, all_images = (
        lax.all_gather(current, "band", axis=0, tiled=True),
        lax.all_gather(image, "band", axis=0, tiled=True),
    )
    ham_rows = jnp.einsum("izc,jzc->ij", current, all_images, precision=lax.Precision.HIGHEST)
    ovl_rows = jnp.einsum("izc,jzc->ij", current, all_filtered, precision=lax.Precision.HIGHEST)
    own_start = lax.axis_index("band") * block_bands
    empty_full = jnp.zeros((total_bands, total_bands), jnp.float32)
    ham_padded = lax.dynamic_update_slice_in_dim(empty_full, ham_rows, own_start, 0)
    ovl_padded = lax.dynamic_update_slice_in_dim(empty_full, ovl_rows, own_start, 0)
    ham_full, ovl_full = lax.psum((ham_padded, ovl_padded), ("dom", "band"))
    hamiltonian = ham_full / ncells_all
    correlation = ovl_full / ncells_all
    lower_factor = jnp.linalg.cholesky(correlation)
    identity = jnp.eye(total_bands, dtype=jnp.float32)
    inverse = lax.linalg.triangular_solve(lower_factor, identity, left_side=True, lower=True)
    projected_full = jnp.dot(
        jnp.dot(inverse, hamiltonian, precision=lax.Precision.HIGHEST),
        inverse.T,
        precision=lax.Precision.HIGHEST,
    )
    projected = lax.dynamic_slice_in_dim(projected_full, own_start, block_bands, 0)
    coefficient = lax.dynamic_slice_in_dim(inverse, own_start, block_bands, 0)
    rotated = jnp.einsum("ij,jzc->izc", coefficient, all_filtered, precision=lax.Precision.HIGHEST)
    return (rotated[:, None], projected)


def solution(mesh):
    return jax.shard_map(
        on_device,
        mesh=mesh,
        in_specs=(
            P("band", "dom", None, None),
            P("dom", None, None),
            P(None, "dom", None, None),
            P(),
            P(),
            P(),
            P(),
        ),
        out_specs=(P("band", "dom", None, None), P("band", None)),
        check_vma=False,
    )
```

profile of v0, /device:TPU:1, one launch (start us, length us, event | category | flops | bytes accessed | tf_op | source)
XLA Modules:
  0.0 1756.5 jit_solution(13044437370495542397)
XLA Ops:
  9.7 6.2 collective-permute-start.1
  19.9 5.2 collective-permute-start.2
  31.0 244.3 %psum.49 = f32[64,32]{0,1:T(8,128)S(1)} all-reduce(f32[64,32]{0,1:T(8,128)S(1)} %convolution_bitcast_fusion.7), channel_id=1, replica_groups=mesh['dom'=64,'band'=8] {'dom'}, use_global_device_ids=true, to_apply=%region_0.1 | all-reduce | flops 2048 | bytes 16384 | tf_op jit(solution)/shard_map/psum | solution.py:78
  284.8 4.7 collective-permute-start.5
  289.6 5.8 collective-permute-start.6
  296.3 241.0 %psum.50 = f32[64,32]{0,1:T(8,128)S(1)} all-reduce(f32[64,32]{0,1:T(8,128)S(1)} %convolution_bitcast_fusion.6), channel_id=1, replica_groups=mesh['dom'=64,'band'=8] {'dom'}, use_global_device_ids=true, to_apply=%region_1.2 | all-reduce | flops 2048 | bytes 16384 | tf_op jit(solution)/shard_map/psum | solution.py:78
  537.4 4.8 fusion.8
  547.1 4.7 collective-permute-start.9
  551.9 5.8 collective-permute-start.10
  558.6 241.0 %psum.51 = f32[64,32]{0,1:T(8,128)S(1)} all-reduce(f32[64,32]{0,1:T(8,128)S(1)} %convolution_bitcast_fusion.5), channel_id=1, replica_groups=mesh['dom'=64,'band'=8] {'dom'}, use_global_device_ids=true, to_apply=%region_2.3 | all-reduce | flops 2048 | bytes 16384 | tf_op jit(solution)/shard_map/psum | solution.py:78
  799.6 4.8 fusion.5
  809.4 4.7 collective-permute-start.13
  814.1 5.8 collective-permute-start.14
  820.8 241.4 %psum.52 = f32[64,32]{0,1:T(8,128)S(1)} all-reduce(f32[64,32]{0,1:T(8,128)S(1)} %convolution_bitcast_fusion.4), channel_id=1, replica_groups=mesh['dom'=64,'band'=8] {'dom'}, use_global_device_ids=true, to_apply=%region_3.4 | all-reduce | flops 2048 | bytes 16384 | tf_op jit(solution)/shard_map/psum | solution.py:78
  1062.4 5.0 fusion.2
  1077.5 5.8 collective-permute-start.18
  1085.2 241.0 %psum.54 = f32[64,32]{0,1:T(8,128)S(1)} all-reduce(f32[64,32]{0,1:T(8,128)S(1)} %convolution_bitcast_fusion.3), channel_id=1, replica_groups=mesh['dom'=64,'band'=8] {'dom'}, use_global_device_ids=true, to_apply=%region_9.10 | all-reduce | flops 2048 | bytes 16384 | tf_op jit(solution)/shard_map/psum | solution.py:78
  1329.7 4.5 convolution_bitcast_fusion.2
  1335.3 67.4 %all-gather.5.cloned.1.call-done = f32[256,6,512]{2,0,1:T(8,128)} async-done(((f32[32,6,512]{2,0,1:T(8,128)}), f32[256,6,512]{2,0,1:T(8,128)}) %all-gather.5.cloned.1.call-update) | async-done | bytes 3145744 | tf_op jit(solution)/shard_map/all_gather | solution.py:127
  1409.2 269.9 %all-reduce.9.cloned.1.call-done = (f32[256,256]{0,1:T(8,128)}, f32[256,256]{0,1:T(8,128)}) async-done(((f32[256,256]{0,1:T(8,128)}, f32[256,256]{0,1:T(8,128)}), (f32[256,256]{0,1:T(8,128)}, f32[256,256]{0,1:T(8,128)})) %all-reduce.9.cloned.1.call-update) | async-done | bytes 524304 | tf_op jit(solution)/shard_map/psum | solution.py:135
  1681.2 11.7 cholesky.49
  1693.0 9.8 custom-call.14
  1703.3 11.7 cholesky.103
  1722.5 19.9 %custom-call.15 = f32[2,128,128]{1,2,0:T(8,128)S(1)} custom-call(f32[2,128,128]{2,1,0:T(8,128)S(1)} %get-tuple-element.9), custom_call_target="InvertDiagBlocksLowerTriangular" | custom-call | tf_op jit(solution)/shard_map/triangular_solve | solution.py:140
  (135 shorter events, 77.8 us)
Async XLA Ops:
  7.2 268.2 %copy-start = (f32[64,1,6,512]{3,1,2,0:T(1,128)S(1)}, f32[64,1,6,512]{3,1,2,0:T(1,128)}, u32[]{:S(2)}) copy-start(f32[64,1,6,512]{3,1,2,0:T(1,128)} %param.9) | copy-start | bytes 2359300
  7.2 1322.5 %all-gather.3.cloned.1.call-start = ((), (), s32[]{:S(2)}) async-start(), calls=%async_computation | async-start | bytes 3538944 | tf_op jit(solution)/shard_map/all_gather | solution.py:126
  8.4 266.9 %collective-permute-start = (f32[32,6,512]{2,0,1:T(8,128)S(1)}, f32[32,6,512]{2,0,1:T(8,128)S(1)}, u32[]{:S(2)}, u32[]{:S(2)}) collective-permute-start(f32[32,6,512]{2,0,1:T(8,128)S(1)} %bitcast.99), channel_id=1, source_target_pairs={{64,0},{72,8},{80,16},{88,24},{96,32},{104,40},{112,48},{120,56},{... | collective-permute-start | bytes 1179656 | tf_op jit(solution)/shard_map/ppermute | solution.py:29
  9.7 265.6 %collective-permute-start.1 = (f32[32,6,512]{2,0,1:T(8,128)S(1)}, f32[32,6,512]{2,0,1:T(8,128)}, u32[]{:S(2)}, u32[]{:S(2)}) collective-permute-start(f32[32,6,512]{2,0,1:T(8,128)S(1)} %bitcast.100), channel_id=1, source_target_pairs={{0,64},{8,72},{16,80},{24,88},{32,96},{40,104},{48,112},{56,120},{... | collective-permute-start | bytes 1179656 | tf_op jit(solution)/shard_map/ppermute | solution.py:29
  15.9 259.3 %collective-permute-start.3 = (f32[32,6,384]{2,0,1:T(8,128)S(1)}, f32[32,6,384]{2,0,1:T(8,128)S(1)}, u32[]{:S(2)}, u32[]{:S(2)}) collective-permute-start(f32[32,6,384]{2,0,1:T(8,128)S(1)} %get-tuple-element.43), channel_id=1, source_target_pairs={{0,8},{8,16},{16,24},{24,32},{32,40},{40,48},{48,56},{56,64},{64,7... | collective-permute-start | bytes 884744 | tf_op jit(solution)/shard_map/ppermute | solution.py:29
  19.9 255.4 %collective-permute-start.2 = (f32[32,6,384]{2,0,1:T(8,128)S(1)}, f32[32,6,384]{2,0,1:T(8,128)S(1)}, u32[]{:S(2)}, u32[]{:S(2)}) collective-permute-start(f32[32,6,384]{2,0,1:T(8,128)S(1)} %get-tuple-element.42), channel_id=1, source_target_pairs={{8,0},{16,8},{24,16},{32,24},{40,32},{48,40},{56,48},{64,56},{72,6... | collective-permute-start | bytes 884744 | tf_op jit(solution)/shard_map/ppermute | solution.py:29
  279.8 257.5 %collective-permute-start.7 = (f32[32,6,384]{2,0,1:T(8,128)S(1)}, f32[32,6,384]{2,0,1:T(8,128)S(1)}, u32[]{:S(2)}, u32[]{:S(2)}) collective-permute-start(f32[32,6,384]{2,0,1:T(8,128)S(1)} %get-tuple-element.41), channel_id=1, source_target_pairs={{0,8},{8,16},{16,24},{24,32},{32,40},{40,48},{48,56},{56,64},{64,7... | collective-permute-start | bytes 884744 | tf_op jit(solution)/shard_map/ppermute | solution.py:29
  283.5 253.8 %collective-permute-start.4 = (f32[32,6,512]{2,0,1:T(8,128)S(1)}, f32[32,6,512]{2,0,1:T(8,128)}, u32[]{:S(2)}, u32[]{:S(2)}) collective-permute-start(f32[32,6,512]{2,0,1:T(8,128)S(1)} %get-tuple-element.46), channel_id=1, source_target_pairs={{64,0},{72,8},{80,16},{88,24},{96,32},{104,40},{112,48},{120,56},{... | collective-permute-start | bytes 1179656 | tf_op jit(solution)/shard_map/ppermute | solution.py:29
  284.8 252.5 %collective-permute-start.5 = (f32[32,6,512]{2,0,1:T(8,128)S(1)}, f32[32,6,512]{2,0,1:T(8,128)}, u32[]{:S(2)}, u32[]{:S(2)}) collective-permute-start(f32[32,6,512]{2,0,1:T(8,128)S(1)} %get-tuple-element.46), channel_id=1, source_target_pairs={{0,64},{8,72},{16,80},{24,88},{32,96},{40,104},{48,112},{56,120},{... | collective-permute-start | bytes 1179656 | tf_op jit(solution)/shard_map/ppermute | solution.py:29
  289.6 247.7 %collective-permute-start.6 = (f32[32,6,384]{2,0,1:T(8,128)S(1)}, f32[32,6,384]{2,0,1:T(8,128)S(1)}, u32[]{:S(2)}, u32[]{:S(2)}) collective-permute-start(f32[32,6,384]{2,0,1:T(8,128)S(1)} %get-tuple-element.40), channel_id=1, source_target_pairs={{8,0},{16,8},{24,16},{32,24},{40,32},{48,40},{56,48},{64,56},{72,6... | collective-permute-start | bytes 884744 | tf_op jit(solution)/shard_map/ppermute | solution.py:29
  542.2 257.3 %collective-permute-start.11 = (f32[32,6,384]{2,0,1:T(8,128)S(1)}, f32[32,6,384]{2,0,1:T(8,128)S(1)}, u32[]{:S(2)}, u32[]{:S(2)}) collective-permute-start(f32[32,6,384]{2,0,1:T(8,128)S(1)} %get-tuple-element.39), channel_id=1, source_target_pairs={{0,8},{8,16},{16,24},{24,32},{32,40},{40,48},{48,56},{56,64},{64,7... | collective-permute-start | bytes 884744 | tf_op jit(solution)/shard_map/ppermute | solution.py:29
  545.8 253.8 %collective-permute-start.8 = (f32[32,6,512]{2,0,1:T(8,128)S(1)}, f32[32,6,512]{2,0,1:T(8,128)}, u32[]{:S(2)}, u32[]{:S(2)}) collective-permute-start(f32[32,6,512]{2,0,1:T(8,128)S(1)} %fusion.8), channel_id=1, source_target_pairs={{64,0},{72,8},{80,16},{88,24},{96,32},{104,40},{112,48},{120,56},{... | collective-permute-start | bytes 1179656 | tf_op jit(solution)/shard_map/ppermute | solution.py:29
  547.1 252.5 %collective-permute-start.9 = (f32[32,6,512]{2,0,1:T(8,128)S(1)}, f32[32,6,512]{2,0,1:T(8,128)}, u32[]{:S(2)}, u32[]{:S(2)}) collective-permute-start(f32[32,6,512]{2,0,1:T(8,128)S(1)} %fusion.8), channel_id=1, source_target_pairs={{0,64},{8,72},{16,80},{24,88},{32,96},{40,104},{48,112},{56,120},{... | collective-permute-start | bytes 1179656 | tf_op jit(solution)/shard_map/ppermute | solution.py:29
  551.9 247.7 %collective-permute-start.10 = (f32[32,6,384]{2,0,1:T(8,128)S(1)}, f32[32,6,384]{2,0,1:T(8,128)S(1)}, u32[]{:S(2)}, u32[]{:S(2)}) collective-permute-start(f32[32,6,384]{2,0,1:T(8,128)S(1)} %get-tuple-element.38), channel_id=1, source_target_pairs={{8,0},{16,8},{24,16},{32,24},{40,32},{48,40},{56,48},{64,56},{72,6... | collective-permute-start | bytes 884744 | tf_op jit(solution)/shard_map/ppermute | solution.py:29
  804.5 257.8 %collective-permute-start.15 = (f32[32,6,384]{2,0,1:T(8,128)S(1)}, f32[32,6,384]{2,0,1:T(8,128)S(1)}, u32[]{:S(2)}, u32[]{:S(2)}) collective-permute-start(f32[32,6,384]{2,0,1:T(8,128)S(1)} %get-tuple-element.37), channel_id=1, source_target_pairs={{0,8},{8,16},{16,24},{24,32},{32,40},{40,48},{48,56},{56,64},{64,7... | collective-permute-start | bytes 884744 | tf_op jit(solution)/shard_map/ppermute | solution.py:29
  808.1 254.3 %collective-permute-start.12 = (f32[32,6,512]{2,0,1:T(8,128)S(1)}, f32[32,6,512]{2,0,1:T(8,128)S(1)}, u32[]{:S(2)}, u32[]{:S(2)}) collective-permute-start(f32[32,6,512]{2,0,1:T(8,128)S(1)} %fusion.5), channel_id=1, source_target_pairs={{64,0},{72,8},{80,16},{88,24},{96,32},{104,40},{112,48},{120,56},{... | collective-permute-start | bytes 1179656 | tf_op jit(solution)/shard_map/ppermute | solution.py:29
  809.4 253.0 %collective-permute-start.13 = (f32[32,6,512]{2,0,1:T(8,128)S(1)}, f32[32,6,512]{2,0,1:T(8,128)}, u32[]{:S(2)}, u32[]{:S(2)}) collective-permute-start(f32[32,6,512]{2,0,1:T(8,128)S(1)} %fusion.5), channel_id=1, source_target_pairs={{0,64},{8,72},{16,80},{24,88},{32,96},{40,104},{48,112},{56,120},{... | collective-permute-start | bytes 1179656 | tf_op jit(solution)/shard_map/ppermute | solution.py:29
  814.1 248.2 %collective-permute-start.14 = (f32[32,6,384]{2,0,1:T(8,128)S(1)}, f32[32,6,384]{2,0,1:T(8,128)S(1)}, u32[]{:S(2)}, u32[]{:S(2)}) collective-permute-start(f32[32,6,384]{2,0,1:T(8,128)S(1)} %get-tuple-element.36), channel_id=1, source_target_pairs={{8,0},{16,8},{24,16},{32,24},{40,32},{48,40},{56,48},{64,56},{72,6... | collective-permute-start | bytes 884744 | tf_op jit(solution)/shard_map/ppermute | solution.py:29
  1067.4 335.3 %all-gather.5.cloned.1.call-start = ((), (), s32[]{:S(2)}) async-start(), calls=%async_computation.1 | async-start | bytes 3538944 | tf_op jit(solution)/shard_map/all_gather | solution.py:127
  1068.6 257.6 %collective-permute-start.19 = (f32[32,6,384]{2,0,1:T(8,128)S(1)}, f32[32,6,384]{2,0,1:T(8,128)S(1)}, u32[]{:S(2)}, u32[]{:S(2)}) collective-permute-start(f32[32,6,384]{2,0,1:T(8,128)S(1)} %get-tuple-element.35), channel_id=1, source_target_pairs={{0,8},{8,16},{16,24},{24,32},{32,40},{40,48},{48,56},{56,64},{64,7... | collective-permute-start | bytes 884744 | tf_op jit(solution)/shard_map/ppermute | solution.py:29
  1072.2 254.1 %collective-permute-start.16 = (f32[32,6,512]{2,0,1:T(8,128)}, f32[32,6,512]{2,0,1:T(8,128)S(1)}, u32[]{:S(2)}, u32[]{:S(2)}) collective-permute-start(f32[32,6,512]{2,0,1:T(8,128)} %fusion.2), channel_id=1, source_target_pairs={{64,0},{72,8},{80,16},{88,24},{96,32},{104,40},{112,48},{120,56},{... | collective-permute-start | bytes 1179656 | tf_op jit(solution)/shard_map/ppermute | solution.py:29
  1073.5 252.8 %collective-permute-start.17 = (f32[32,6,512]{2,0,1:T(8,128)}, f32[32,6,512]{2,0,1:T(8,128)S(1)}, u32[]{:S(2)}, u32[]{:S(2)}) collective-permute-start(f32[32,6,512]{2,0,1:T(8,128)} %fusion.2), channel_id=1, source_target_pairs={{0,64},{8,72},{16,80},{24,88},{32,96},{40,104},{48,112},{56,120},{... | collective-permute-start | bytes 1179656 | tf_op jit(solution)/shard_map/ppermute | solution.py:29
  1077.5 248.7 %collective-permute-start.18 = (f32[32,6,384]{2,0,1:T(8,128)S(1)}, f32[32,6,384]{2,0,1:T(8,128)S(1)}, u32[]{:S(2)}, u32[]{:S(2)}) collective-permute-start(f32[32,6,384]{2,0,1:T(8,128)S(1)} %get-tuple-element.34), channel_id=1, source_target_pairs={{8,0},{16,8},{24,16},{32,24},{40,32},{48,40},{56,48},{64,56},{72,6... | collective-permute-start | bytes 884744 | tf_op jit(solution)/shard_map/ppermute | solution.py:29
  1329.6 349.4 %all-reduce.9.cloned.1.call-start = ((), (), s32[]{:S(2)}) async-start(), calls=%async_computation.2 | async-start | bytes 1048576 | tf_op jit(solution)/shard_map/psum | solution.py:135
  (6 other events, 677.3 us)
Sparse Core Ops, SparseCore 0:
  1067.5 66.9 all-gather.2
  1329.8 72.8 all-gather.4
  1409.3 269.7 all-reduce.8
where the time goes:
time: 1770 us; the launch traced here: 1760 us
  blocking collectives  1210 us (68%)
  waiting for transfers between devices  337 us (19%)
  starting transfers between devices  78 us (4%)
  other arithmetic  60.4 us (3%)
  matrix products  43.9 us (2%)
    psum x5, blocking collectives, hamiltonian_apply(): correlations = lax.psum(correlations, 'dom')  1210 us
    psum x1, waiting for transfers between devices, on_device(): ham_full, ovl_full = lax.psum((ham_padded, ovl_padded), ('dom', 'band'))  270 us
    ppermute x20, starting transfers between devices, from_behind(): return lax.ppermute(shard, axis, pairs)  77.9 us
    all_gather x1, waiting for transfers between devices, on_device(): lax.all_gather(image, 'band', axis=0, tiled=True)  67.4 us
  transfers between devices with their start and end apart: 23, of which 2 were waited for; matrix products, arithmetic and copies ran while one was open for 1% of the time, Pallas kernels for 0%

commit v1 on v0

v1 whole, which is shorter than its diff:
```python
import jax
import jax.numpy as jnp
import numpy as np
from jax import lax
from jax.experimental import pallas as pl
from jax.experimental.pallas import tpu as pltpu
from jax.sharding import PartitionSpec as P

NY = 64
NCELLS = 196608
PROJ_CELLS = 1000
COEFFS = [
    -5369.0 / 1800.0,
    12.0 / 7.0,
    -15.0 / 56.0,
    10.0 / 189.0,
    -1.0 / 112.0,
    2.0 / 1925.0,
    -1.0 / 16632.0,
]
CENTER = 9.5
HALF = 6.5
KIN = [-0.5 * c for c in COEFFS]
HIGH = lax.Precision.HIGHEST
F32 = jnp.float32


PIECE = 6
P1_ROWS = 40
BOX = 10
P2_ROWS = 48


def vmem():
    return pl.BlockSpec(memory_space=pltpu.VMEM)


def smem():
    return pl.BlockSpec(memory_space=pltpu.SMEM)


def params():
    return pltpu.CompilerParams(vmem_limit_bytes=56 * 1024 * 1024)


def pack_kernel(at_ref, pos_ref, proj_ref, pot_ref, out_ref, pad_ref):
    pad_ref[...] = jnp.zeros_like(pad_ref)
    pad_ref[:, 0:24, :] = proj_ref[...]
    lane = lax.broadcasted_iota(jnp.int32, (8, 128), 1)
    sub = lax.broadcasted_iota(jnp.int32, (8, 128), 0)
    z_cell = pos_ref[0] + sub
    x_first = pos_ref[1] + lane // 64
    slot = (lane % 64) // 16
    in_y = lane % 16 < 10

    def pair(i, carry):
        for m in range(2):
            a = 2 * i + m
            z0 = at_ref[0, a]
            x0 = at_ref[1, a]
            y0 = at_ref[2, a]
            in_z = (z_cell >= z0) & (z_cell < z0 + 10)
            packed = jnp.zeros((8, 128), F32)
            for j in range(4):
                x_cell = x_first + 2 * j
                inside = in_z & (x_cell >= x0) & (x_cell < x0 + 10)
                rows = pad_ref[a, pl.ds(j, 8, stride=4), :]
                rows = jnp.where(inside, rows, 0.0)
                rows = pltpu.roll(rows, (128 + 16 * j - y0) % 128, 1)
                packed = packed + jnp.where(in_y & (slot == j), rows, 0.0)
            out_ref[i, pl.ds(PIECE * m, PIECE), :] = packed[0:PIECE]
        out_ref[i, pl.ds(12, 24), :] = pot_ref[...]
        return carry

    lax.fori_loop(0, 32, pair, 0)


def boxes_kernel(at_ref, pos_ref, got_ref, orb_ref, out_ref, col_ref):
    col_ref[...] = jnp.zeros_like(col_ref)
    sub = lax.broadcasted_iota(jnp.int32, (16, 128), 0)
    for m in range(2):
        for zb in range(8):
            part = got_ref[4 * zb, PIECE * m : PIECE * (m + 1), :]
            for q in range(1, 4):
                part = part + got_ref[4 * zb + q, PIECE * m : PIECE * (m + 1), :]
            col_ref[m, 6 * zb : 6 * zb + 6, :] = part
    boxes = []
    for m in range(2):
        z0 = at_ref[0, 2 * pos_ref[2] + m]
        boxes.append(col_ref[m, pl.ds(z0, 16), :][0:BOX])

    def send(n, carry):
        out_ref[n, 0:BOX, :] = boxes[0]
        out_ref[n, BOX : 2 * BOX, :] = boxes[1]
        out_ref[n, 20:44, :] = orb_ref[n]
        out_ref[n, 44:48, :] = jnp.zeros((4, 128), F32)
        return carry

    lax.fori_loop(0, 32, send, 0)


def filter_kernel(
    at_ref, pos_ref, strength_ref, taps_ref, own_ref, oth_ref, ownp_ref, othp_ref, out_ref,
    fld, pot, tiles, parts, scaled,
):
    core = pos_ref[3]
    fld[...] = jnp.zeros_like(fld)
    tiles[...] = jnp.zeros_like(tiles)
    for src, src_pot, c in ((own_ref, ownp_ref, core), (oth_ref, othp_ref, 1 - core)):
        for i in range(32):
            zb, q = i // 4, i % 4
            for j in range(4):
                xp = 8 * q + 4 * c + j
                fld[0, 3 + xp, 8 + 6 * zb : 14 + 6 * zb, :] = src.at[i][pl.ds(20 + j, 6, stride=4), :]
                pot[xp, 6 * zb : 6 * zb + 6, :] = src_pot.at[i][pl.ds(12 + j, 6, stride=4), :]

    lane = lax.broadcasted_iota(jnp.int32, (BOX, 128), 1)
    slot = (lane % 64) // 16

    def expand(a, carry):
        xs = jnp.minimum(at_ref[1, a] // 2, 26)
        y0 = at_ref[2, a]
        start = BOX * (a % 2)
        own = own_ref[a // 2, pl.ds(start, BOX), :]
        oth = oth_ref[a // 2, pl.ds(start, BOX), :]
        for w in range(6):
            xp = xs + w
            j = xp % 4
            box = jnp.where((xp // 4) % 2 == core, own, oth)
            box = jnp.where(slot == j, box, 0.0)
            tiles[6 * a + w, 0:BOX, :] = pltpu.roll(box, (128 + y0 - 16 * j) % 128, 1)
        return carry

    lax.fori_loop(0, 64, expand, 0)

    ones = jnp.ones((128, 128), F32)
    low_half = lax.broadcasted_iota(jnp.int32, (48, 128), 1) < 64

    def step(cur, nxt, prev, ca, cb, cg):
        def inner(a, carry):
            xs = jnp.minimum(at_ref[1, a] // 2, 26)
            z0 = at_ref[0, a]
            win = fld[cur, pl.ds(3 + xs, 6), pl.ds(8 + z0, 16), :]
            prod = jnp.sum(win * tiles[pl.ds(6 * a, 6)], axis=0)
            parts[pl.ds(a, 1), :] = jnp.sum(prod, axis=0, keepdims=True)
            return carry

        lax.fori_loop(0, 64, inner, 0, unroll=4)
        sums = jnp.dot(parts[...], ones, precision=HIGH, preferred_element_type=F32)
        scaled[...] = sums * (ca * strength_ref[...])

        def along_y(t, carry):
            rows = fld[cur, pl.ds(3 + 8 * t, 8), 8:56, :].reshape(384, 128)
            got = jnp.dot(rows, taps_ref[...], precision=HIGH, preferred_element_type=F32)
            fld[nxt, pl.ds(3 + 8 * t, 8), 8:56, :] = got.reshape(8, 48, 128)
            return carry

        lax.fori_loop(0, 4, along_y, 0)

        def odd(x):
            def at(d):
                return fld[cur, 3 + x + d, 8:56, :]

            total = KIN[1] * (at(0) + at(-1)) + KIN[3] * (at(1) + at(-2)) + KIN[5] * (at(2) + at(-3))
            return pltpu.roll(total, 64, 1)

        def local(x, here):
            after = odd(x + 1)
            center = fld[cur, 3 + x, 8:56, :]
            total = fld[nxt, 3 + x, 8:56, :] + jnp.where(low_half, here, after)
            total = total + (3.0 * KIN[0] + pot[x]) * center
            for o in range(1, 7):
                pair = fld[cur, 3 + x, 8 + o : 56 + o, :] + fld[cur, 3 + x, 8 - o : 56 - o, :]
                if o % 2 == 0:
                    pair = pair + (fld[cur, 3 + x + o // 2, 8:56, :] + fld[cur, 3 + x - o // 2, 8:56, :])
                total = total + KIN[o] * pair
            total = ca * total
            if cb != 0.0:
                total = total + cb * center
            if cg != 0.0:
                total = total + cg * fld[prev, 3 + x, 8:56, :]
            fld[nxt, 3 + x, 8:56, :] = total
            return after

        lax.fori_loop(0, 32, local, odd(0))

        def outer(a, carry):
            xs = jnp.minimum(at_ref[1, a] // 2, 26)
            z0 = at_ref[0, a]
            win = (nxt, pl.ds(3 + xs, 6), pl.ds(8 + z0, 16), slice(None))
            fld[win] = fld[win] + scaled[pl.ds(a, 1), :][None] * tiles[pl.ds(6 * a, 6)]
            return carry

        lax.fori_loop(0, 64, outer, 0)

    def send(which, place):
        for i in range(32):
            zb, q = i // 4, i % 4
            for j in range(4):
                xp = 8 * q + 4 * core + j
                for kh in range(2):
                    z = 8 + 6 * zb + 3 * kh
                    to = ((2 * j + kh) * 32 + i) * 6 + place
                    out_ref[to : to + 3, :] = fld[which, 3 + xp, z : z + 3, :]

    step(0, 1, 2, 1.0 / HALF, -CENTER / HALF, 0.0)
    step(1, 2, 0, 2.0 / HALF, -2.0 * CENTER / HALF, -1.0)
    step(2, 0, 1, 2.0 / HALF, -2.0 * CENTER / HALF, -1.0)
    step(0, 1, 2, 2.0 / HALF, -2.0 * CENTER / HALF, -1.0)
    step(1, 2, 0, 1.0, 0.0, 0.0)
    send(1, 0)
    send(2, 3)


def y_taps():
    taps = np.zeros((128, 128), np.float32)
    for half in range(2):
        for y in range(NY):
            for o in range(1, 7):
                for to in (y - o, y + o):
                    if 0 <= to < NY:
                        taps[half * 64 + y, half * 64 + to] = KIN[o]
    return taps


def same_core():
    return [[2 * i + c for i in range(32)] for c in range(2)]


def same_core_all():
    return [[(2 * i + c) * 8 + y for y in range(8) for i in range(32)] for c in range(2)]


def x_groups():
    return [[16 * z + i for i in range(16)] for z in range(4)]


def zy_groups():
    return [[(16 * z + i) * 8 + y for z in range(4) for y in range(8)] for i in range(16)]


def pack(at, pos, proj, pot):
    return pl.pallas_call(
        pack_kernel,
        out_shape=jax.ShapeDtypeStruct((32, P1_ROWS, 128), F32),
        in_specs=[smem(), smem(), vmem(), vmem()],
        out_specs=vmem(),
        scratch_shapes=[pltpu.VMEM((64, 32, 128), F32)],
        compiler_params=params(),
        name="pack",
    )(at, pos, proj, pot)


def boxes(at, pos, got, orb):
    return pl.pallas_call(
        boxes_kernel,
        out_shape=jax.ShapeDtypeStruct((32, P2_ROWS, 128), F32),
        in_specs=[smem(), smem(), vmem(), vmem()],
        out_specs=vmem(),
        scratch_shapes=[pltpu.VMEM((2, 64, 128), F32)],
        compiler_params=params(),
        name="boxes",
    )(at, pos, got, orb)


def chebyshev(at, pos, strength, taps, own, oth, own_pot, oth_pot):
    return pl.pallas_call(
        filter_kernel,
        out_shape=jax.ShapeDtypeStruct((1536, 128), F32),
        in_specs=[smem(), smem()] + [vmem()] * 6,
        out_specs=vmem(),
        scratch_shapes=[
            pltpu.VMEM((3, 38, 64, 128), F32),
            pltpu.VMEM((32, 48, 128), F32),
            pltpu.VMEM((64 * 6, 16, 128), F32),
            pltpu.VMEM((64, 128), F32),
            pltpu.VMEM((64, 128), F32),
        ],
        compiler_params=params(),
        name="chebyshev",
    )(at, pos, strength, taps, own, oth, own_pot, oth_pot)


def swap_cores(values):
    return lax.ppermute(values, "dom", [(i, i ^ 1) for i in range(64)])


def sum_everywhere(values):
    mine = lax.all_to_all(values, "dom", 0, 0, tiled=True, axis_index_groups=x_groups())
    mine = jnp.sum(mine, axis=0)
    spread = jnp.broadcast_to(mine[None], (32,) + mine.shape)
    spread = lax.all_to_all(spread, ("dom", "band"), 0, 0, tiled=True, axis_index_groups=zy_groups())
    mine = jnp.sum(spread, axis=0)
    spread = jnp.broadcast_to(mine[None], (16,) + mine.shape)
    return lax.all_to_all(spread, "dom", 0, 0, tiled=True, axis_index_groups=x_groups())


def on_device(orbitals, potential, proj_shape, proj_strength, atom_z, atom_x, atom_y):
    me = lax.axis_index("dom")
    at = jnp.stack([atom_z, atom_x, atom_y])
    pos = jnp.stack([me // 8 * 6, me % 8 * 8, me // 2, me % 2]).astype(jnp.int32)
    strength = jnp.broadcast_to((proj_strength / PROJ_CELLS)[:, None], (64, 128))
    first = pack(at, pos, proj_shape.reshape(64, 24, 128), potential.reshape(24, 128))
    first = lax.all_to_all(first, "dom", 0, 0, tiled=True, axis_index_groups=same_core())
    first_oth = swap_cores(first)
    second = boxes(at, pos, first, orbitals.reshape(32, 24, 128))
    second = lax.all_to_all(second, "dom", 0, 0, tiled=True, axis_index_groups=same_core())
    second_oth = swap_cores(second)
    both = chebyshev(at, pos, strength, jnp.asarray(y_taps()), second, second_oth, first, first_oth)
    both = lax.all_to_all(both, ("dom", "band"), 0, 0, tiled=True, axis_index_groups=same_core_all())
    both = both.reshape(256, 6, 128)
    filtered = both[:, 0:3].reshape(256, 384)
    image = both[:, 3:6].reshape(256, 384)
    correlation = lax.dot_general(filtered, filtered, (((1,), (1,)), ((), ())), precision=HIGH)
    hamiltonian = lax.dot_general(filtered, image, (((1,), (1,)), ((), ())), precision=HIGH)
    total = sum_everywhere(jnp.stack([correlation, hamiltonian]).reshape(16, 64, 128))
    total = total.reshape(2, 256, 256) / NCELLS
    correlation, hamiltonian = total[0], total[1]
    lower = jnp.linalg.cholesky(correlation)
    inverse = lax.linalg.triangular_solve(lower, jnp.eye(256, dtype=F32), left_side=True, lower=True)
    projected = jnp.dot(jnp.dot(inverse, hamiltonian, precision=HIGH), inverse.T, precision=HIGH)
    projected = lax.dynamic_slice_in_dim(projected, 32 * lax.axis_index("band"), 32, 0)
    rotated = jnp.dot(inverse, filtered, precision=HIGH)
    rotated = lax.all_to_all(rotated.reshape(8, 96, 128), "band", 0, 0, tiled=True)
    rotated = rotated.reshape(4, 2, 32, 3, 128).transpose(2, 1, 3, 0, 4)
    return (rotated.reshape(32, 1, 6, 512), projected)


def solution(mesh):
    return jax.shard_map(
        on_device,
        mesh=mesh,
        in_specs=(
            P("band", "dom", None, None),
            P("dom", None, None),
            P(None, "dom", None, None),
            P(),
            P(),
            P(),
            P(),
        ),
        out_specs=(P("band", "dom", None, None), P("band", None)),
        check_vma=False,
    )
```

time: 1770 us -> 318 us (0.18)
  blocking collectives: 1210 us -> 148 us
  waiting for transfers between devices: 337 us -> 23.1 us
  starting transfers between devices: 78 us -> 21.1 us
  Pallas kernels: 0 us -> 51.5 us
  matrix products: 43.9 us -> 4.3 us
    psum x5 -> x0, blocking collectives: 1210 us -> none  [hamiltonian_apply(): correlations = lax.psum(correlations, 'dom')]
    psum x1 -> x0, waiting for transfers between devices: 270 us -> none  [on_device(): ham_full, ovl_full = lax.psum((ham_padded, ovl_padded), ('dom', 'band'))]
    all_to_all x0 -> x5, blocking collectives: none -> 148 us  [the longest x1 43 us: on_device(): lax.all_to_all(both, ('dom', 'band'), 0, 0, tiled=True, axis_index_groups...]
    ppermute x20 -> x2, starting transfers between devices: 77.9 us -> 7.71 us  [swap_cores(): return lax.ppermute(values, 'dom', [(i, i ^ 1) for i in range(64)])]
    all_gather x2 -> x0, waiting for transfers between devices: 67.4 us -> none  [the longest x1 67.4 us: on_device(): lax.all_gather(image, 'band', axis=0, tiled=True)]
    pallas_call x0 -> x3, Pallas kernels: none -> 51.5 us  [the longest x1 44 us: chebyshev(): pl.pallas_call(filter_kernel, out_shape=jax.ShapeDtypeStruct((1536, 128),...]
    dot_general x15 -> x5, matrix products: 42.5 us -> 2.99 us  [the longest x1 0.82 us: on_device(): lax.dot_general(filtered, filtered, (((1,), (1,)), ((), ())), precision=H...]
    all_to_all x0 -> x2, waiting for transfers between devices: none -> 21.1 us  [the longest x1 11.4 us: on_device(): lax.all_to_all(rotated.reshape(8, 96, 128), 'band', 0, 0, tiled=True)]
  transfers between devices with their start and end apart: 23 -> 4, of which waited for: 2 -> 3; matrix products, arithmetic and copies ran while one was open for 1% -> 0% of each run, Pallas kernels for 0% -> 0%
where the time goes in v1:
time: 318 us; the launch traced here: 317 us
  blocking collectives  148 us (47%)
  other arithmetic  55.4 us (17%)
  Pallas kernels  51.5 us (16%)
  waiting for transfers between devices  23.1 us (7%)
  starting transfers between devices  21.1 us (7%)
  local copies, waits for them, and re-layouts  11.2 us (4%)
  matrix products  4.3 us (1%)
    pallas_call x1, Pallas kernels, chebyshev(): pl.pallas_call(filter_kernel, out_shape=jax.ShapeDtypeStruct((1536, 128),...  44 us
    all_to_all x1, blocking collectives, on_device(): lax.all_to_all(both, ('dom', 'band'), 0, 0, tiled=True, axis_index_groups...  43 us
    another operation x6, other arithmetic, on_device(): lower = jnp.linalg.cholesky(correlation)  34 us
    all_to_all x1, blocking collectives, on_device(): lax.all_to_all(first, 'dom', 0, 0, tiled=True, axis_index_groups=same_cor...  32.5 us
    all_to_all x1, blocking collectives, sum_everywhere(): lax.all_to_all(spread, ('dom', 'band'), 0, 0, tiled=True, axis_index_grou...  30.3 us
    all_to_all x1, blocking collectives, on_device(): lax.all_to_all(second, 'dom', 0, 0, tiled=True, axis_index_groups=same_co...  25.5 us
    another operation x3, other arithmetic, on_device(): lax.linalg.triangular_solve(lower, jnp.eye(256, dtype=F32), left_side=Tru...  19.9 us
    all_to_all x1, blocking collectives, sum_everywhere(): lax.all_to_all(values, 'dom', 0, 0, tiled=True, axis_index_groups=x_group...  16.7 us
  transfers between devices with their start and end apart: 4, of which 3 were waited for; matrix products, arithmetic and copies ran while one was open for 0% of the time, Pallas kernels for 0%

profile of v1, /device:TPU:1, one launch (start us, length us, event | category | flops | bytes accessed | tf_op | source)
XLA Modules:
  0.0 316.8 jit_solution(6177244907040220032)
XLA Ops:
  2.6 5.1 %pack.1 = f32[32,40,128]{2,1,0:T(8,128)} custom-call(s32[3,64]{1,0:T(4,128)} %pad_add_fusion.at_ref, s32[4]{0:T(128)} %pad_add_fusion.1.pos_ref, f32[64,24,128]{2,1,0:T(8,128)} %bitcast.60, f32[24,128]{1,0:T(8,128)} %bitcast.63), custom_call_target="tpu_custom_call" | custom-call | tf_op jit(solution)/shard_map/pack/pallas_call | solution.py:243
  7.7 32.5 %all_to_all.39.got_ref.ownp_ref = f32[32,40,128]{2,1,0:T(8,128)} all-to-all(f32[32,40,128]{2,1,0:T(8,128)} %pack.1), channel_id=1, replica_groups={{0,16,32,48,64,80,96,112,128,144,160,176,192,208,224,240,256,272,288,30..., dimensions={0} | all-to-all | bytes 1310720 | tf_op jit(solution)/shard_map/all_to_all | solution.py:304
  40.3 2.3 boxes.1
  42.6 25.5 %all_to_all.40.own_ref = f32[32,48,128]{2,1,0:T(8,128)S(1)} all-to-all(f32[32,48,128]{2,1,0:T(8,128)} %boxes.1), channel_id=1, replica_groups={{0,16,32,48,64,80,96,112,128,144,160,176,192,208,224,240,256,272,288,30..., dimensions={0} | all-to-all | bytes 1572864 | tf_op jit(solution)/shard_map/all_to_all | solution.py:307
  68.1 5.8 %collective-permute-start = (f32[32,48,128]{2,1,0:T(8,128)S(1)}, f32[32,48,128]{2,1,0:T(8,128)S(1)}, u32[]{:S(2)}, u32[]{:S(2)}) collective-permute-start(f32[32,48,128]{2,1,0:T(8,128)S(1)} %all_to_all.40.own_ref), channel_id=1, source_target_pairs={{0,8},{8,0},{16,24},{24,16},{32,40},{40,32},{48,56},{56,48},{64,72... | collective-permute-start | bytes 2359304 | tf_op jit(solution)/shard_map/ppermute | solution.py:285
  73.9 1.9 collective-permute-start.1
  75.8 2.0 collective-permute-done.1.othp_ref
  79.0 44.0 %chebyshev.1 = f32[1536,128]{1,0:T(8,128)} custom-call(s32[3,64]{1,0:T(4,128)} %pad_add_fusion.at_ref, s32[4]{0:T(128)} %pad_add_fusion.1.pos_ref, f32[64,128]{1,0:T(8,128)} %broadcast_in_dim.7.strength_ref, f32[128,128]{1,0:T(8,128)} %constant.144.clone.taps_ref, f32[32,48,128]{2,1,0:T(8,128)} %copy-done.1, f32[32,48,128]{2,1,0:T(8,128)} %copy-done.2, ...), custom_call_target="tpu_custom_call" | custom-call | tf_op jit(solution)/shard_map/chebyshev/pallas_call | solution.py:267
  123.1 1.2 all_to_all.26
  124.3 43.0 %all_to_all.41 = f32[256,6,128]{2,1,0:T(8,128)S(1)} all-to-all(f32[256,6,128]{2,1,0:T(8,128)S(1)} %all_to_all.26), channel_id=1, replica_groups={{0,16,32,48,64,80,96,112,128,144,160,176,192,208,224,240,256,272,288,30..., dimensions={0} | all-to-all | bytes 1572864 | tf_op jit(solution)/shard_map/all_to_all | solution.py:310
  169.4 16.7 %all_to_all.42 = f32[16,64,128]{2,1,0:T(8,128)S(1)} all-to-all(f32[16,64,128]{2,1,0:T(8,128)S(1)} %reshape.63), channel_id=1, replica_groups={{0,8,16,24,32,40,48,56,64,72,80,88,96,104,112,120},{128,136,144,152,160..., dimensions={0} | all-to-all | bytes 1048576 | tf_op jit(solution)/shard_map/all_to_all | solution.py:289
  186.2 30.3 %all_to_all.43 = f32[32,64,128]{2,1,0:T(8,128)S(1)} all-to-all(f32[32,64,128]{2,1,0:T(8,128)S(1)} %broadcast_in_dim.8), channel_id=1, replica_groups={{0,1,2,3,4,5,6,7,128,129,130,131,132,133,134,135,256,257,258,259,260,26..., dimensions={0} | all-to-all | bytes 2097152 | tf_op jit(solution)/shard_map/all_to_all | solution.py:292
  216.6 0.8 broadcast_in_dim.9
  217.4 7.9 %all-to-all-start.5 = ((f32[16,64,128]{2,1,0:T(8,128)}), f32[16,64,128]{2,1,0:T(8,128)S(1)}, u32[]{:S(2)}, u32[]{:S(2)}) async-start(f32[16,64,128]{2,1,0:T(8,128)} %broadcast_in_dim.9), calls=%async_computation.5 | async-start | bytes 1048576 | tf_op jit(solution)/shard_map/all_to_all | solution.py:295
  225.3 9.8 %all-to-all-done.5 = f32[16,64,128]{2,1,0:T(8,128)S(1)} async-done(((f32[16,64,128]{2,1,0:T(8,128)}), f32[16,64,128]{2,1,0:T(8,128)S(1)}, u32[]{:S(2)}, u32[]{:S(2)}) %all-to-all-start.5) | async-done | bytes 524320 | tf_op jit(solution)/shard_map/all_to_all | solution.py:295
  235.5 11.7 %cholesky.50 = f32[128,128]{1,0:T(8,128)S(1)} custom-call(f32[128,128]{1,0:T(8,128)S(1)} %cholesky.118), custom_call_target="Cholesky" | custom-call | tf_op jit(solution)/shard_map/jit(cholesky)/cholesky | solution.py:319
  247.2 9.8 %custom-call.14 = f32[1,128,128]{1,2,0:T(8,128)S(1)} custom-call(f32[1,128,128]{2,1,0:T(8,128)S(1)} %get-tuple-element.33), custom_call_target="InvertDiagBlocksLowerTriangular" | custom-call | tf_op jit(solution)/shard_map/jit(cholesky)/cholesky | solution.py:319
  257.5 11.7 %cholesky.105 = f32[128,128]{1,0:T(8,128)S(1)} custom-call(f32[128,128]{1,0:T(8,128)S(1)} %convolution_subtract_fusion.1), custom_call_target="Cholesky" | custom-call | tf_op jit(solution)/shard_map/jit(cholesky)/cholesky | solution.py:319
  271.3 3.9 %while.1 = (s32[]{:T(128)}, f32[256,256]{1,0:T(8,128)S(1)}, s32[2,2]{1,0:T(2,128)S(1)}, f32[2,128,128]{2,1,0:T(8,128)S(1)}, s32[]{:T(128)}) while((s32[]{:T(128)}, f32[256,256]{1,0:T(8,128)S(1)}, s32[2,2]{1,0:T(2,128)S(1)}, f32[2,128,128]{2,1,0:T(8,128)S(1)}, s32[]{:T(128)}) %tuple.32), condition=%wide.while_cond, body=%wide.while_body.sunk | while | flops 2 | bytes 131181 | solution.py:320
  271.9 1.4 bitcast_dynamic-update-slice_fusion.2
  273.9 1.4 bitcast_dynamic-update-slice_fusion.2
  275.3 19.9 %custom-call.15 = f32[2,128,128]{1,2,0:T(8,128)S(1)} custom-call(f32[2,128,128]{2,1,0:T(8,128)S(1)} %get-tuple-element.9), custom_call_target="InvertDiagBlocksLowerTriangular" | custom-call | tf_op jit(solution)/shard_map/triangular_solve | solution.py:320
  297.4 5.5 %all-to-all-start.6 = ((f32[8,96,128]{2,1,0:T(8,128)}), f32[8,96,128]{2,1,0:T(8,128)S(1)}, u32[]{:S(2)}, u32[]{:S(2)}) async-start(f32[8,96,128]{2,1,0:T(8,128)} %reshape.65), calls=%async_computation.6 | async-start | bytes 786432 | tf_op jit(solution)/shard_map/all_to_all | solution.py:324
  304.4 11.4 %all-to-all-done.6 = f32[8,96,128]{2,1,0:T(8,128)S(1)} async-done(((f32[8,96,128]{2,1,0:T(8,128)}), f32[8,96,128]{2,1,0:T(8,128)S(1)}, u32[]{:S(2)}, u32[]{:S(2)}) %all-to-all-start.6) | async-done | bytes 393248 | tf_op jit(solution)/shard_map/all_to_all | solution.py:324
  (62 shorter events, 13.0 us)
Async XLA Ops:
  0.7 0.7 copy-start.4
  0.7 0.7 copy-start.5
  0.7 0.7 copy-start.6
  42.6 31.3 %copy-start = (f32[32,40,128]{2,1,0:T(8,128)S(1)}, f32[32,40,128]{2,1,0:T(8,128)}, u32[]{:S(2)}) copy-start(f32[32,40,128]{2,1,0:T(8,128)} %all_to_all.39.got_ref.ownp_ref) | copy-start | bytes 1966084
  42.6 33.3 %copy-start.7 = (f32[64]{0:T(128)S(1)}, f32[64]{0:T(128)}, u32[]{:S(2)}) copy-start(f32[64]{0:T(128)} %param.11) | copy-start | bytes 772
  68.1 10.6 %copy-start.1 = (f32[32,48,128]{2,1,0:T(8,128)}, f32[32,48,128]{2,1,0:T(8,128)S(1)}, u32[]{:S(2)}) copy-start(f32[32,48,128]{2,1,0:T(8,128)S(1)} %all_to_all.40.own_ref) | copy-start | bytes 2359300
  68.1 9.8 %collective-permute-start = (f32[32,48,128]{2,1,0:T(8,128)S(1)}, f32[32,48,128]{2,1,0:T(8,128)S(1)}, u32[]{:S(2)}, u32[]{:S(2)}) collective-permute-start(f32[32,48,128]{2,1,0:T(8,128)S(1)} %all_to_all.40.own_ref), channel_id=1, source_target_pairs={{0,8},{8,0},{16,24},{24,16},{32,40},{40,32},{48,56},{56,48},{64,72... | collective-permute-start | bytes 2359304 | tf_op jit(solution)/shard_map/ppermute | solution.py:285
  73.9 4.0 %collective-permute-start.1 = (f32[32,40,128]{2,1,0:T(8,128)S(1)}, f32[32,40,128]{2,1,0:T(8,128)S(1)}, u32[]{:S(2)}, u32[]{:S(2)}) collective-permute-start(f32[32,40,128]{2,1,0:T(8,128)S(1)} %copy-done), channel_id=1, source_target_pairs={{0,8},{8,0},{16,24},{24,16},{32,40},{40,32},{48,56},{56,48},{64,72... | collective-permute-start | bytes 1966088 | tf_op jit(solution)/shard_map/ppermute | solution.py:285
  77.9 0.8 copy-start.3
  77.9 1.1 copy-start.2
  217.4 17.7 %all-to-all-start.5 = ((f32[16,64,128]{2,1,0:T(8,128)}), f32[16,64,128]{2,1,0:T(8,128)S(1)}, u32[]{:S(2)}, u32[]{:S(2)}) async-start(f32[16,64,128]{2,1,0:T(8,128)} %broadcast_in_dim.9), calls=%async_computation.5 | async-start | bytes 1048576 | tf_op jit(solution)/shard_map/all_to_all | solution.py:295
  297.4 18.4 %all-to-all-start.6 = ((f32[8,96,128]{2,1,0:T(8,128)}), f32[8,96,128]{2,1,0:T(8,128)S(1)}, u32[]{:S(2)}, u32[]{:S(2)}) async-start(f32[8,96,128]{2,1,0:T(8,128)} %reshape.65), calls=%async_computation.6 | async-start | bytes 786432 | tf_op jit(solution)/shard_map/all_to_all | solution.py:324

commit v2 on v1

--- a/solution.py
+++ b/solution.py
@@ -72,7 +72,7 @@
         out_ref[i, pl.ds(12, 24), :] = pot_ref[...]
         return carry
 
-    lax.fori_loop(0, 32, pair, 0)
+    lax.fori_loop(0, 32, pair, 0, unroll=4)
 
 
 def boxes_kernel(at_ref, pos_ref, got_ref, orb_ref, out_ref, col_ref):
@@ -100,7 +100,7 @@
 
 
 def filter_kernel(
-    at_ref, pos_ref, strength_ref, taps_ref, own_ref, oth_ref, ownp_ref, othp_ref, out_ref,
+    at_ref, pos_ref, strength_ref, tapy_ref, tapz_ref, own_ref, oth_ref, ownp_ref, othp_ref, out_ref,
     fld, pot, tiles, parts, scaled,
 ):
     core = pos_ref[3]
@@ -131,10 +131,11 @@
             tiles[6 * a + w, 0:BOX, :] = pltpu.roll(box, (128 + y0 - 16 * j) % 128, 1)
         return carry
 
-    lax.fori_loop(0, 64, expand, 0)
+    lax.fori_loop(0, 64, expand, 0, unroll=8)
 
     ones = jnp.ones((128, 128), F32)
-    low_half = lax.broadcasted_iota(jnp.int32, (48, 128), 1) < 64
+    low_half = lax.broadcasted_iota(jnp.int32, (8, 128), 1) < 64
+    high_y = tapy_ref[:, 0:128]
 
     def step(cur, nxt, prev, ca, cb, cg):
         def inner(a, carry):
@@ -145,44 +146,61 @@
             parts[pl.ds(a, 1), :] = jnp.sum(prod, axis=0, keepdims=True)
             return carry
 
-        lax.fori_loop(0, 64, inner, 0, unroll=4)
+        lax.fori_loop(0, 64, inner, 0, unroll=8)
         sums = jnp.dot(parts[...], ones, precision=HIGH, preferred_element_type=F32)
         scaled[...] = sums * (ca * strength_ref[...])
 
-        def along_y(t, carry):
-            rows = fld[cur, pl.ds(3 + 8 * t, 8), 8:56, :].reshape(384, 128)
-            got = jnp.dot(rows, taps_ref[...], precision=HIGH, preferred_element_type=F32)
-            fld[nxt, pl.ds(3 + 8 * t, 8), 8:56, :] = got.reshape(8, 48, 128)
+        def along_yz(t, carry):
+            rows = fld[cur, pl.ds(3 + 4 * t, 4), 8:56, :]
+            high = rows.astype(jnp.bfloat16)
+            rest = (rows - high.astype(F32)).astype(jnp.bfloat16)
+            flat, flat_rest = high.reshape(192, 128), rest.reshape(192, 128)
+            got = jnp.dot(flat, tapy_ref[...], preferred_element_type=F32)
+            got = got[:, 0:128] + got[:, 128:256]
+            got = got + jnp.dot(flat_rest, high_y, preferred_element_type=F32)
+            wide = jnp.concatenate([high[n] for n in range(4)], axis=1)
+            wide_rest = jnp.concatenate([rest[n] for n in range(4)], axis=1)
+            by_z = jnp.dot(tapz_ref[...], wide, preferred_element_type=F32)
+            by_z = by_z[0:48] + by_z[48:96]
+            by_z = by_z + jnp.dot(tapz_ref[0:48, :], wide_rest, preferred_element_type=F32)
+            for n in range(4):
+                fld[nxt, 3 + 4 * t + n, 8:56, :] = got[48 * n : 48 * n + 48] + by_z[:, 128 * n : 128 * n + 128]
             return carry
 
-        lax.fori_loop(0, 4, along_y, 0)
-
-        def odd(x):
-            def at(d):
-                return fld[cur, 3 + x + d, 8:56, :]
-
-            total = KIN[1] * (at(0) + at(-1)) + KIN[3] * (at(1) + at(-2)) + KIN[5] * (at(2) + at(-3))
-            return pltpu.roll(total, 64, 1)
-
-        def local(x, here):
-            after = odd(x + 1)
-            center = fld[cur, 3 + x, 8:56, :]
-            total = fld[nxt, 3 + x, 8:56, :] + jnp.where(low_half, here, after)
-            total = total + (3.0 * KIN[0] + pot[x]) * center
-            for o in range(1, 7):
-                pair = fld[cur, 3 + x, 8 + o : 56 + o, :] + fld[cur, 3 + x, 8 - o : 56 - o, :]
-                if o % 2 == 0:
-                    pair = pair + (fld[cur, 3 + x + o // 2, 8:56, :] + fld[cur, 3 + x - o // 2, 8:56, :])
-                total = total + KIN[o] * pair
-            total = ca * total
-            if cb != 0.0:
-                total = total + cb * center
-            if cg != 0.0:
-                total = total + cg * fld[prev, 3 + x, 8:56, :]
-            fld[nxt, 3 + x, 8:56, :] = total
-            return after
-
-        lax.fori_loop(0, 32, local, odd(0))
+        lax.fori_loop(0, 8, along_yz, 0)
+
+        def along_x(zt, carry):
+            rows = pl.ds(pl.multiple_of(8 + 8 * zt, 8), 8)
+            own_rows = pl.ds(pl.multiple_of(8 * zt, 8), 8)
+            zero = jnp.zeros((8, 128), F32)
+            line = {x: zero for x in (-3, -2, -1, 32, 33, 34, 35)}
+            for x in range(3):
+                line[x] = fld[cur, 3 + x, rows, :]
+
+            def odd(x):
+                total = KIN[1] * (line[x] + line[x - 1]) + KIN[3] * (line[x + 1] + line[x - 2])
+                total = total + KIN[5] * (line[x + 2] + line[x - 3])
+                return pltpu.roll(total, 64, 1)
+
+            here = odd(0)
+            for x in range(32):
+                if x + 3 < 32:
+                    line[x + 3] = fld[cur, 6 + x, rows, :]
+                after = odd(x + 1)
+                total = fld[nxt, 3 + x, rows, :] + jnp.where(low_half, here, after)
+                total = total + (3.0 * KIN[0] + pot[x, own_rows, :]) * line[x]
+                for o in (1, 2, 3):
+                    total = total + KIN[2 * o] * (line[x + o] + line[x - o])
+                total = ca * total
+                if cb != 0.0:
+                    total = total + cb * line[x]
+                if cg != 0.0:
+                    total = total + cg * fld[prev, 3 + x, rows, :]
+                fld[nxt, 3 + x, rows, :] = total
+                here = after
+            return carry
+
+        lax.fori_loop(0, 6, along_x, 0)
 
         def outer(a, carry):
             xs = jnp.minimum(at_ref[1, a] // 2, 26)
@@ -191,7 +209,7 @@
             fld[win] = fld[win] + scaled[pl.ds(a, 1), :][None] * tiles[pl.ds(6 * a, 6)]
             return carry
 
-        lax.fori_loop(0, 64, outer, 0)
+        lax.fori_loop(0, 64, outer, 0, unroll=4)
 
     def send(which, place):
         for i in range(32):
@@ -212,15 +230,21 @@
     send(2, 3)
 
 
-def y_taps():
-    taps = np.zeros((128, 128), np.float32)
-    for half in range(2):
-        for y in range(NY):
+def band_matrix(n, blocks):
+    taps = np.zeros((n * blocks, n * blocks), np.float32)
+    for b in range(blocks):
+        for k in range(n):
             for o in range(1, 7):
-                for to in (y - o, y + o):
-                    if 0 <= to < NY:
-                        taps[half * 64 + y, half * 64 + to] = KIN[o]
+                for to in (k - o, k + o):
+                    if 0 <= to < n:
+                        taps[b * n + k, b * n + to] = KIN[o]
     return taps
+
+
+def two_parts(taps, axis):
+    high = jnp.asarray(taps).astype(jnp.bfloat16)
+    rest = (jnp.asarray(taps) - high.astype(F32)).astype(jnp.bfloat16)
+    return jnp.concatenate([high, rest], axis=axis)
 
 
 def same_core():
@@ -263,11 +287,13 @@
     )(at, pos, got, orb)
 
 
-def chebyshev(at, pos, strength, taps, own, oth, own_pot, oth_pot):
+def chebyshev(at, pos, strength, own, oth, own_pot, oth_pot):
+    tapy = two_parts(band_matrix(NY, 2), 1)
+    tapz = two_parts(band_matrix(48, 1), 0)
     return pl.pallas_call(
         filter_kernel,
         out_shape=jax.ShapeDtypeStruct((1536, 128), F32),
-        in_specs=[smem(), smem()] + [vmem()] * 6,
+        in_specs=[smem(), smem()] + [vmem()] * 7,
         out_specs=vmem(),
         scratch_shapes=[
             pltpu.VMEM((3, 38, 64, 128), F32),
@@ -278,7 +304,132 @@
         ],
         compiler_params=params(),
         name="chebyshev",
-    )(at, pos, strength, taps, own, oth, own_pot, oth_pot)
+    )(at, pos, strength, tapy, tapz, own, oth, own_pot, oth_pot)
+
+
+def dot(a, b):
+    return jnp.dot(a, b, precision=HIGH, preferred_element_type=F32)
+
+
+def dot_t(a, b):
+    return lax.dot_general(a, b, (((1,), (1,)), ((), ())), precision=HIGH, preferred_element_type=F32)
+
+
+def gram_kernel(both_ref, out_ref):
+    f = [both_ref[pl.ds(r, 256, stride=6), :] for r in range(3)]
+    g = [both_ref[pl.ds(3 + r, 256, stride=6), :] for r in range(3)]
+    f = jnp.concatenate(f, axis=1)
+    g = jnp.concatenate(g, axis=1)
+    corr = dot_t(f, f)
+    ham = dot_t(f, g)
+    row = lax.broadcasted_iota(jnp.int32, (256, 256), 0)
+    col = lax.broadcasted_iota(jnp.int32, (256, 256), 1)
+    packed = jnp.where(row >= col, corr, ham)
+    diag = jnp.sum(jnp.where(row == col, ham, 0.0), axis=0, keepdims=True)
+    out_ref[...] = jnp.zeros_like(out_ref)
+    for q in range(16):
+        out_ref[q, 0:16, :] = packed[16 * q : 16 * q + 16, 0:128]
+        out_ref[q, 16:32, :] = packed[16 * q : 16 * q + 16, 128:256]
+    out_ref[0, 32:33, :] = diag[:, 0:128]
+    out_ref[0, 33:34, :] = diag[:, 128:256]
+
+
+def ortho_kernel(pos_ref, total_ref, both_ref, rot_ref, proj_ref, corr, ham, inv, work):
+    row = lax.broadcasted_iota(jnp.int32, (256, 256), 0)
+    col = lax.broadcasted_iota(jnp.int32, (256, 256), 1)
+    below = row > col
+    same = row == col
+    scale = 1.0 / NCELLS
+    for q in range(16):
+        work[16 * q : 16 * q + 16, 0:128] = total_ref[q, 0:16, :]
+        work[16 * q : 16 * q + 16, 128:256] = total_ref[q, 16:32, :]
+    packed = work[...] * scale
+    turned = packed.T
+    diag = jnp.concatenate([total_ref[0, 32:33, :], total_ref[0, 33:34, :]], axis=1) * scale
+    corr[...] = jnp.where(row >= col, packed, turned)
+    ham[...] = jnp.where(same, diag, jnp.where(below, turned, packed))
+
+    def half_lower(e):
+        return jnp.where(below, e, jnp.where(same, 0.5 * e, 0.0))
+
+    own = jnp.where(same, corr[...], 0.0)
+    by_col = lax.rsqrt(jnp.sum(own, axis=0, keepdims=True))
+    by_row = lax.rsqrt(jnp.sum(own, axis=1, keepdims=True))
+    first = half_lower(by_row * corr[...] * by_col - jnp.where(same, 1.0, 0.0))
+    inv[...] = jnp.where(same, by_col, 0.0) - first * by_col
+
+    def rough(a, b, turn=False):
+        dims = (((1,), (1 if turn else 0,)), ((), ()))
+        return lax.dot_general(
+            a.astype(jnp.bfloat16), b.astype(jnp.bfloat16), dims, preferred_element_type=F32
+        )
+
+    for _ in range(2):
+        x = inv[...]
+        e = rough(rough(x, corr[...]), x, True) - jnp.where(same, 1.0, 0.0)
+        inv[...] = x - rough(half_lower(e), x)
+
+    def refine(state):
+        count, _ = state
+        x = inv[...]
+        e = dot_t(dot(x, corr[...]), x) - jnp.where(same, 1.0, 0.0)
+        inv[...] = x - dot(half_lower(e), x)
+        return count + 1, jnp.sum(e * e)
+
+    def going(state):
+        count, size = state
+        return (count < 8) & jnp.logical_not(size < 1e-8)
+
+    _, size = lax.while_loop(going, refine, (jnp.int32(0), jnp.float32(1.0)))
+    least = jnp.min(jnp.where(same, inv[...], 1.0))
+
+    @pl.when(jnp.logical_not((size < 1e-8) & (least > 0.0)))
+    def _():
+        work[...] = corr[...]
+        inv[...] = jnp.where(same, 1.0, 0.0)
+
+        def column(j, carry):
+            picked = jnp.sum(jnp.where(col == j, work[...], 0.0), axis=1, keepdims=True)
+            at_j = lax.broadcasted_iota(jnp.int32, (256, 1), 0)
+            pivot = jnp.sum(jnp.where(at_j == j, picked, 0.0), axis=0, keepdims=True)
+            factor = 1.0 / jnp.sqrt(pivot)
+            inv[pl.ds(j, 1), :] = inv[pl.ds(j, 1), :] * factor
+            down = jnp.where(at_j > j, picked, 0.0) * factor
+            work[...] = work[...] - down * (work[pl.ds(j, 1), :] * factor)
+            inv[...] = inv[...] - down * inv[pl.ds(j, 1), :]
+            return carry
+
+        lax.fori_loop(0, 256, column, 0)
+
+    x = inv[...]
+    mine = inv[pl.ds(pl.multiple_of(32 * pos_ref[4], 32), 32), :]
+    proj_ref[...] = dot_t(dot(mine, ham[...]), x)
+    for r in range(3):
+        part = dot(x, both_ref[pl.ds(r, 256, stride=6), :])
+        rot_ref[pl.ds(r, 256, stride=3), :] = part
+
+
+def gram(both):
+    return pl.pallas_call(
+        gram_kernel,
+        out_shape=jax.ShapeDtypeStruct((16, 40, 128), F32),
+        in_specs=[vmem()],
+        out_specs=vmem(),
+        compiler_params=params(),
+        name="gram",
+    )(both)
+
+
+def ortho(pos, total, both):
+    return pl.pallas_call(
+        ortho_kernel,
+        out_shape=[jax.ShapeDtypeStruct((768, 128), F32), jax.ShapeDtypeStruct((32, 256), F32)],
+        in_specs=[smem(), vmem(), vmem()],
+        out_specs=[vmem(), vmem()],
+        scratch_shapes=[pltpu.VMEM((256, 256), F32)] * 4,
+        compiler_params=params(),
+        name="ortho",
+    )(pos, total, both)
 
 
 def swap_cores(values):
@@ -298,7 +449,7 @@
 def on_device(orbitals, potential, proj_shape, proj_strength, atom_z, atom_x, atom_y):
     me = lax.axis_index("dom")
     at = jnp.stack([atom_z, atom_x, atom_y])
-    pos = jnp.stack([me // 8 * 6, me % 8 * 8, me // 2, me % 2]).astype(jnp.int32)
+    pos = jnp.stack([me // 8 * 6, me % 8 * 8, me // 2, me % 2, lax.axis_index("band")]).astype(jnp.int32)
     strength = jnp.broadcast_to((proj_strength / PROJ_CELLS)[:, None], (64, 128))
     first = pack(at, pos, proj_shape.reshape(64, 24, 128), potential.reshape(24, 128))
     first = lax.all_to_all(first, "dom", 0, 0, tiled=True, axis_index_groups=same_core())
@@ -306,21 +457,10 @@
     second = boxes(at, pos, first, orbitals.reshape(32, 24, 128))
     second = lax.all_to_all(second, "dom", 0, 0, tiled=True, axis_index_groups=same_core())
     second_oth = swap_cores(second)
-    both = chebyshev(at, pos, strength, jnp.asarray(y_taps()), second, second_oth, first, first_oth)
+    both = chebyshev(at, pos, strength, second, second_oth, first, first_oth)
     both = lax.all_to_all(both, ("dom", "band"), 0, 0, tiled=True, axis_index_groups=same_core_all())
-    both = both.reshape(256, 6, 128)
-    filtered = both[:, 0:3].reshape(256, 384)
-    image = both[:, 3:6].reshape(256, 384)
-    correlation = lax.dot_general(filtered, filtered, (((1,), (1,)), ((), ())), precision=HIGH)
-    hamiltonian = lax.dot_general(filtered, image, (((1,), (1,)), ((), ())), precision=HIGH)
-    total = sum_everywhere(jnp.stack([correlation, hamiltonian]).reshape(16, 64, 128))
-    total = total.reshape(2, 256, 256) / NCELLS
-    correlation, hamiltonian = total[0], total[1]
-    lower = jnp.linalg.cholesky(correlation)
-    inverse = lax.linalg.triangular_solve(lower, jnp.eye(256, dtype=F32), left_side=True, lower=True)
-    projected = jnp.dot(jnp.dot(inverse, hamiltonian, precision=HIGH), inverse.T, precision=HIGH)
-    projected = lax.dynamic_slice_in_dim(projected, 32 * lax.axis_index("band"), 32, 0)
-    rotated = jnp.dot(inverse, filtered, precision=HIGH)
+    total = sum_everywhere(gram(both))
+    rotated, projected = ortho(pos, total, both)
     rotated = lax.all_to_all(rotated.reshape(8, 96, 128), "band", 0, 0, tiled=True)
     rotated = rotated.reshape(4, 2, 32, 3, 128).transpose(2, 1, 3, 0, 4)
     return (rotated.reshape(32, 1, 6, 512), projected)

time: 318 us -> 296 us (0.931)
  Pallas kernels: 51.5 us -> 107 us
  other arithmetic: 55.4 us -> 0.67 us
  blocking collectives: 148 us -> 171 us
  waiting for transfers between devices: 23.1 us -> 2.04 us
  starting transfers between devices: 21.1 us -> 7.71 us
  local copies, waits for them, and re-layouts: 11.2 us -> 5.73 us
  matrix products: 4.3 us -> 0 us
    pallas_call x0 -> x2, Pallas kernels: none -> 71.6 us  [the longest x1 68.7 us: ortho(): pl.pallas_call(ortho_kernel, out_shape=[jax.ShapeDtypeStruct((768, 128),...]
    another operation x11 -> x0, other arithmetic: 54.6 us -> none  [the longest x6 34 us: on_device(): lower = jnp.linalg.cholesky(correlation)]
    all_to_all x0 -> x2, blocking collectives: none -> 33.7 us  [the longest x1 17.6 us: on_device(): lax.all_to_all(rotated.reshape(8, 96, 128), 'band', 0, 0, tiled=True)]
    all_to_all x2 -> x0, waiting for transfers between devices: 21.1 us -> none  [the longest x1 11.4 us: on_device(): lax.all_to_all(rotated.reshape(8, 96, 128), 'band', 0, 0, tiled=True)]
    pallas_call x1, Pallas kernels: 44 us -> 29.6 us  [chebyshev(): pl.pallas_call(filter_kernel, out_shape=jax.ShapeDtypeStruct((1536, 128),...]
    all_to_all x2 -> x0, starting transfers between devices: 13.4 us -> none  [the longest x1 7.87 us: sum_everywhere(): lax.all_to_all(spread, 'dom', 0, 0, tiled=True, axis_index_groups=x_group...]
    all_to_all x1, blocking collectives: 30.3 us -> 21.6 us  [sum_everywhere(): lax.all_to_all(spread, ('dom', 'band'), 0, 0, tiled=True, axis_index_grou...]
    another operation x9 -> x1, local copies, waits for them, and re-layouts: 3.99 us -> 0.57 us  [on_device(): jnp.stack([me // 8 * 6, me % 8 * 8, me // 2, me % 2, lax.axis_index('band...]
  transfers between devices with their start and end apart: 4 -> 2, of which waited for: 3 -> 1; matrix products, arithmetic and copies ran while one was open for 0% -> 0% of each run, Pallas kernels for 0% -> 0%
where the time goes in v2:
time: 296 us; the launch traced here: 295 us
  blocking collectives  171 us (58%)
  Pallas kernels  107 us (36%)
  starting transfers between devices  7.71 us (3%)
  local copies, waits for them, and re-layouts  5.73 us (2%)
    pallas_call x1, Pallas kernels, ortho(): pl.pallas_call(ortho_kernel, out_shape=[jax.ShapeDtypeStruct((768, 128),...  68.7 us
    all_to_all x1, blocking collectives, on_device(): lax.all_to_all(both, ('dom', 'band'), 0, 0, tiled=True, axis_index_groups...  43 us
    all_to_all x1, blocking collectives, on_device(): lax.all_to_all(first, 'dom', 0, 0, tiled=True, axis_index_groups=same_cor...  32.5 us
    pallas_call x1, Pallas kernels, chebyshev(): pl.pallas_call(filter_kernel, out_shape=jax.ShapeDtypeStruct((1536, 128),...  29.6 us
    all_to_all x1, blocking collectives, on_device(): lax.all_to_all(second, 'dom', 0, 0, tiled=True, axis_index_groups=same_co...  25.5 us
    all_to_all x1, blocking collectives, sum_everywhere(): lax.all_to_all(spread, ('dom', 'band'), 0, 0, tiled=True, axis_index_grou...  21.6 us
    all_to_all x1, blocking collectives, on_device(): lax.all_to_all(rotated.reshape(8, 96, 128), 'band', 0, 0, tiled=True)  17.6 us
    all_to_all x1, blocking collectives, sum_everywhere(): lax.all_to_all(spread, 'dom', 0, 0, tiled=True, axis_index_groups=x_group...  16 us
  transfers between devices with their start and end apart: 2, of which 1 were waited for; matrix products, arithmetic and copies ran while one was open for 0% of the time, Pallas kernels for 0%

profile of v2, /device:TPU:1, one launch (start us, length us, event | category | flops | bytes accessed | tf_op | source)
XLA Modules:
  0.0 295.0 jit_solution(12254986770832612314)
XLA Ops:
  0.7 0.6 copy-done.4
  1.4 0.6 pad_add_fusion.at_ref
  1.9 0.6 stack.35.pos_ref
  2.5 3.6 %pack.1 = f32[32,40,128]{2,1,0:T(8,128)} custom-call(s32[3,64]{1,0:T(4,128)} %pad_add_fusion.at_ref, s32[5]{0:T(128)} %stack.35.pos_ref, f32[64,24,128]{2,1,0:T(8,128)} %bitcast.17, f32[24,128]{1,0:T(8,128)} %bitcast.21), custom_call_target="tpu_custom_call" | custom-call | tf_op jit(solution)/shard_map/pack/pallas_call | solution.py:267
  6.1 32.5 %all_to_all.41.got_ref.ownp_ref = f32[32,40,128]{2,1,0:T(8,128)} all-to-all(f32[32,40,128]{2,1,0:T(8,128)} %pack.1), channel_id=1, replica_groups={{0,16,32,48,64,80,96,112,128,144,160,176,192,208,224,240,256,272,288,30..., dimensions={0} | all-to-all | bytes 1310720 | tf_op jit(solution)/shard_map/all_to_all | solution.py:455
  38.6 2.3 boxes.1
  40.9 25.5 %all_to_all.42.own_ref = f32[32,48,128]{2,1,0:T(8,128)S(1)} all-to-all(f32[32,48,128]{2,1,0:T(8,128)} %boxes.1), channel_id=1, replica_groups={{0,16,32,48,64,80,96,112,128,144,160,176,192,208,224,240,256,272,288,30..., dimensions={0} | all-to-all | bytes 1572864 | tf_op jit(solution)/shard_map/all_to_all | solution.py:458
  66.4 5.8 %collective-permute-start = (f32[32,48,128]{2,1,0:T(8,128)S(1)}, f32[32,48,128]{2,1,0:T(8,128)S(1)}, u32[]{:S(2)}, u32[]{:S(2)}) collective-permute-start(f32[32,48,128]{2,1,0:T(8,128)S(1)} %all_to_all.42.own_ref), channel_id=1, source_target_pairs={{0,8},{8,0},{16,24},{24,16},{32,40},{40,32},{48,56},{56,48},{64,72... | collective-permute-start | bytes 2359304 | tf_op jit(solution)/shard_map/ppermute | solution.py:436
  72.2 1.9 collective-permute-start.1
  74.2 2.0 collective-permute-done.1.othp_ref
  76.2 0.8 broadcast_in_dim.6.strength_ref
  77.1 0.3 copy-done.2
  77.3 29.6 %chebyshev.1 = f32[1536,128]{1,0:T(8,128)} custom-call(s32[3,64]{1,0:T(4,128)} %pad_add_fusion.at_ref, s32[5]{0:T(128)} %stack.35.pos_ref, f32[64,128]{1,0:T(8,128)} %broadcast_in_dim.6.strength_ref, bf16[128,256]{1,0:T(8,128)(2,1)} %constant.72.tapy_ref, bf16[96,48]{1,0:T(8,128)(2,1)} %constant.77.tapz_ref, f32[32,48,128]{2,1,0:T(8,128)} %copy-done.1, ...), custom_call_target="tpu_custom_call" | custom-call | tf_op jit(solution)/shard_map/chebyshev/pallas_call | solution.py:293
  107.0 1.2 all_to_all.27
  108.2 43.0 %all_to_all.43 = f32[256,6,128]{2,1,0:T(8,128)S(1)} all-to-all(f32[256,6,128]{2,1,0:T(8,128)S(1)} %all_to_all.27), channel_id=1, replica_groups={{0,16,32,48,64,80,96,112,128,144,160,176,192,208,224,240,256,272,288,30..., dimensions={0} | all-to-all | bytes 1572864 | tf_op jit(solution)/shard_map/all_to_all | solution.py:461
  151.2 1.0 all_to_all.29.both_ref
  152.2 2.9 gram.1
  155.0 14.7 %all_to_all.44 = f32[16,40,128]{2,1,0:T(8,128)S(1)} all-to-all(f32[16,40,128]{2,1,0:T(8,128)} %gram.1), channel_id=1, replica_groups={{0,8,16,24,32,40,48,56,64,72,80,88,96,104,112,120},{128,136,144,152,160..., dimensions={0} | all-to-all | bytes 655360 | tf_op jit(solution)/shard_map/all_to_all | solution.py:440
  169.9 21.6 %all_to_all.45 = f32[32,40,128]{2,1,0:T(8,128)S(1)} all-to-all(f32[32,40,128]{2,1,0:T(8,128)S(1)} %broadcast_in_dim.7), channel_id=1, replica_groups={{0,1,2,3,4,5,6,7,128,129,130,131,132,133,134,135,256,257,258,259,260,26..., dimensions={0} | all-to-all | bytes 1310720 | tf_op jit(solution)/shard_map/all_to_all | solution.py:443
  191.6 16.0 %all_to_all.46.total_ref = f32[16,40,128]{2,1,0:T(8,128)} all-to-all(f32[16,40,128]{2,1,0:T(8,128)S(1)} %broadcast_in_dim.8), channel_id=1, replica_groups={{0,8,16,24,32,40,48,56,64,72,80,88,96,104,112,120},{128,136,144,152,160..., dimensions={0} | all-to-all | bytes 655360 | tf_op jit(solution)/shard_map/all_to_all | solution.py:446
  207.6 68.7 %ortho.1 = (f32[768,128]{1,0:T(8,128)}, f32[32,256]{1,0:T(8,128)}) custom-call(s32[5]{0:T(128)} %stack.35.pos_ref, f32[16,40,128]{2,1,0:T(8,128)} %all_to_all.46.total_ref, f32[1536,128]{1,0:T(8,128)} %all_to_all.29.both_ref), custom_call_target="tpu_custom_call" | custom-call | tf_op jit(solution)/shard_map/ortho/pallas_call | solution.py:424
  276.3 17.6 %all_to_all.47 = f32[8,96,128]{2,1,0:T(8,128)S(1)} all-to-all(f32[8,96,128]{2,1,0:T(8,128)} %bitcast.20), channel_id=1, replica_groups=mesh['dom'=64,'band'=8] {'band'}, dimensions={0} | all-to-all | bytes 786432 | tf_op jit(solution)/shard_map/all_to_all | solution.py:464
  293.9 0.2 copy.19
  294.2 0.8 copy.22
  (20 shorter events, 0.2 us)
Async XLA Ops:
  0.7 0.7 copy-start.4
  0.7 0.7 copy-start.5
  0.7 0.7 copy-start.6
  40.9 31.3 %copy-start = (f32[32,40,128]{2,1,0:T(8,128)S(1)}, f32[32,40,128]{2,1,0:T(8,128)}, u32[]{:S(2)}) copy-start(f32[32,40,128]{2,1,0:T(8,128)} %all_to_all.41.got_ref.ownp_ref) | copy-start | bytes 1966084
  40.9 33.3 %copy-start.7 = (f32[64]{0:T(128)S(1)}, f32[64]{0:T(128)}, u32[]{:S(2)}) copy-start(f32[64]{0:T(128)} %param.12) | copy-start | bytes 772
  66.4 10.6 %copy-start.1 = (f32[32,48,128]{2,1,0:T(8,128)}, f32[32,48,128]{2,1,0:T(8,128)S(1)}, u32[]{:S(2)}) copy-start(f32[32,48,128]{2,1,0:T(8,128)S(1)} %all_to_all.42.own_ref) | copy-start | bytes 2359300
  66.4 9.8 %collective-permute-start = (f32[32,48,128]{2,1,0:T(8,128)S(1)}, f32[32,48,128]{2,1,0:T(8,128)S(1)}, u32[]{:S(2)}, u32[]{:S(2)}) collective-permute-start(f32[32,48,128]{2,1,0:T(8,128)S(1)} %all_to_all.42.own_ref), channel_id=1, source_target_pairs={{0,8},{8,0},{16,24},{24,16},{32,40},{40,32},{48,56},{56,48},{64,72... | collective-permute-start | bytes 2359304 | tf_op jit(solution)/shard_map/ppermute | solution.py:436
  72.2 4.0 %collective-permute-start.1 = (f32[32,40,128]{2,1,0:T(8,128)S(1)}, f32[32,40,128]{2,1,0:T(8,128)S(1)}, u32[]{:S(2)}, u32[]{:S(2)}) collective-permute-start(f32[32,40,128]{2,1,0:T(8,128)S(1)} %copy-done), channel_id=1, source_target_pairs={{0,8},{8,0},{16,24},{24,16},{32,40},{40,32},{48,56},{56,48},{64,72... | collective-permute-start | bytes 1966088 | tf_op jit(solution)/shard_map/ppermute | solution.py:436
  76.2 0.8 copy-start.3
  76.2 1.1 copy-start.2

commit v3 on v2

--- a/solution.py
+++ b/solution.py
@@ -25,10 +25,8 @@
 F32 = jnp.float32
 
 
-PIECE = 6
-P1_ROWS = 40
-BOX = 10
-P2_ROWS = 48
+P1_ROWS = 32
+P2_ROWS = 40
 
 
 def vmem():
@@ -44,14 +42,17 @@
 
 
 def pack_kernel(at_ref, pos_ref, proj_ref, pot_ref, out_ref, pad_ref):
-    pad_ref[...] = jnp.zeros_like(pad_ref)
+    pad_ref[:, 24:48, :] = jnp.zeros((64, 24, 128), F32)
     pad_ref[:, 0:24, :] = proj_ref[...]
     lane = lax.broadcasted_iota(jnp.int32, (8, 128), 1)
     sub = lax.broadcasted_iota(jnp.int32, (8, 128), 0)
-    z_cell = pos_ref[0] + sub
-    x_first = pos_ref[1] + lane // 64
-    slot = (lane % 64) // 16
-    in_y = lane % 16 < 10
+    slot_lane = lane % 64
+    z_cells, x_cells, slots = [], [], []
+    for s in range(6):
+        row = s + 6 * sub
+        z_cells.append(pos_ref[0] + row // 4)
+        x_cells.append(pos_ref[1] + 2 * (row % 4) + lane // 64)
+        slots.append((slot_lane >= 10 * s) & (slot_lane < 10 * s + 10))
 
     def pair(i, carry):
         for m in range(2):
@@ -59,49 +60,50 @@
             z0 = at_ref[0, a]
             x0 = at_ref[1, a]
             y0 = at_ref[2, a]
-            in_z = (z_cell >= z0) & (z_cell < z0 + 10)
             packed = jnp.zeros((8, 128), F32)
-            for j in range(4):
-                x_cell = x_first + 2 * j
-                inside = in_z & (x_cell >= x0) & (x_cell < x0 + 10)
-                rows = pad_ref[a, pl.ds(j, 8, stride=4), :]
+            for s in range(6):
+                z, x = z_cells[s], x_cells[s]
+                inside = (z >= z0) & (z < z0 + 10) & (x >= x0) & (x < x0 + 10)
+                rows = pad_ref[a, pl.ds(s, 8, stride=6), :]
                 rows = jnp.where(inside, rows, 0.0)
-                rows = pltpu.roll(rows, (128 + 16 * j - y0) % 128, 1)
-                packed = packed + jnp.where(in_y & (slot == j), rows, 0.0)
-            out_ref[i, pl.ds(PIECE * m, PIECE), :] = packed[0:PIECE]
-        out_ref[i, pl.ds(12, 24), :] = pot_ref[...]
+                rows = pltpu.roll(rows, (128 + 10 * s - y0) & 127, 1)
+                packed = jnp.where(slots[s], rows, packed)
+            out_ref[i, pl.ds(4 * m, 4), :] = packed[0:4]
+        out_ref[i, pl.ds(8, 24), :] = pot_ref[...]
         return carry
 
     lax.fori_loop(0, 32, pair, 0, unroll=4)
+
+
+def first_row(z0):
+    return (4 * z0 * 171) >> 10
 
 
 def boxes_kernel(at_ref, pos_ref, got_ref, orb_ref, out_ref, col_ref):
     col_ref[...] = jnp.zeros_like(col_ref)
-    sub = lax.broadcasted_iota(jnp.int32, (16, 128), 0)
-    for m in range(2):
-        for zb in range(8):
-            part = got_ref[4 * zb, PIECE * m : PIECE * (m + 1), :]
-            for q in range(1, 4):
-                part = part + got_ref[4 * zb + q, PIECE * m : PIECE * (m + 1), :]
-            col_ref[m, 6 * zb : 6 * zb + 6, :] = part
+    for zb in range(8):
+        part = got_ref[4 * zb, 0:8, :]
+        for q in range(1, 4):
+            part = part + got_ref[4 * zb + q, 0:8, :]
+        col_ref[0, 4 * zb : 4 * zb + 4, :] = part[0:4]
+        col_ref[1, 4 * zb : 4 * zb + 4, :] = part[4:8]
     boxes = []
     for m in range(2):
         z0 = at_ref[0, 2 * pos_ref[2] + m]
-        boxes.append(col_ref[m, pl.ds(z0, 16), :][0:BOX])
+        boxes.append(col_ref[m, pl.ds(first_row(z0), 8), :])
 
     def send(n, carry):
-        out_ref[n, 0:BOX, :] = boxes[0]
-        out_ref[n, BOX : 2 * BOX, :] = boxes[1]
-        out_ref[n, 20:44, :] = orb_ref[n]
-        out_ref[n, 44:48, :] = jnp.zeros((4, 128), F32)
+        out_ref[n, 0:8, :] = boxes[0]
+        out_ref[n, 8:16, :] = boxes[1]
+        out_ref[n, 16:40, :] = orb_ref[n]
         return carry
 
-    lax.fori_loop(0, 32, send, 0)
+    lax.fori_loop(0, 32, send, 0, unroll=4)
 
 
 def filter_kernel(
     at_ref, pos_ref, strength_ref, tapy_ref, tapz_ref, own_ref, oth_ref, ownp_ref, othp_ref, out_ref,
-    fld, pot, tiles, parts, scaled,
+    fld, pot, half, tiles, parts, scaled,
 ):
     core = pos_ref[3]
     fld[...] = jnp.zeros_like(fld)
@@ -111,27 +113,32 @@
             zb, q = i // 4, i % 4
             for j in range(4):
                 xp = 8 * q + 4 * c + j
-                fld[0, 3 + xp, 8 + 6 * zb : 14 + 6 * zb, :] = src.at[i][pl.ds(20 + j, 6, stride=4), :]
-                pot[xp, 6 * zb : 6 * zb + 6, :] = src_pot.at[i][pl.ds(12 + j, 6, stride=4), :]
-
-    lane = lax.broadcasted_iota(jnp.int32, (BOX, 128), 1)
-    slot = (lane % 64) // 16
+                fld[0, 3 + xp, 8 + 6 * zb : 14 + 6 * zb, :] = src.at[i][pl.ds(16 + j, 6, stride=4), :]
+                pot[xp, 6 * zb : 6 * zb + 6, :] = src_pot.at[i][pl.ds(8 + j, 6, stride=4), :]
+
+    half[pl.ds(core, 1)] = own_ref[:, 0:16, :].reshape(1, 64, 8, 128)
+    half[pl.ds(1 - core, 1)] = oth_ref[:, 0:16, :].reshape(1, 64, 8, 128)
+    slot_lane = lax.broadcasted_iota(jnp.int32, (4, 128), 1) & 63
 
     def expand(a, carry):
-        xs = jnp.minimum(at_ref[1, a] // 2, 26)
+        xs = jnp.minimum(at_ref[1, a] >> 1, 26)
         y0 = at_ref[2, a]
-        start = BOX * (a % 2)
-        own = own_ref[a // 2, pl.ds(start, BOX), :]
-        oth = oth_ref[a // 2, pl.ds(start, BOX), :]
+        z0 = at_ref[0, a]
+        begin = 4 * z0 - 6 * first_row(z0)
         for w in range(6):
             xp = xs + w
-            j = xp % 4
-            box = jnp.where((xp // 4) % 2 == core, own, oth)
-            box = jnp.where(slot == j, box, 0.0)
-            tiles[6 * a + w, 0:BOX, :] = pltpu.roll(box, (128 + y0 - 16 * j) % 128, 1)
+            for v in range(3):
+                n = 4 if v == 0 else 3
+                place = begin + (xp & 3) + 4 * v
+                row = (place * 11) >> 6
+                left = 10 * (place - 6 * row)
+                box = half[(xp >> 2) & 1, a, pl.ds(row, n, stride=2), :]
+                in_slot = (slot_lane[0:n] >= left) & (slot_lane[0:n] < left + 10)
+                box = jnp.where(in_slot, box, 0.0)
+                tiles[6 * a + w, pl.ds(v, n, stride=3), :] = pltpu.roll(box, (128 + y0 - left) & 127, 1)
         return carry
 
-    lax.fori_loop(0, 64, expand, 0, unroll=8)
+    lax.fori_loop(0, 64, expand, 0, unroll=4)
 
     ones = jnp.ones((128, 128), F32)
     low_half = lax.broadcasted_iota(jnp.int32, (8, 128), 1) < 64
@@ -139,7 +146,7 @@
 
     def step(cur, nxt, prev, ca, cb, cg):
         def inner(a, carry):
-            xs = jnp.minimum(at_ref[1, a] // 2, 26)
+            xs = jnp.minimum(at_ref[1, a] >> 1, 26)
             z0 = at_ref[0, a]
             win = fld[cur, pl.ds(3 + xs, 6), pl.ds(8 + z0, 16), :]
             prod = jnp.sum(win * tiles[pl.ds(6 * a, 6)], axis=0)
@@ -167,7 +174,7 @@
                 fld[nxt, 3 + 4 * t + n, 8:56, :] = got[48 * n : 48 * n + 48] + by_z[:, 128 * n : 128 * n + 128]
             return carry
 
-        lax.fori_loop(0, 8, along_yz, 0)
+        lax.fori_loop(0, 8, along_yz, 0, unroll=8)
 
         def along_x(zt, carry):
             rows = pl.ds(pl.multiple_of(8 + 8 * zt, 8), 8)
@@ -203,7 +210,7 @@
         lax.fori_loop(0, 6, along_x, 0)
 
         def outer(a, carry):
-            xs = jnp.minimum(at_ref[1, a] // 2, 26)
+            xs = jnp.minimum(at_ref[1, a] >> 1, 26)
             z0 = at_ref[0, a]
             win = (nxt, pl.ds(3 + xs, 6), pl.ds(8 + z0, 16), slice(None))
             fld[win] = fld[win] + scaled[pl.ds(a, 1), :][None] * tiles[pl.ds(6 * a, 6)]
@@ -269,7 +276,7 @@
         out_shape=jax.ShapeDtypeStruct((32, P1_ROWS, 128), F32),
         in_specs=[smem(), smem(), vmem(), vmem()],
         out_specs=vmem(),
-        scratch_shapes=[pltpu.VMEM((64, 32, 128), F32)],
+        scratch_shapes=[pltpu.VMEM((64, 48, 128), F32)],
         compiler_params=params(),
         name="pack",
     )(at, pos, proj, pot)
@@ -281,7 +288,7 @@
         out_shape=jax.ShapeDtypeStruct((32, P2_ROWS, 128), F32),
         in_specs=[smem(), smem(), vmem(), vmem()],
         out_specs=vmem(),
-        scratch_shapes=[pltpu.VMEM((2, 64, 128), F32)],
+        scratch_shapes=[pltpu.VMEM((2, 40, 128), F32)],
         compiler_params=params(),
         name="boxes",
     )(at, pos, got, orb)
@@ -298,6 +305,7 @@
         scratch_shapes=[
             pltpu.VMEM((3, 38, 64, 128), F32),
             pltpu.VMEM((32, 48, 128), F32),
+            pltpu.VMEM((2, 64, 8, 128), F32),
             pltpu.VMEM((64 * 6, 16, 128), F32),
             pltpu.VMEM((64, 128), F32),
             pltpu.VMEM((64, 128), F32),
@@ -458,7 +466,9 @@
     second = lax.all_to_all(second, "dom", 0, 0, tiled=True, axis_index_groups=same_core())
     second_oth = swap_cores(second)
     both = chebyshev(at, pos, strength, second, second_oth, first, first_oth)
+    both = both.reshape(256, 3, 2, 128)
     both = lax.all_to_all(both, ("dom", "band"), 0, 0, tiled=True, axis_index_groups=same_core_all())
+    both = both.reshape(1536, 128)
     total = sum_everywhere(gram(both))
     rotated, projected = ortho(pos, total, both)
     rotated = lax.all_to_all(rotated.reshape(8, 96, 128), "band", 0, 0, tiled=True)

time: 296 us -> 275 us (0.929)
  blocking collectives: 171 us -> 160 us
  Pallas kernels: 107 us -> 99.1 us
    pallas_call x1, Pallas kernels: 29.6 us -> 22.3 us  [chebyshev(): pl.pallas_call(filter_kernel, out_shape=jax.ShapeDtypeStruct((1536, 128),...]
    all_to_all x1, blocking collectives: 43 us -> 37.6 us  [on_device(): lax.all_to_all(both, ('dom', 'band'), 0, 0, tiled=True, axis_index_groups...]
where the time goes in v3:
time: 275 us; the launch traced here: 274 us
  blocking collectives  160 us (58%)
  Pallas kernels  99.1 us (36%)
  starting transfers between devices  7.49 us (3%)
  local copies, waits for them, and re-layouts  3.53 us (1%)
    pallas_call x1, Pallas kernels, ortho(): pl.pallas_call(ortho_kernel, out_shape=[jax.ShapeDtypeStruct((768, 128),...  68.7 us
    all_to_all x1, blocking collectives, on_device(): lax.all_to_all(both, ('dom', 'band'), 0, 0, tiled=True, axis_index_groups...  37.6 us
    all_to_all x1, blocking collectives, on_device(): lax.all_to_all(first, 'dom', 0, 0, tiled=True, axis_index_groups=same_cor...  30.1 us
    all_to_all x1, blocking collectives, on_device(): lax.all_to_all(second, 'dom', 0, 0, tiled=True, axis_index_groups=same_co...  22.9 us
    pallas_call x1, Pallas kernels, chebyshev(): pl.pallas_call(filter_kernel, out_shape=jax.ShapeDtypeStruct((1536, 128),...  22.3 us
    all_to_all x1, blocking collectives, sum_everywhere(): lax.all_to_all(spread, ('dom', 'band'), 0, 0, tiled=True, axis_index_grou...  21.6 us
    all_to_all x1, blocking collectives, on_device(): lax.all_to_all(rotated.reshape(8, 96, 128), 'band', 0, 0, tiled=True)  17.6 us
    all_to_all x1, blocking collectives, sum_everywhere(): lax.all_to_all(spread, 'dom', 0, 0, tiled=True, axis_index_groups=x_group...  16.1 us
  transfers between devices with their start and end apart: 2, of which 1 were waited for; matrix products, arithmetic and copies ran while one was open for 0% of the time, Pallas kernels for 0%

profile of v3, /device:TPU:1, one launch (start us, length us, event | category | flops | bytes accessed | tf_op | source)
XLA Modules:
  0.0 273.8 jit_solution(11703613112537777347)
XLA Ops:
  0.7 0.6 copy-done.4
  1.3 0.0 copy-done.5
  1.4 0.6 pad_add_fusion.at_ref
  1.9 0.7 stack.35.pos_ref
  2.6 3.1 %pack.1 = f32[32,32,128]{2,1,0:T(8,128)} custom-call(s32[3,64]{1,0:T(4,128)} %pad_add_fusion.at_ref, s32[5]{0:T(128)} %stack.35.pos_ref, f32[64,24,128]{2,1,0:T(8,128)} %bitcast.22, f32[24,128]{1,0:T(8,128)} %bitcast.26), custom_call_target="tpu_custom_call" | custom-call | tf_op jit(solution)/shard_map/pack/pallas_call | solution.py:274
  5.8 30.1 %all_to_all.35.got_ref.ownp_ref = f32[32,32,128]{2,1,0:T(8,128)} all-to-all(f32[32,32,128]{2,1,0:T(8,128)} %pack.1), channel_id=1, replica_groups={{0,16,32,48,64,80,96,112,128,144,160,176,192,208,224,240,256,272,288,30..., dimensions={0} | all-to-all | bytes 1048576 | tf_op jit(solution)/shard_map/all_to_all | solution.py:463
  35.8 2.1 boxes.1
  37.9 22.9 %all_to_all.36.own_ref = f32[32,40,128]{2,1,0:T(8,128)S(1)} all-to-all(f32[32,40,128]{2,1,0:T(8,128)} %boxes.1), channel_id=1, replica_groups={{0,16,32,48,64,80,96,112,128,144,160,176,192,208,224,240,256,272,288,30..., dimensions={0} | all-to-all | bytes 1310720 | tf_op jit(solution)/shard_map/all_to_all | solution.py:466
  60.9 5.6 %collective-permute-start = (f32[32,40,128]{2,1,0:T(8,128)S(1)}, f32[32,40,128]{2,1,0:T(8,128)S(1)}, u32[]{:S(2)}, u32[]{:S(2)}) collective-permute-start(f32[32,40,128]{2,1,0:T(8,128)S(1)} %all_to_all.36.own_ref), channel_id=1, source_target_pairs={{0,8},{8,0},{16,24},{24,16},{32,40},{40,32},{48,56},{56,48},{64,72... | collective-permute-start | bytes 1966088 | tf_op jit(solution)/shard_map/ppermute | solution.py:444
  66.5 1.9 collective-permute-start.1
  68.4 1.9 collective-permute-done.1.othp_ref
  70.3 0.8 broadcast_in_dim.6.strength_ref
  71.1 0.2 copy-done.2
  71.3 22.3 %chebyshev.1 = f32[1536,128]{1,0:T(8,128)} custom-call(s32[3,64]{1,0:T(4,128)} %pad_add_fusion.at_ref, s32[5]{0:T(128)} %stack.35.pos_ref, f32[64,128]{1,0:T(8,128)} %broadcast_in_dim.6.strength_ref, bf16[128,256]{1,0:T(8,128)(2,1)} %constant.72.tapy_ref, bf16[96,48]{1,0:T(8,128)(2,1)} %constant.77.tapz_ref, f32[32,40,128]{2,1,0:T(8,128)} %copy-done.1, ...), custom_call_target="tpu_custom_call" | custom-call | tf_op jit(solution)/shard_map/chebyshev/pallas_call | solution.py:300
  93.6 37.6 %all_to_all.37 = f32[256,3,2,128]{3,2,1,0:T(2,128)} all-to-all(f32[256,3,2,128]{3,2,1,0:T(2,128)} %bitcast.20), channel_id=1, replica_groups={{0,16,32,48,64,80,96,112,128,144,160,176,192,208,224,240,256,272,288,30..., dimensions={0} | all-to-all | bytes 1572864 | tf_op jit(solution)/shard_map/all_to_all | solution.py:470
  131.2 2.9 %gram.1 = f32[16,40,128]{2,1,0:T(8,128)} custom-call(f32[1536,128]{1,0:T(8,128)} %bitcast.18), custom_call_target="tpu_custom_call" | custom-call | tf_op jit(solution)/shard_map/gram/pallas_call | solution.py:421
  134.1 14.5 %all_to_all.38 = f32[16,40,128]{2,1,0:T(8,128)S(1)} all-to-all(f32[16,40,128]{2,1,0:T(8,128)} %gram.1), channel_id=1, replica_groups={{0,8,16,24,32,40,48,56,64,72,80,88,96,104,112,120},{128,136,144,152,160..., dimensions={0} | all-to-all | bytes 655360 | tf_op jit(solution)/shard_map/all_to_all | solution.py:448
  148.7 21.6 %all_to_all.39 = f32[32,40,128]{2,1,0:T(8,128)S(1)} all-to-all(f32[32,40,128]{2,1,0:T(8,128)S(1)} %broadcast_in_dim.7), channel_id=1, replica_groups={{0,1,2,3,4,5,6,7,128,129,130,131,132,133,134,135,256,257,258,259,260,26..., dimensions={0} | all-to-all | bytes 1310720 | tf_op jit(solution)/shard_map/all_to_all | solution.py:451
  170.3 0.1 reduce_sum.19
  170.3 16.1 %all_to_all.40.total_ref = f32[16,40,128]{2,1,0:T(8,128)} all-to-all(f32[16,40,128]{2,1,0:T(8,128)S(1)} %broadcast_in_dim.8), channel_id=1, replica_groups={{0,8,16,24,32,40,48,56,64,72,80,88,96,104,112,120},{128,136,144,152,160..., dimensions={0} | all-to-all | bytes 655360 | tf_op jit(solution)/shard_map/all_to_all | solution.py:454
  186.4 68.7 %ortho.1 = (f32[768,128]{1,0:T(8,128)}, f32[32,256]{1,0:T(8,128)}) custom-call(s32[5]{0:T(128)} %stack.35.pos_ref, f32[16,40,128]{2,1,0:T(8,128)} %all_to_all.40.total_ref, f32[1536,128]{1,0:T(8,128)} %bitcast.19), custom_call_target="tpu_custom_call" | custom-call | tf_op jit(solution)/shard_map/ortho/pallas_call | solution.py:432
  255.1 17.6 %all_to_all.41 = f32[8,96,128]{2,1,0:T(8,128)S(1)} all-to-all(f32[8,96,128]{2,1,0:T(8,128)} %bitcast.24), channel_id=1, replica_groups=mesh['dom'=64,'band'=8] {'band'}, dimensions={0} | all-to-all | bytes 786432 | tf_op jit(solution)/shard_map/all_to_all | solution.py:474
  272.7 0.2 copy.19
  272.9 0.8 copy.22
  (18 shorter events, 0.1 us)
Async XLA Ops:
  0.7 0.7 copy-start.4
  0.7 0.7 copy-start.5
  0.7 0.7 copy-start.6
  37.9 28.5 %copy-start = (f32[32,32,128]{2,1,0:T(8,128)S(1)}, f32[32,32,128]{2,1,0:T(8,128)}, u32[]{:S(2)}) copy-start(f32[32,32,128]{2,1,0:T(8,128)} %all_to_all.35.got_ref.ownp_ref) | copy-start | bytes 1572868
  37.9 30.5 %copy-start.7 = (f32[64]{0:T(128)S(1)}, f32[64]{0:T(128)}, u32[]{:S(2)}) copy-start(f32[64]{0:T(128)} %param.12) | copy-start | bytes 772
  60.9 10.2 %copy-start.1 = (f32[32,40,128]{2,1,0:T(8,128)}, f32[32,40,128]{2,1,0:T(8,128)S(1)}, u32[]{:S(2)}) copy-start(f32[32,40,128]{2,1,0:T(8,128)S(1)} %all_to_all.36.own_ref) | copy-start | bytes 1966084
  60.9 9.4 %collective-permute-start = (f32[32,40,128]{2,1,0:T(8,128)S(1)}, f32[32,40,128]{2,1,0:T(8,128)S(1)}, u32[]{:S(2)}, u32[]{:S(2)}) collective-permute-start(f32[32,40,128]{2,1,0:T(8,128)S(1)} %all_to_all.36.own_ref), channel_id=1, source_target_pairs={{0,8},{8,0},{16,24},{24,16},{32,40},{40,32},{48,56},{56,48},{64,72... | collective-permute-start | bytes 1966088 | tf_op jit(solution)/shard_map/ppermute | solution.py:444
  66.5 3.8 %collective-permute-start.1 = (f32[32,32,128]{2,1,0:T(8,128)S(1)}, f32[32,32,128]{2,1,0:T(8,128)S(1)}, u32[]{:S(2)}, u32[]{:S(2)}) collective-permute-start(f32[32,32,128]{2,1,0:T(8,128)S(1)} %copy-done), channel_id=1, source_target_pairs={{0,8},{8,0},{16,24},{24,16},{32,40},{40,32},{48,56},{56,48},{64,72... | collective-permute-start | bytes 1572872 | tf_op jit(solution)/shard_map/ppermute | solution.py:444
  70.3 0.8 copy-start.3
  70.3 1.0 copy-start.2

commit v4 on v3

--- a/solution.py
+++ b/solution.py
@@ -29,6 +29,10 @@
 P2_ROWS = 40
 
 
+def place():
+    return lax.axis_index("dom"), lax.axis_index("band")
+
+
 def vmem():
     return pl.BlockSpec(memory_space=pltpu.VMEM)
 
@@ -41,7 +45,10 @@
     return pltpu.CompilerParams(vmem_limit_bytes=56 * 1024 * 1024)
 
 
-def pack_kernel(at_ref, pos_ref, proj_ref, pot_ref, out_ref, pad_ref):
+def pack_kernel(z_ref, x_ref, y_ref, proj_ref, pot_ref, out_ref, pad_ref):
+    me, _ = place()
+    z_first = (me >> 3) * 6
+    x_first = (me & 7) * 8
     pad_ref[:, 24:48, :] = jnp.zeros((64, 24, 128), F32)
     pad_ref[:, 0:24, :] = proj_ref[...]
     lane = lax.broadcasted_iota(jnp.int32, (8, 128), 1)
@@ -50,16 +57,16 @@
     z_cells, x_cells, slots = [], [], []
     for s in range(6):
         row = s + 6 * sub
-        z_cells.append(pos_ref[0] + row // 4)
-        x_cells.append(pos_ref[1] + 2 * (row % 4) + lane // 64)
+        z_cells.append(z_first + row // 4)
+        x_cells.append(x_first + 2 * (row % 4) + lane // 64)
         slots.append((slot_lane >= 10 * s) & (slot_lane < 10 * s + 10))
 
     def pair(i, carry):
         for m in range(2):
             a = 2 * i + m
-            z0 = at_ref[0, a]
-            x0 = at_ref[1, a]
-            y0 = at_ref[2, a]
+            z0 = z_ref[a]
+            x0 = x_ref[a]
+            y0 = y_ref[a]
             packed = jnp.zeros((8, 128), F32)
             for s in range(6):
                 z, x = z_cells[s], x_cells[s]
@@ -79,7 +86,8 @@
     return (4 * z0 * 171) >> 10
 
 
-def boxes_kernel(at_ref, pos_ref, got_ref, orb_ref, out_ref, col_ref):
+def boxes_kernel(z_ref, got_ref, orb_ref, out_ref, col_ref):
+    me, _ = place()
     col_ref[...] = jnp.zeros_like(col_ref)
     for zb in range(8):
         part = got_ref[4 * zb, 0:8, :]
@@ -89,7 +97,7 @@
         col_ref[1, 4 * zb : 4 * zb + 4, :] = part[4:8]
     boxes = []
     for m in range(2):
-        z0 = at_ref[0, 2 * pos_ref[2] + m]
+        z0 = z_ref[2 * (me >> 1) + m]
         boxes.append(col_ref[m, pl.ds(first_row(z0), 8), :])
 
     def send(n, carry):
@@ -102,12 +110,14 @@
 
 
 def filter_kernel(
-    at_ref, pos_ref, strength_ref, tapy_ref, tapz_ref, own_ref, oth_ref, ownp_ref, othp_ref, out_ref,
+    z_ref, x_ref, y_ref, strength_ref, tapy_ref, tapz_ref, pick_ref, own_ref, oth_ref, ownp_ref, othp_ref, out_ref,
     fld, pot, half, tiles, parts, scaled,
 ):
-    core = pos_ref[3]
-    fld[...] = jnp.zeros_like(fld)
-    tiles[...] = jnp.zeros_like(tiles)
+    core = place()[0] & 1
+    for edge in (slice(0, 3), slice(35, 38)):
+        fld[:, edge, :, :] = jnp.zeros((3, 3, 64, 128), F32)
+    for edge in (slice(0, 8), slice(56, 64)):
+        fld[:, 3:35, edge, :] = jnp.zeros((3, 32, 8, 128), F32)
     for src, src_pot, c in ((own_ref, ownp_ref, core), (oth_ref, othp_ref, 1 - core)):
         for i in range(32):
             zb, q = i // 4, i % 4
@@ -116,29 +126,28 @@
                 fld[0, 3 + xp, 8 + 6 * zb : 14 + 6 * zb, :] = src.at[i][pl.ds(16 + j, 6, stride=4), :]
                 pot[xp, 6 * zb : 6 * zb + 6, :] = src_pot.at[i][pl.ds(8 + j, 6, stride=4), :]
 
-    half[pl.ds(core, 1)] = own_ref[:, 0:16, :].reshape(1, 64, 8, 128)
-    half[pl.ds(1 - core, 1)] = oth_ref[:, 0:16, :].reshape(1, 64, 8, 128)
-    slot_lane = lax.broadcasted_iota(jnp.int32, (4, 128), 1) & 63
+    half[:, pl.ds(pl.multiple_of(8 * core, 8), 8), :] = own_ref[:, 0:16, :].reshape(64, 8, 128)
+    half[:, pl.ds(pl.multiple_of(8 - 8 * core, 8), 8), :] = oth_ref[:, 0:16, :].reshape(64, 8, 128)
+    slot_lane = lax.broadcasted_iota(jnp.int32, (16, 128), 1) & 63
+    in_slot = [(slot_lane >= 10 * n) & (slot_lane < 10 * n + 10) for n in range(6)]
 
     def expand(a, carry):
-        xs = jnp.minimum(at_ref[1, a] >> 1, 26)
-        y0 = at_ref[2, a]
-        z0 = at_ref[0, a]
+        xs = jnp.minimum(x_ref[a] >> 1, 26)
+        y0 = y_ref[a]
+        z0 = z_ref[a]
         begin = 4 * z0 - 6 * first_row(z0)
-        for w in range(6):
-            xp = xs + w
-            for v in range(3):
-                n = 4 if v == 0 else 3
-                place = begin + (xp & 3) + 4 * v
-                row = (place * 11) >> 6
-                left = 10 * (place - 6 * row)
-                box = half[(xp >> 2) & 1, a, pl.ds(row, n, stride=2), :]
-                in_slot = (slot_lane[0:n] >= left) & (slot_lane[0:n] < left + 10)
-                box = jnp.where(in_slot, box, 0.0)
-                tiles[6 * a + w, pl.ds(v, n, stride=3), :] = pltpu.roll(box, (128 + y0 - left) & 127, 1)
+        box = half[a]
+        moved = [
+            pltpu.roll(jnp.where(in_slot[n], box, 0.0), (128 + y0 - 10 * n) & 127, 1) for n in range(6)
+        ]
+        high, rest = parts_of(jnp.concatenate(moved, axis=0))
+        pick = pick_ref[4 * begin + (xs & 7)]
+        got = jnp.dot(pick, high, preferred_element_type=F32)
+        got = got + jnp.dot(pick, rest, preferred_element_type=F32)
+        tiles[pl.ds(6 * a, 6)] = got.reshape(6, 16, 128)
         return carry
 
-    lax.fori_loop(0, 64, expand, 0, unroll=4)
+    lax.fori_loop(0, 64, expand, 0, unroll=16)
 
     ones = jnp.ones((128, 128), F32)
     low_half = lax.broadcasted_iota(jnp.int32, (8, 128), 1) < 64
@@ -146,16 +155,16 @@
 
     def step(cur, nxt, prev, ca, cb, cg):
         def inner(a, carry):
-            xs = jnp.minimum(at_ref[1, a] >> 1, 26)
-            z0 = at_ref[0, a]
+            xs = jnp.minimum(x_ref[a] >> 1, 26)
+            z0 = z_ref[a]
             win = fld[cur, pl.ds(3 + xs, 6), pl.ds(8 + z0, 16), :]
             prod = jnp.sum(win * tiles[pl.ds(6 * a, 6)], axis=0)
             parts[pl.ds(a, 1), :] = jnp.sum(prod, axis=0, keepdims=True)
             return carry
 
-        lax.fori_loop(0, 64, inner, 0, unroll=8)
+        lax.fori_loop(0, 64, inner, 0, unroll=16)
         sums = jnp.dot(parts[...], ones, precision=HIGH, preferred_element_type=F32)
-        scaled[...] = sums * (ca * strength_ref[...])
+        scaled[...] = sums
 
         def along_yz(t, carry):
             rows = fld[cur, pl.ds(3 + 4 * t, 4), 8:56, :]
@@ -207,13 +216,14 @@
                 here = after
             return carry
 
-        lax.fori_loop(0, 6, along_x, 0)
+        lax.fori_loop(0, 6, along_x, 0, unroll=2)
 
         def outer(a, carry):
-            xs = jnp.minimum(at_ref[1, a] >> 1, 26)
-            z0 = at_ref[0, a]
+            xs = jnp.minimum(x_ref[a] >> 1, 26)
+            z0 = z_ref[a]
             win = (nxt, pl.ds(3 + xs, 6), pl.ds(8 + z0, 16), slice(None))
-            fld[win] = fld[win] + scaled[pl.ds(a, 1), :][None] * tiles[pl.ds(6 * a, 6)]
+            weight = scaled[pl.ds(a, 1), :] * (strength_ref[a] * (ca / PROJ_CELLS))
+            fld[win] = fld[win] + weight[None] * tiles[pl.ds(6 * a, 6)]
             return carry
 
         lax.fori_loop(0, 64, outer, 0, unroll=4)
@@ -248,6 +258,18 @@
     return taps
 
 
+def box_rows():
+    pick = np.zeros((24, 96, 96), np.float32)
+    for begin in (0, 2, 4):
+        for first in range(8):
+            for w in range(6):
+                xp = first + w
+                for z in range(10):
+                    row, slot = divmod(begin + xp % 4 + 4 * z, 6)
+                    pick[4 * begin + first, 16 * w + z, 16 * slot + 8 * (xp // 4 % 2) + row] = 1.0
+    return pick
+
+
 def two_parts(taps, axis):
     high = jnp.asarray(taps).astype(jnp.bfloat16)
     rest = (jnp.asarray(taps) - high.astype(F32)).astype(jnp.bfloat16)
@@ -262,57 +284,71 @@
     return [[(2 * i + c) * 8 + y for y in range(8) for i in range(32)] for c in range(2)]
 
 
-def x_groups():
-    return [[16 * z + i for i in range(16)] for z in range(4)]
-
-
-def zy_groups():
-    return [[(16 * z + i) * 8 + y for z in range(4) for y in range(8)] for i in range(16)]
-
-
-def pack(at, pos, proj, pot):
+def near_groups():
+    return [
+        [(16 * z + 2 * x + c) * 8 + 2 * t + u for x in range(8) for u in range(2)]
+        for z in range(4)
+        for c in range(2)
+        for t in range(4)
+    ]
+
+
+def far_groups():
+    return [
+        [(16 * z + 2 * x + c) * 8 + 2 * t + u for z in range(4) for t in range(4)]
+        for x in range(8)
+        for c in range(2)
+        for u in range(2)
+    ]
+
+
+def exchange(values, groups):
+    return lax.all_to_all(values, ("dom", "band"), 0, 0, tiled=True, axis_index_groups=groups)
+
+
+def pack(at, proj, pot):
     return pl.pallas_call(
         pack_kernel,
         out_shape=jax.ShapeDtypeStruct((32, P1_ROWS, 128), F32),
-        in_specs=[smem(), smem(), vmem(), vmem()],
+        in_specs=[smem()] * 3 + [vmem()] * 2,
         out_specs=vmem(),
         scratch_shapes=[pltpu.VMEM((64, 48, 128), F32)],
         compiler_params=params(),
         name="pack",
-    )(at, pos, proj, pot)
-
-
-def boxes(at, pos, got, orb):
+    )(*at, proj, pot)
+
+
+def boxes(at, got, orb):
     return pl.pallas_call(
         boxes_kernel,
         out_shape=jax.ShapeDtypeStruct((32, P2_ROWS, 128), F32),
-        in_specs=[smem(), smem(), vmem(), vmem()],
+        in_specs=[smem()] + [vmem()] * 2,
         out_specs=vmem(),
         scratch_shapes=[pltpu.VMEM((2, 40, 128), F32)],
         compiler_params=params(),
         name="boxes",
-    )(at, pos, got, orb)
-
-
-def chebyshev(at, pos, strength, own, oth, own_pot, oth_pot):
+    )(at[0], got, orb)
+
+
+def chebyshev(at, strength, own, oth, own_pot, oth_pot):
     tapy = two_parts(band_matrix(NY, 2), 1)
     tapz = two_parts(band_matrix(48, 1), 0)
     return pl.pallas_call(
         filter_kernel,
         out_shape=jax.ShapeDtypeStruct((1536, 128), F32),
-        in_specs=[smem(), smem()] + [vmem()] * 7,
+        in_specs=[smem()] * 4 + [vmem()] * 7,
         out_specs=vmem(),
         scratch_shapes=[
             pltpu.VMEM((3, 38, 64, 128), F32),
             pltpu.VMEM((32, 48, 128), F32),
-            pltpu.VMEM((2, 64, 8, 128), F32),
+            pltpu.VMEM((64, 16, 128), F32),
             pltpu.VMEM((64 * 6, 16, 128), F32),
             pltpu.VMEM((64, 128), F32),
             pltpu.VMEM((64, 128), F32),
         ],
         compiler_params=params(),
         name="chebyshev",
-    )(at, pos, strength, tapy, tapz, own, oth, own_pot, oth_pot)
+    )(*at, strength, tapy, tapz, jnp.asarray(box_rows(), jnp.bfloat16), own, oth, own_pot, oth_pot)
 
 
 def dot(a, b):
@@ -323,37 +359,55 @@
     return lax.dot_general(a, b, (((1,), (1,)), ((), ())), precision=HIGH, preferred_element_type=F32)
 
 
-def gram_kernel(both_ref, out_ref):
-    f = [both_ref[pl.ds(r, 256, stride=6), :] for r in range(3)]
-    g = [both_ref[pl.ds(3 + r, 256, stride=6), :] for r in range(3)]
-    f = jnp.concatenate(f, axis=1)
-    g = jnp.concatenate(g, axis=1)
-    corr = dot_t(f, f)
-    ham = dot_t(f, g)
+def parts_of(a):
+    high = a.astype(jnp.bfloat16)
+    return high, (a - high.astype(F32)).astype(jnp.bfloat16)
+
+
+def dot_parts(a, b, turn=False):
+    dims = (((1,), (1 if turn else 0,)), ((), ()))
+    (ah, ar), (bh, br) = a, b
+    total = lax.dot_general(ah, br, dims, preferred_element_type=F32)
+    total = total + lax.dot_general(ar, bh, dims, preferred_element_type=F32)
+    return total + lax.dot_general(ah, bh, dims, preferred_element_type=F32)
+
+
+def gram_kernel(both_ref, mine_ref, other_ref):
+    core = place()[0] & 1
+    f = jnp.concatenate([both_ref[pl.ds(r, 256, stride=6), :] for r in range(3)], axis=1)
+    g = jnp.concatenate([both_ref[pl.ds(3 + r, 256, stride=6), :] for r in range(3)], axis=1)
+    f = parts_of(f)
+    corr = dot_parts(f, f, True)
+    ham = dot_parts(f, parts_of(g), True)
     row = lax.broadcasted_iota(jnp.int32, (256, 256), 0)
     col = lax.broadcasted_iota(jnp.int32, (256, 256), 1)
     packed = jnp.where(row >= col, corr, ham)
     diag = jnp.sum(jnp.where(row == col, ham, 0.0), axis=0, keepdims=True)
-    out_ref[...] = jnp.zeros_like(out_ref)
-    for q in range(16):
-        out_ref[q, 0:16, :] = packed[16 * q : 16 * q + 16, 0:128]
-        out_ref[q, 16:32, :] = packed[16 * q : 16 * q + 16, 128:256]
-    out_ref[0, 32:33, :] = diag[:, 0:128]
-    out_ref[0, 33:34, :] = diag[:, 128:256]
-
-
-def ortho_kernel(pos_ref, total_ref, both_ref, rot_ref, proj_ref, corr, ham, inv, work):
+    for ref, first in ((mine_ref, core == 0), (other_ref, core == 1)):
+        half = jnp.where(first, packed[:, 0:128], packed[:, 128:256])
+        for q in range(16):
+            ref[q, 0:16, :] = half[16 * q : 16 * q + 16]
+            ref[q, 16:24, :] = jnp.zeros((8, 128), F32)
+        ref[0, 16:17, :] = jnp.where(first, diag[:, 0:128], diag[:, 128:256])
+
+
+def ortho_kernel(own_ref, oth_ref, both_ref, rot_ref, proj_ref, corr, ham, inv, work):
+    me, block = place()
+    core = me & 1
     row = lax.broadcasted_iota(jnp.int32, (256, 256), 0)
     col = lax.broadcasted_iota(jnp.int32, (256, 256), 1)
     below = row > col
     same = row == col
     scale = 1.0 / NCELLS
-    for q in range(16):
-        work[16 * q : 16 * q + 16, 0:128] = total_ref[q, 0:16, :]
-        work[16 * q : 16 * q + 16, 128:256] = total_ref[q, 16:32, :]
+    diag = []
+    for h in range(2):
+        for q in range(16):
+            half = jnp.where(core == h, own_ref[q, 0:16, :], oth_ref[q, 0:16, :])
+            work[16 * q : 16 * q + 16, 128 * h : 128 * h + 128] = half
+        diag.append(jnp.where(core == h, own_ref[0, 16:17, :], oth_ref[0, 16:17, :]))
     packed = work[...] * scale
     turned = packed.T
-    diag = jnp.concatenate([total_ref[0, 32:33, :], total_ref[0, 33:34, :]], axis=1) * scale
+    diag = jnp.concatenate(diag, axis=1) * scale
     corr[...] = jnp.where(row >= col, packed, turned)
     ham[...] = jnp.where(same, diag, jnp.where(below, turned, packed))
 
@@ -386,12 +440,12 @@
 
     def going(state):
         count, size = state
-        return (count < 8) & jnp.logical_not(size < 1e-8)
+        return (count < 8) & jnp.logical_not(size < 1e-6)
 
     _, size = lax.while_loop(going, refine, (jnp.int32(0), jnp.float32(1.0)))
     least = jnp.min(jnp.where(same, inv[...], 1.0))
 
-    @pl.when(jnp.logical_not((size < 1e-8) & (least > 0.0)))
+    @pl.when(jnp.logical_not((size < 1e-6) & (least > 0.0)))
     def _():
         work[...] = corr[...]
         inv[...] = jnp.where(same, 1.0, 0.0)
@@ -410,34 +464,35 @@
         lax.fori_loop(0, 256, column, 0)
 
     x = inv[...]
-    mine = inv[pl.ds(pl.multiple_of(32 * pos_ref[4], 32), 32), :]
+    mine = inv[pl.ds(pl.multiple_of(32 * block, 32), 32), :]
     proj_ref[...] = dot_t(dot(mine, ham[...]), x)
+    f = jnp.concatenate([both_ref[pl.ds(r, 256, stride=6), :] for r in range(3)], axis=1)
+    turned = dot_parts(parts_of(x), parts_of(f))
     for r in range(3):
-        part = dot(x, both_ref[pl.ds(r, 256, stride=6), :])
-        rot_ref[pl.ds(r, 256, stride=3), :] = part
+        rot_ref[pl.ds(r, 256, stride=3), :] = turned[:, 128 * r : 128 * r + 128]
 
 
 def gram(both):
     return pl.pallas_call(
         gram_kernel,
-        out_shape=jax.ShapeDtypeStruct((16, 40, 128), F32),
+        out_shape=[jax.ShapeDtypeStruct((16, 24, 128), F32)] * 2,
         in_specs=[vmem()],
-        out_specs=vmem(),
+        out_specs=[vmem()] * 2,
         compiler_params=params(),
         name="gram",
     )(both)
 
 
-def ortho(pos, total, both):
+def ortho(own, oth, both):
     return pl.pallas_call(
         ortho_kernel,
         out_shape=[jax.ShapeDtypeStruct((768, 128), F32), jax.ShapeDtypeStruct((32, 256), F32)],
-        in_specs=[smem(), vmem(), vmem()],
-        out_specs=[vmem(), vmem()],
+        in_specs=[vmem()] * 3,
+        out_specs=[vmem()] * 2,
         scratch_shapes=[pltpu.VMEM((256, 256), F32)] * 4,
         compiler_params=params(),
         name="ortho",
-    )(pos, total, both)
+    )(own, oth, both)
 
 
 def swap_cores(values):
@@ -445,32 +500,27 @@
 
 
 def sum_everywhere(values):
-    mine = lax.all_to_all(values, "dom", 0, 0, tiled=True, axis_index_groups=x_groups())
-    mine = jnp.sum(mine, axis=0)
-    spread = jnp.broadcast_to(mine[None], (32,) + mine.shape)
-    spread = lax.all_to_all(spread, ("dom", "band"), 0, 0, tiled=True, axis_index_groups=zy_groups())
-    mine = jnp.sum(spread, axis=0)
-    spread = jnp.broadcast_to(mine[None], (16,) + mine.shape)
-    return lax.all_to_all(spread, "dom", 0, 0, tiled=True, axis_index_groups=x_groups())
+    for groups in (near_groups(), far_groups()):
+        part = jnp.sum(exchange(values, groups), axis=0)
+        values = jnp.broadcast_to(part[None], values.shape)
+    return exchange(values, near_groups())
 
 
 def on_device(orbitals, potential, proj_shape, proj_strength, atom_z, atom_x, atom_y):
-    me = lax.axis_index("dom")
-    at = jnp.stack([atom_z, atom_x, atom_y])
-    pos = jnp.stack([me // 8 * 6, me % 8 * 8, me // 2, me % 2, lax.axis_index("band")]).astype(jnp.int32)
-    strength = jnp.broadcast_to((proj_strength / PROJ_CELLS)[:, None], (64, 128))
-    first = pack(at, pos, proj_shape.reshape(64, 24, 128), potential.reshape(24, 128))
+    at = (atom_z, atom_x, atom_y)
+    first = pack(at, proj_shape.reshape(64, 24, 128), potential.reshape(24, 128))
     first = lax.all_to_all(first, "dom", 0, 0, tiled=True, axis_index_groups=same_core())
     first_oth = swap_cores(first)
-    second = boxes(at, pos, first, orbitals.reshape(32, 24, 128))
+    second = boxes(at, first, orbitals.reshape(32, 24, 128))
     second = lax.all_to_all(second, "dom", 0, 0, tiled=True, axis_index_groups=same_core())
     second_oth = swap_cores(second)
-    both = chebyshev(at, pos, strength, second, second_oth, first, first_oth)
+    both = chebyshev(at, proj_strength, second, second_oth, first, first_oth)
     both = both.reshape(256, 3, 2, 128)
-    both = lax.all_to_all(both, ("dom", "band"), 0, 0, tiled=True, axis_index_groups=same_core_all())
+    both = exchange(both, same_core_all())
     both = both.reshape(1536, 128)
-    total = sum_everywhere(gram(both))
-    rotated, projected = ortho(pos, total, both)
+    mine, other = gram(both)
+    mine = sum_everywhere(mine + swap_cores(other))
+    rotated, projected = ortho(mine, swap_cores(mine), both)
     rotated = lax.all_to_all(rotated.reshape(8, 96, 128), "band", 0, 0, tiled=True)
     rotated = rotated.reshape(4, 2, 32, 3, 128).transpose(2, 1, 3, 0, 4)
     return (rotated.reshape(32, 1, 6, 512), projected)

time: 275 us -> 266 us (0.967)
  blocking collectives: 160 us -> 144 us
  starting transfers between devices: 7.49 us -> 18.2 us
  Pallas kernels: 99.1 us -> 93.5 us
    all_to_all x4, blocking collectives: 89.7 us -> 72.5 us  [exchange(): lax.all_to_all(values, ('dom', 'band'), 0, 0, tiled=True, axis_index_grou...]
    ppermute x2 -> x4, starting transfers between devices: 7.49 us -> 18.2 us  [swap_cores(): return lax.ppermute(values, 'dom', [(i, i ^ 1) for i in range(64)])]
    pallas_call x1, Pallas kernels: 22.3 us -> 17.5 us  [chebyshev(): pl.pallas_call(filter_kernel, out_shape=jax.ShapeDtypeStruct((1536, 128),...]
  transfers between devices with their start and end apart: 2 -> 4, of which waited for: 1 -> 3; matrix products, arithmetic and copies ran while one was open for 0% -> 0% of each run, Pallas kernels for 0% -> 0%
where the time goes in v4:
time: 266 us; the launch traced here: 265 us
  blocking collectives  144 us (54%)
  Pallas kernels  93.5 us (35%)
  starting transfers between devices  18.2 us (7%)
  waiting for transfers between devices  4.19 us (2%)
  local copies, waits for them, and re-layouts  3.47 us (1%)
    all_to_all x4, blocking collectives, exchange(): lax.all_to_all(values, ('dom', 'band'), 0, 0, tiled=True, axis_index_grou...  72.5 us
    pallas_call x1, Pallas kernels, ortho(): pl.pallas_call(ortho_kernel, out_shape=[jax.ShapeDtypeStruct((768, 128),...  68.4 us
    all_to_all x1, blocking collectives, on_device(): lax.all_to_all(first, 'dom', 0, 0, tiled=True, axis_index_groups=same_cor...  30.1 us
    all_to_all x1, blocking collectives, on_device(): lax.all_to_all(second, 'dom', 0, 0, tiled=True, axis_index_groups=same_co...  22.9 us
    all_to_all x1, blocking collectives, on_device(): lax.all_to_all(rotated.reshape(8, 96, 128), 'band', 0, 0, tiled=True)  18.5 us
    ppermute x4, starting transfers between devices, swap_cores(): return lax.ppermute(values, 'dom', [(i, i ^ 1) for i in range(64)])  18.2 us
    pallas_call x1, Pallas kernels, chebyshev(): pl.pallas_call(filter_kernel, out_shape=jax.ShapeDtypeStruct((1536, 128),...  17.5 us
  transfers between devices with their start and end apart: 4, of which 3 were waited for; matrix products, arithmetic and copies ran while one was open for 0% of the time, Pallas kernels for 0%

profile of v4, /device:TPU:1, one launch (start us, length us, event | category | flops | bytes accessed | tf_op | source)
XLA Modules:
  0.0 265.1 jit_solution(2961283538759968026)
XLA Ops:
  0.6 3.1 %pack.1 = f32[32,32,128]{2,1,0:T(8,128)} custom-call(s32[64]{0:T(128)} %z_ref.5, s32[64]{0:T(128)} %x_ref.3, s32[64]{0:T(128)} %y_ref.3, f32[64,24,128]{2,1,0:T(8,128)} %bitcast.14, f32[24,128]{1,0:T(8,128)} %bitcast.18), custom_call_target="tpu_custom_call" | custom-call | tf_op jit(solution)/shard_map/pack/pallas_call | solution.py:310
  3.7 30.1 %all_to_all.35.got_ref.ownp_ref = f32[32,32,128]{2,1,0:T(8,128)} all-to-all(f32[32,32,128]{2,1,0:T(8,128)} %pack.1), channel_id=1, replica_groups={{0,16,32,48,64,80,96,112,128,144,160,176,192,208,224,240,256,272,288,30..., dimensions={0} | all-to-all | bytes 1048576 | tf_op jit(solution)/shard_map/all_to_all | solution.py:512
  33.8 2.1 boxes.1
  35.9 22.9 %all_to_all.36.own_ref = f32[32,40,128]{2,1,0:T(8,128)S(1)} all-to-all(f32[32,40,128]{2,1,0:T(8,128)} %boxes.1), channel_id=1, replica_groups={{0,16,32,48,64,80,96,112,128,144,160,176,192,208,224,240,256,272,288,30..., dimensions={0} | all-to-all | bytes 1310720 | tf_op jit(solution)/shard_map/all_to_all | solution.py:515
  58.8 5.6 %collective-permute-start = (f32[32,40,128]{2,1,0:T(8,128)S(1)}, f32[32,40,128]{2,1,0:T(8,128)S(1)}, u32[]{:S(2)}, u32[]{:S(2)}) collective-permute-start(f32[32,40,128]{2,1,0:T(8,128)S(1)} %all_to_all.36.own_ref), channel_id=1, source_target_pairs={{0,8},{8,0},{16,24},{24,16},{32,40},{40,32},{48,56},{56,48},{64,72... | collective-permute-start | bytes 1966088 | tf_op jit(solution)/shard_map/ppermute | solution.py:499
  64.4 1.9 collective-permute-start.1
  66.3 1.9 collective-permute-done.1.othp_ref
  68.2 0.8 copy-done.4
  69.0 0.9 copy-done.3
  69.9 17.5 %chebyshev.1 = f32[1536,128]{1,0:T(8,128)} custom-call(s32[64]{0:T(128)} %z_ref.5, s32[64]{0:T(128)} %x_ref.3, s32[64]{0:T(128)} %y_ref.3, f32[64]{0:T(128)} %strength_ref.1, bf16[128,256]{1,0:T(8,128)(2,1)} %constant.18.tapy_ref, bf16[96,48]{1,0:T(8,128)(2,1)} %constant.23.tapz_ref, bf16[24,96,96]{2,1,0:T(8,128)(2,1)} %constant.10.clone.pick_ref, ...), custom_call_target="tpu_custom_call" | custom-call | tf_op jit(solution)/shard_map/chebyshev/pallas_call | solution.py:336
  87.3 37.6 %all_to_all.37 = f32[256,3,2,128]{3,2,1,0:T(2,128)} all-to-all(f32[256,3,2,128]{3,2,1,0:T(2,128)} %bitcast.12), channel_id=1, replica_groups={{0,16,32,48,64,80,96,112,128,144,160,176,192,208,224,240,256,272,288,30..., dimensions={0} | all-to-all | bytes 1572864 | tf_op jit(solution)/shard_map/all_to_all | solution.py:306
  124.9 2.5 gram.1
  127.4 4.2 %collective-permute-start.2 = (f32[16,24,128]{2,1,0:T(8,128)}, f32[16,24,128]{2,1,0:T(8,128)S(1)}, u32[]{:S(2)}, u32[]{:S(2)}) collective-permute-start(f32[16,24,128]{2,1,0:T(8,128)} %get-tuple-element.7), channel_id=1, source_target_pairs={{0,8},{8,0},{16,24},{24,16},{32,40},{40,32},{48,56},{56,48},{64,72... | collective-permute-start | bytes 589832 | tf_op jit(solution)/shard_map/ppermute | solution.py:499
  131.6 1.3 collective-permute-done.2
  132.9 0.9 add.3
  133.8 10.6 %all_to_all.38 = f32[16,24,128]{2,1,0:T(8,128)S(1)} all-to-all(f32[16,24,128]{2,1,0:T(8,128)S(1)} %add.3), channel_id=1, replica_groups={{0,1,16,17,32,33,48,49,64,65,80,81,96,97,112,113},{2,3,18,19,34,35,50,5..., dimensions={0} | all-to-all | bytes 393216 | tf_op jit(solution)/shard_map/all_to_all | solution.py:306
  144.5 14.9 %all_to_all.39 = f32[16,24,128]{2,1,0:T(8,128)S(1)} all-to-all(f32[16,24,128]{2,1,0:T(8,128)S(1)} %broadcast_in_dim.4), channel_id=1, replica_groups={{0,2,4,6,128,130,132,134,256,258,260,262,384,386,388,390},{1,3,5,7,129,..., dimensions={0} | all-to-all | bytes 393216 | tf_op jit(solution)/shard_map/all_to_all | solution.py:306
  159.5 9.4 %all_to_all.40.own_ref = f32[16,24,128]{2,1,0:T(8,128)S(1)} all-to-all(f32[16,24,128]{2,1,0:T(8,128)S(1)} %broadcast_in_dim.5), channel_id=1, replica_groups={{0,1,16,17,32,33,48,49,64,65,80,81,96,97,112,113},{2,3,18,19,34,35,50,5..., dimensions={0} | all-to-all | bytes 393216 | tf_op jit(solution)/shard_map/all_to_all | solution.py:306
  168.9 6.4 %collective-permute-start.3 = (f32[16,24,128]{2,1,0:T(8,128)S(1)}, f32[16,24,128]{2,1,0:T(8,128)S(1)}, u32[]{:S(2)}, u32[]{:S(2)}) collective-permute-start(f32[16,24,128]{2,1,0:T(8,128)S(1)} %all_to_all.40.own_ref), channel_id=1, source_target_pairs={{0,8},{8,0},{16,24},{24,16},{32,40},{40,32},{48,56},{56,48},{64,72... | collective-permute-start | bytes 589832 | tf_op jit(solution)/shard_map/ppermute | solution.py:499
  175.3 1.0 collective-permute-done.3.oth_ref
  176.4 0.7 copy-done.5
  177.0 68.4 %ortho.1 = (f32[768,128]{1,0:T(8,128)}, f32[32,256]{1,0:T(8,128)}) custom-call(f32[16,24,128]{2,1,0:T(8,128)} %copy-done.2, f32[16,24,128]{2,1,0:T(8,128)} %copy-done.5, f32[1536,128]{1,0:T(8,128)} %bitcast.11), custom_call_target="tpu_custom_call" | custom-call | tf_op jit(solution)/shard_map/ortho/pallas_call | solution.py:487
  245.5 18.5 %all_to_all.41 = f32[8,96,128]{2,1,0:T(8,128)S(1)} all-to-all(f32[8,96,128]{2,1,0:T(8,128)} %bitcast.16), channel_id=1, replica_groups=mesh['dom'=64,'band'=8] {'band'}, dimensions={0} | all-to-all | bytes 786432 | tf_op jit(solution)/shard_map/all_to_all | solution.py:524
  264.2 0.8 copy.23
  (15 shorter events, 0.3 us)
Async XLA Ops:
  35.9 28.5 %copy-start = (f32[32,32,128]{2,1,0:T(8,128)S(1)}, f32[32,32,128]{2,1,0:T(8,128)}, u32[]{:S(2)}) copy-start(f32[32,32,128]{2,1,0:T(8,128)} %all_to_all.35.got_ref.ownp_ref) | copy-start | bytes 1572868
  58.8 9.4 %copy-start.1 = (f32[32,40,128]{2,1,0:T(8,128)}, f32[32,40,128]{2,1,0:T(8,128)S(1)}, u32[]{:S(2)}) copy-start(f32[32,40,128]{2,1,0:T(8,128)S(1)} %all_to_all.36.own_ref) | copy-start | bytes 1966084
  58.8 9.4 %collective-permute-start = (f32[32,40,128]{2,1,0:T(8,128)S(1)}, f32[32,40,128]{2,1,0:T(8,128)S(1)}, u32[]{:S(2)}, u32[]{:S(2)}) collective-permute-start(f32[32,40,128]{2,1,0:T(8,128)S(1)} %all_to_all.36.own_ref), channel_id=1, source_target_pairs={{0,8},{8,0},{16,24},{24,16},{32,40},{40,32},{48,56},{56,48},{64,72... | collective-permute-start | bytes 1966088 | tf_op jit(solution)/shard_map/ppermute | solution.py:499
  64.4 3.8 %collective-permute-start.1 = (f32[32,32,128]{2,1,0:T(8,128)S(1)}, f32[32,32,128]{2,1,0:T(8,128)S(1)}, u32[]{:S(2)}, u32[]{:S(2)}) collective-permute-start(f32[32,32,128]{2,1,0:T(8,128)S(1)} %copy-done), channel_id=1, source_target_pairs={{0,8},{8,0},{16,24},{24,16},{32,40},{40,32},{48,56},{56,48},{64,72... | collective-permute-start | bytes 1572872 | tf_op jit(solution)/shard_map/ppermute | solution.py:499
  68.2 0.8 copy-start.4
  69.0 0.9 copy-start.3
  127.4 5.5 %collective-permute-start.2 = (f32[16,24,128]{2,1,0:T(8,128)}, f32[16,24,128]{2,1,0:T(8,128)S(1)}, u32[]{:S(2)}, u32[]{:S(2)}) collective-permute-start(f32[16,24,128]{2,1,0:T(8,128)} %get-tuple-element.7), channel_id=1, source_target_pairs={{0,8},{8,0},{16,24},{24,16},{32,40},{40,32},{48,56},{56,48},{64,72... | collective-permute-start | bytes 589832 | tf_op jit(solution)/shard_map/ppermute | solution.py:499
  168.9 7.5 %copy-start.2 = (f32[16,24,128]{2,1,0:T(8,128)}, f32[16,24,128]{2,1,0:T(8,128)S(1)}, u32[]{:S(2)}) copy-start(f32[16,24,128]{2,1,0:T(8,128)S(1)} %all_to_all.40.own_ref) | copy-start | bytes 589828
  168.9 7.5 %collective-permute-start.3 = (f32[16,24,128]{2,1,0:T(8,128)S(1)}, f32[16,24,128]{2,1,0:T(8,128)S(1)}, u32[]{:S(2)}, u32[]{:S(2)}) collective-permute-start(f32[16,24,128]{2,1,0:T(8,128)S(1)} %all_to_all.40.own_ref), channel_id=1, source_target_pairs={{0,8},{8,0},{16,24},{24,16},{32,40},{40,32},{48,56},{56,48},{64,72... | collective-permute-start | bytes 589832 | tf_op jit(solution)/shard_map/ppermute | solution.py:499
  176.4 0.7 copy-start.5

commit v5 on v4

--- a/solution.py
+++ b/solution.py
@@ -41,8 +41,8 @@
     return pl.BlockSpec(memory_space=pltpu.SMEM)
 
 
-def params():
-    return pltpu.CompilerParams(vmem_limit_bytes=56 * 1024 * 1024)
+def params(megabytes):
+    return pltpu.CompilerParams(vmem_limit_bytes=megabytes * 1024 * 1024)
 
 
 def pack_kernel(z_ref, x_ref, y_ref, proj_ref, pot_ref, out_ref, pad_ref):
@@ -313,7 +313,7 @@
         in_specs=[smem()] * 3 + [vmem()] * 2,
         out_specs=vmem(),
         scratch_shapes=[pltpu.VMEM((64, 48, 128), F32)],
-        compiler_params=params(),
+        compiler_params=params(8),
         name="pack",
     )(*at, proj, pot)
 
@@ -325,7 +325,7 @@
         in_specs=[smem()] + [vmem()] * 2,
         out_specs=vmem(),
         scratch_shapes=[pltpu.VMEM((2, 40, 128), F32)],
-        compiler_params=params(),
+        compiler_params=params(6),
         name="boxes",
     )(at[0], got, orb)
 
@@ -346,7 +346,7 @@
             pltpu.VMEM((64, 128), F32),
             pltpu.VMEM((64, 128), F32),
         ],
-        compiler_params=params(),
+        compiler_params=params(24),
         name="chebyshev",
     )(*at, strength, tapy, tapz, jnp.asarray(box_rows(), jnp.bfloat16), own, oth, own_pot, oth_pot)
 
@@ -372,9 +372,12 @@
     return total + lax.dot_general(ah, bh, dims, preferred_element_type=F32)
 
 
-def gram_kernel(both_ref, mine_ref, other_ref):
+def gram_kernel(both_ref, mine_ref, other_ref, f_ref):
     core = place()[0] & 1
-    f = jnp.concatenate([both_ref[pl.ds(r, 256, stride=6), :] for r in range(3)], axis=1)
+    f = [both_ref[pl.ds(r, 256, stride=6), :] for r in range(3)]
+    for r in range(3):
+        f_ref[r] = f[r]
+    f = jnp.concatenate(f, axis=1)
     g = jnp.concatenate([both_ref[pl.ds(3 + r, 256, stride=6), :] for r in range(3)], axis=1)
     f = parts_of(f)
     corr = dot_parts(f, f, True)
@@ -391,7 +394,7 @@
         ref[0, 16:17, :] = jnp.where(first, diag[:, 0:128], diag[:, 128:256])
 
 
-def ortho_kernel(own_ref, oth_ref, both_ref, rot_ref, proj_ref, corr, ham, inv, work):
+def ortho_kernel(own_ref, oth_ref, rows_ref, proj_ref, corr, ham, inv, work):
     me, block = place()
     core = me & 1
     row = lax.broadcasted_iota(jnp.int32, (256, 256), 0)
@@ -466,33 +469,51 @@
     x = inv[...]
     mine = inv[pl.ds(pl.multiple_of(32 * block, 32), 32), :]
     proj_ref[...] = dot_t(dot(mine, ham[...]), x)
-    f = jnp.concatenate([both_ref[pl.ds(r, 256, stride=6), :] for r in range(3)], axis=1)
-    turned = dot_parts(parts_of(x), parts_of(f))
-    for r in range(3):
-        rot_ref[pl.ds(r, 256, stride=3), :] = turned[:, 128 * r : 128 * r + 128]
+    rows_ref[...] = mine
+
+
+def rotate_kernel(rows_ref, all_ref, out_ref):
+    rows = parts_of(rows_ref[...])
+    for part in range(8):
+        j, kh = part // 2, part % 2
+        f = jnp.concatenate([all_ref[3 * part + t] for t in range(3)], axis=1)
+        turned = dot_parts(rows, parts_of(f))
+        for t in range(3):
+            out_ref[pl.ds((3 * kh + t) * 4 + j, 32, stride=24), :] = turned[:, 128 * t : 128 * t + 128]
 
 
 def gram(both):
     return pl.pallas_call(
         gram_kernel,
-        out_shape=[jax.ShapeDtypeStruct((16, 24, 128), F32)] * 2,
+        out_shape=[jax.ShapeDtypeStruct((16, 24, 128), F32)] * 2 + [jax.ShapeDtypeStruct((3, 256, 128), F32)],
         in_specs=[vmem()],
-        out_specs=[vmem()] * 2,
-        compiler_params=params(),
+        out_specs=[vmem()] * 3,
+        compiler_params=params(8),
         name="gram",
     )(both)
 
 
-def ortho(own, oth, both):
+def ortho(own, oth):
     return pl.pallas_call(
         ortho_kernel,
-        out_shape=[jax.ShapeDtypeStruct((768, 128), F32), jax.ShapeDtypeStruct((32, 256), F32)],
-        in_specs=[vmem()] * 3,
+        out_shape=[jax.ShapeDtypeStruct((32, 256), F32)] * 2,
+        in_specs=[vmem()] * 2,
         out_specs=[vmem()] * 2,
         scratch_shapes=[pltpu.VMEM((256, 256), F32)] * 4,
-        compiler_params=params(),
+        compiler_params=params(8),
         name="ortho",
-    )(own, oth, both)
+    )(own, oth)
+
+
+def rotate(rows, every):
+    return pl.pallas_call(
+        rotate_kernel,
+        out_shape=jax.ShapeDtypeStruct((768, 128), F32),
+        in_specs=[vmem()] * 2,
+        out_specs=vmem(),
+        compiler_params=params(12),
+        name="rotate",
+    )(rows, every)
 
 
 def swap_cores(values):
@@ -518,11 +539,11 @@
     both = both.reshape(256, 3, 2, 128)
     both = exchange(both, same_core_all())
     both = both.reshape(1536, 128)
-    mine, other = gram(both)
+    mine, other, filtered = gram(both)
+    every = lax.all_gather(filtered, "band", axis=0, tiled=True)
     mine = sum_everywhere(mine + swap_cores(other))
-    rotated, projected = ortho(mine, swap_cores(mine), both)
-    rotated = lax.all_to_all(rotated.reshape(8, 96, 128), "band", 0, 0, tiled=True)
-    rotated = rotated.reshape(4, 2, 32, 3, 128).transpose(2, 1, 3, 0, 4)
+    rows, projected = ortho(mine, swap_cores(mine))
+    rotated = rotate(rows, every)
     return (rotated.reshape(32, 1, 6, 512), projected)
 
 

time: 266 us -> 260 us (0.977)
  between operations: 0.71 us -> 14.2 us
  blocking collectives: 144 us -> 131 us
  Pallas kernels: 93.5 us -> 87.1 us
  local copies, waits for them, and re-layouts: 3.47 us -> 6.74 us
    all_to_all x1 -> x0, blocking collectives: 18.5 us -> none  [on_device(): lax.all_to_all(rotated.reshape(8, 96, 128), 'band', 0, 0, tiled=True)]
    all_to_all x4, blocking collectives: 72.5 us -> 78.3 us  [exchange(): lax.all_to_all(values, ('dom', 'band'), 0, 0, tiled=True, axis_index_grou...]
    unnamed x13 -> x28, local copies, waits for them, and re-layouts: 3.2 us -> 6.71 us
    pallas_call x1 -> x2, Pallas kernels: 68.4 us -> 68.3 us  [the longest x1 66.8 us: ortho(): pl.pallas_call(ortho_kernel, out_shape=[jax.ShapeDtypeStruct((32, 256), F...]
  transfers between devices with their start and end apart: 4 -> 5, of which waited for: 3 -> 3; matrix products, arithmetic and copies ran while one was open for 0% -> 0% of each run, Pallas kernels for 0% -> 26%
where the time goes in v5:
time: 260 us
  blocking collectives  131 us (50%)
  Pallas kernels  87.1 us (34%)
  starting transfers between devices  17.1 us (7%)
  between operations  14.2 us (5%)
  local copies, waits for them, and re-layouts  6.74 us (3%)
  waiting for transfers between devices  3.99 us (2%)
    all_to_all x4, blocking collectives, exchange(): lax.all_to_all(values, ('dom', 'band'), 0, 0, tiled=True, axis_index_grou...  78.3 us
    pallas_call x1, Pallas kernels, ortho(): pl.pallas_call(ortho_kernel, out_shape=[jax.ShapeDtypeStruct((32, 256), F...  66.8 us
    all_to_all x1, blocking collectives, on_device(): lax.all_to_all(first, 'dom', 0, 0, tiled=True, axis_index_groups=same_cor...  29.8 us
    all_to_all x1, blocking collectives, on_device(): lax.all_to_all(second, 'dom', 0, 0, tiled=True, axis_index_groups=same_co...  22.6 us
    ppermute x4, starting transfers between devices, swap_cores(): return lax.ppermute(values, 'dom', [(i, i ^ 1) for i in range(64)])  17 us
    pallas_call x1, Pallas kernels, chebyshev(): pl.pallas_call(filter_kernel, out_shape=jax.ShapeDtypeStruct((1536, 128),...  15.3 us
    unnamed x28, local copies, waits for them, and re-layouts  6.71 us
  transfers between devices with their start and end apart: 5, of which 3 were waited for; matrix products, arithmetic and copies ran while one was open for 0% of the time, Pallas kernels for 26%

profile of v5, /device:TPU:1, one launch (start us, length us, event | category | flops | bytes accessed | tf_op | source)
XLA Modules:
  0.0 259.8 jit_solution(8382769613544148928)
XLA Ops:
  7.3 1.1 copy-done.1
  8.4 0.7 copy-done.6
  9.1 0.7 copy-done.7
  9.8 0.7 copy-done.9
  11.1 1.7 pack.1
  12.7 29.8 %all_to_all.30.got_ref.ownp_ref = f32[32,32,128]{2,1,0:T(8,128)S(1)} all-to-all(f32[32,32,128]{2,1,0:T(8,128)S(1)} %pack.1), channel_id=1, replica_groups={{0,16,32,48,64,80,96,112,128,144,160,176,192,208,224,240,256,272,288,30..., dimensions={0} | all-to-all | bytes 1048576 | tf_op jit(solution)/shard_map/all_to_all | solution.py:533
  42.5 1.0 copy-done.3
  44.1 22.6 %all_to_all.31.own_ref = f32[32,40,128]{2,1,0:T(8,128)S(1)} all-to-all(f32[32,40,128]{2,1,0:T(8,128)S(1)} %boxes.1), channel_id=1, replica_groups={{0,16,32,48,64,80,96,112,128,144,160,176,192,208,224,240,256,272,288,30..., dimensions={0} | all-to-all | bytes 1310720 | tf_op jit(solution)/shard_map/all_to_all | solution.py:536
  66.7 5.6 %collective-permute-start = (f32[32,40,128]{2,1,0:T(8,128)S(1)}, f32[32,40,128]{2,1,0:T(8,128)S(1)}, u32[]{:S(2)}, u32[]{:S(2)}) collective-permute-start(f32[32,40,128]{2,1,0:T(8,128)S(1)} %all_to_all.31.own_ref), channel_id=1, source_target_pairs={{0,8},{8,0},{16,24},{24,16},{32,40},{40,32},{48,56},{56,48},{64,72... | collective-permute-start | bytes 1966088 | tf_op jit(solution)/shard_map/ppermute | solution.py:520
  72.3 1.9 collective-permute-start.1
  74.3 1.9 collective-permute-done.1.othp_ref
  76.2 15.3 %chebyshev.1 = f32[1536,128]{1,0:T(8,128)S(1)} custom-call(s32[64]{0:T(128)S(1)} %copy-done.8, s32[64]{0:T(128)S(1)} %copy-done.10, s32[64]{0:T(128)S(1)} %copy-done.12, f32[64]{0:T(128)S(1)} %copy-done.13, bf16[128,256]{1,0:T(8,128)(2,1)S(1)} %copy-done.4, bf16[96,48]{1,0:T(8,128)(2,1)S(1)} %copy-done.5, bf16[24,96,96]{2,1,0:T(8,128)(2,1)S(1)} %copy-done.2, ...), custom_call_target="tpu_custom_call" | custom-call | tf_op jit(solution)/shard_map/chebyshev/pallas_call | solution.py:336
  91.5 37.3 %all_to_all.32 = f32[256,3,2,128]{3,2,1,0:T(2,128)S(1)} all-to-all(f32[256,3,2,128]{3,2,1,0:T(2,128)S(1)} %bitcast.6), channel_id=1, replica_groups={{0,16,32,48,64,80,96,112,128,144,160,176,192,208,224,240,256,272,288,30..., dimensions={0} | all-to-all | bytes 1572864 | tf_op jit(solution)/shard_map/all_to_all | solution.py:306
  128.8 1.2 gram.1
  129.9 4.2 %collective-permute-start.2 = (f32[16,24,128]{2,1,0:T(8,128)S(1)}, f32[16,24,128]{2,1,0:T(8,128)S(1)}, u32[]{:S(2)}, u32[]{:S(2)}) collective-permute-start(f32[16,24,128]{2,1,0:T(8,128)S(1)} %get-tuple-element.8), channel_id=1, source_target_pairs={{0,8},{8,0},{16,24},{24,16},{32,40},{40,32},{48,56},{56,48},{64,72... | collective-permute-start | bytes 589832 | tf_op jit(solution)/shard_map/ppermute | solution.py:520
  134.2 1.0 collective-permute-done.2
  135.3 12.5 %all_to_all.33 = f32[16,24,128]{2,1,0:T(8,128)S(1)} all-to-all(f32[16,24,128]{2,1,0:T(8,128)S(1)} %add.3), channel_id=1, replica_groups={{0,1,16,17,32,33,48,49,64,65,80,81,96,97,112,113},{2,3,18,19,34,35,50,5..., dimensions={0} | all-to-all | bytes 393216 | tf_op jit(solution)/shard_map/all_to_all | solution.py:306
  147.8 17.8 %all_to_all.34 = f32[16,24,128]{2,1,0:T(8,128)S(1)} all-to-all(f32[16,24,128]{2,1,0:T(8,128)S(1)} %broadcast_in_dim.4), channel_id=1, replica_groups={{0,2,4,6,128,130,132,134,256,258,260,262,384,386,388,390},{1,3,5,7,129,..., dimensions={0} | all-to-all | bytes 393216 | tf_op jit(solution)/shard_map/all_to_all | solution.py:306
  165.6 10.8 %all_to_all.35.own_ref = f32[16,24,128]{2,1,0:T(8,128)S(1)} all-to-all(f32[16,24,128]{2,1,0:T(8,128)S(1)} %broadcast_in_dim.5), channel_id=1, replica_groups={{0,1,16,17,32,33,48,49,64,65,80,81,96,97,112,113},{2,3,18,19,34,35,50,5..., dimensions={0} | all-to-all | bytes 393216 | tf_op jit(solution)/shard_map/all_to_all | solution.py:306
  176.4 5.3 %collective-permute-start.3 = (f32[16,24,128]{2,1,0:T(8,128)S(1)}, f32[16,24,128]{2,1,0:T(8,128)S(1)}, u32[]{:S(2)}, u32[]{:S(2)}) collective-permute-start(f32[16,24,128]{2,1,0:T(8,128)S(1)} %all_to_all.35.own_ref), channel_id=1, source_target_pairs={{0,8},{8,0},{16,24},{24,16},{32,40},{40,32},{48,56},{56,48},{64,72... | collective-permute-start | bytes 589832 | tf_op jit(solution)/shard_map/ppermute | solution.py:520
  181.7 1.0 collective-permute-done.3.oth_ref
  182.8 66.8 %ortho.1 = (f32[32,256]{1,0:T(8,128)S(1)}, f32[32,256]{1,0:T(8,128)}) custom-call(f32[16,24,128]{2,1,0:T(8,128)S(1)} %all_to_all.35.own_ref, f32[16,24,128]{2,1,0:T(8,128)S(1)} %collective-permute-done.3.oth_ref), custom_call_target="tpu_custom_call" | custom-call | tf_op jit(solution)/shard_map/ortho/pallas_call | solution.py:497
  249.5 1.9 copy-done
  251.4 1.6 rotate.1
  (32 shorter events, 1.5 us)
Async XLA Ops:
  7.2 69.0 %copy-start.8 = (s32[64]{0:T(128)S(1)}, s32[64]{0:T(128)}, u32[]{:S(2)}) copy-start(s32[64]{0:T(128)} %z_ref.5) | copy-start | bytes 772
  7.2 69.0 %copy-start.10 = (s32[64]{0:T(128)S(1)}, s32[64]{0:T(128)}, u32[]{:S(2)}) copy-start(s32[64]{0:T(128)} %x_ref.3) | copy-start | bytes 772
  7.2 69.0 %copy-start.12 = (s32[64]{0:T(128)S(1)}, s32[64]{0:T(128)}, u32[]{:S(2)}) copy-start(s32[64]{0:T(128)} %y_ref.3) | copy-start | bytes 772
  7.2 69.0 %copy-start.13 = (f32[64]{0:T(128)S(1)}, f32[64]{0:T(128)}, u32[]{:S(2)}) copy-start(f32[64]{0:T(128)} %strength_ref.1) | copy-start | bytes 772
  7.2 242.3 %all-gather.2.cloned.1.call-start = ((), (), s32[]{:S(2)}) async-start(), calls=%async_computation.6 | async-start | bytes 3538944 | tf_op jit(solution)/shard_map/all_gather | solution.py:543
  7.3 1.1 copy-start.1
  8.4 0.7 copy-start.6
  9.1 0.7 copy-start.7
  9.7 0.7 copy-start.9
  10.4 0.7 copy-start.11
  11.1 65.1 %copy-start.2 = (bf16[24,96,96]{2,1,0:T(8,128)(2,1)S(1)}, bf16[24,96,96]{2,1,0:T(8,128)(2,1)}, u32[]{:S(2)}) copy-start(bf16[24,96,96]{2,1,0:T(8,128)(2,1)} %constant.10.clone.pick_ref) | copy-start | bytes 1327108
  11.1 65.1 %copy-start.4 = (bf16[128,256]{1,0:T(8,128)(2,1)S(1)}, bf16[128,256]{1,0:T(8,128)(2,1)}, u32[]{:S(2)}) copy-start(bf16[128,256]{1,0:T(8,128)(2,1)} %constant.18.tapy_ref) | copy-start | bytes 196612
  11.1 65.1 %copy-start.5 = (bf16[96,48]{1,0:T(8,128)(2,1)S(1)}, bf16[96,48]{1,0:T(8,128)(2,1)}, u32[]{:S(2)}) copy-start(bf16[96,48]{1,0:T(8,128)(2,1)} %constant.23.tapz_ref) | copy-start | bytes 27652
  42.5 1.0 copy-start.3
  66.7 9.4 %collective-permute-start = (f32[32,40,128]{2,1,0:T(8,128)S(1)}, f32[32,40,128]{2,1,0:T(8,128)S(1)}, u32[]{:S(2)}, u32[]{:S(2)}) collective-permute-start(f32[32,40,128]{2,1,0:T(8,128)S(1)} %all_to_all.31.own_ref), channel_id=1, source_target_pairs={{0,8},{8,0},{16,24},{24,16},{32,40},{40,32},{48,56},{56,48},{64,72... | collective-permute-start | bytes 1966088 | tf_op jit(solution)/shard_map/ppermute | solution.py:520
  72.3 3.8 %collective-permute-start.1 = (f32[32,32,128]{2,1,0:T(8,128)S(1)}, f32[32,32,128]{2,1,0:T(8,128)S(1)}, u32[]{:S(2)}, u32[]{:S(2)}) collective-permute-start(f32[32,32,128]{2,1,0:T(8,128)S(1)} %all_to_all.30.got_ref.ownp_ref), channel_id=1, source_target_pairs={{0,8},{8,0},{16,24},{24,16},{32,40},{40,32},{48,56},{56,48},{64,72... | collective-permute-start | bytes 1572872 | tf_op jit(solution)/shard_map/ppermute | solution.py:520
  129.9 5.3 %collective-permute-start.2 = (f32[16,24,128]{2,1,0:T(8,128)S(1)}, f32[16,24,128]{2,1,0:T(8,128)S(1)}, u32[]{:S(2)}, u32[]{:S(2)}) collective-permute-start(f32[16,24,128]{2,1,0:T(8,128)S(1)} %get-tuple-element.8), channel_id=1, source_target_pairs={{0,8},{8,0},{16,24},{24,16},{32,40},{40,32},{48,56},{56,48},{64,72... | collective-permute-start | bytes 589832 | tf_op jit(solution)/shard_map/ppermute | solution.py:520
  176.4 6.3 %collective-permute-start.3 = (f32[16,24,128]{2,1,0:T(8,128)S(1)}, f32[16,24,128]{2,1,0:T(8,128)S(1)}, u32[]{:S(2)}, u32[]{:S(2)}) collective-permute-start(f32[16,24,128]{2,1,0:T(8,128)S(1)} %all_to_all.35.own_ref), channel_id=1, source_target_pairs={{0,8},{8,0},{16,24},{24,16},{32,40},{40,32},{48,56},{56,48},{64,72... | collective-permute-start | bytes 589832 | tf_op jit(solution)/shard_map/ppermute | solution.py:520
  249.5 1.9 copy-start
Sparse Core Ops, SparseCore 0:
  130.1 47.9 all-gather.1

commit v6 on v5

--- a/solution.py
+++ b/solution.py
@@ -286,16 +286,16 @@
 
 def near_groups():
     return [
-        [(16 * z + 2 * x + c) * 8 + 2 * t + u for x in range(8) for u in range(2)]
-        for z in range(4)
+        [(16 * (2 * h + u) + 2 * x + c) * 8 + y for x in range(8) for u in range(2)]
+        for h in range(2)
         for c in range(2)
-        for t in range(4)
+        for y in range(8)
     ]
 
 
 def far_groups():
     return [
-        [(16 * z + 2 * x + c) * 8 + 2 * t + u for z in range(4) for t in range(4)]
+        [(16 * (2 * h + u) + 2 * x + c) * 8 + y for h in range(2) for y in range(8)]
         for x in range(8)
         for c in range(2)
         for u in range(2)
@@ -313,7 +313,7 @@
         in_specs=[smem()] * 3 + [vmem()] * 2,
         out_specs=vmem(),
         scratch_shapes=[pltpu.VMEM((64, 48, 128), F32)],
-        compiler_params=params(8),
+        compiler_params=params(56),
         name="pack",
     )(*at, proj, pot)
 
@@ -472,14 +472,13 @@
     rows_ref[...] = mine
 
 
-def rotate_kernel(rows_ref, all_ref, out_ref):
-    rows = parts_of(rows_ref[...])
-    for part in range(8):
-        j, kh = part // 2, part % 2
-        f = jnp.concatenate([all_ref[3 * part + t] for t in range(3)], axis=1)
-        turned = dot_parts(rows, parts_of(f))
-        for t in range(3):
-            out_ref[pl.ds((3 * kh + t) * 4 + j, 32, stride=24), :] = turned[:, 128 * t : 128 * t + 128]
+def rotate_kernel(rows_ref, every_ref, out_ref):
+    part = pl.program_id(0)
+    first = 12 * (part & 1) + (part >> 1)
+    f = jnp.concatenate([every_ref[t] for t in range(3)], axis=1)
+    turned = dot_parts(parts_of(rows_ref[...]), parts_of(f))
+    for t in range(3):
+        out_ref[pl.ds(first + 4 * t, 32, stride=24), :] = turned[:, 128 * t : 128 * t + 128]
 
 
 def gram(both):
@@ -509,9 +508,13 @@
     return pl.pallas_call(
         rotate_kernel,
         out_shape=jax.ShapeDtypeStruct((768, 128), F32),
-        in_specs=[vmem()] * 2,
-        out_specs=vmem(),
-        compiler_params=params(12),
+        grid=(8,),
+        in_specs=[
+            pl.BlockSpec((32, 256), lambda part: (0, 0)),
+            pl.BlockSpec((3, 256, 128), lambda part: (part, 0, 0)),
+        ],
+        out_specs=pl.BlockSpec((768, 128), lambda part: (0, 0)),
+        compiler_params=params(56),
         name="rotate",
     )(rows, every)
 
@@ -533,6 +536,7 @@
     first = lax.all_to_all(first, "dom", 0, 0, tiled=True, axis_index_groups=same_core())
     first_oth = swap_cores(first)
     second = boxes(at, first, orbitals.reshape(32, 24, 128))
+    second, first_oth = lax.optimization_barrier((second, first_oth))
     second = lax.all_to_all(second, "dom", 0, 0, tiled=True, axis_index_groups=same_core())
     second_oth = swap_cores(second)
     both = chebyshev(at, proj_strength, second, second_oth, first, first_oth)

time: 260 us -> 267 us (1.027)
  Pallas kernels: 87.1 us -> 92.8 us
  local copies, waits for them, and re-layouts: 6.74 us -> 2.32 us
  blocking collectives: 131 us -> 134 us
    unnamed x28 -> x20, local copies, waits for them, and re-layouts: 6.71 us -> 2.29 us
    pallas_call x1, Pallas kernels: 1.56 us -> 5.92 us  [rotate(): pl.pallas_call(rotate_kernel, out_shape=jax.ShapeDtypeStruct((768, 128),...]
  transfers between devices with their start and end apart: 5 -> 5, of which waited for: 3 -> 3; matrix products, arithmetic and copies ran while one was open for 0% -> 0% of each run, Pallas kernels for 26% -> 25%
where the time goes in v6:
time: 267 us; the launch traced here: 266 us
  blocking collectives  134 us (50%)
  Pallas kernels  92.8 us (35%)
  starting transfers between devices  19.3 us (7%)
  between operations  14.2 us (5%)
  waiting for transfers between devices  3.82 us (1%)
    all_to_all x4, blocking collectives, exchange(): lax.all_to_all(values, ('dom', 'band'), 0, 0, tiled=True, axis_index_grou...  80.5 us
    pallas_call x1, Pallas kernels, ortho(): pl.pallas_call(ortho_kernel, out_shape=[jax.ShapeDtypeStruct((32, 256), F...  66.8 us
    all_to_all x1, blocking collectives, on_device(): lax.all_to_all(first, 'dom', 0, 0, tiled=True, axis_index_groups=same_cor...  30 us
    all_to_all x1, blocking collectives, on_device(): lax.all_to_all(second, 'dom', 0, 0, tiled=True, axis_index_groups=same_co...  23.4 us
    ppermute x4, starting transfers between devices, swap_cores(): return lax.ppermute(values, 'dom', [(i, i ^ 1) for i in range(64)])  19.2 us
    pallas_call x1, Pallas kernels, chebyshev(): pl.pallas_call(filter_kernel, out_shape=jax.ShapeDtypeStruct((1536, 128),...  15.2 us
    pallas_call x1, Pallas kernels, rotate(): pl.pallas_call(rotate_kernel, out_shape=jax.ShapeDtypeStruct((768, 128),...  5.92 us
  transfers between devices with their start and end apart: 5, of which 3 were waited for; matrix products, arithmetic and copies ran while one was open for 0% of the time, Pallas kernels for 25%

profile of v6, /device:TPU:1, one launch (start us, length us, event | category | flops | bytes accessed | tf_op | source)
XLA Modules:
  0.0 266.3 jit_solution(15239520232737938828)
XLA Ops:
  7.2 0.0 all-gather.2.cloned.1.call-start
  7.3 3.1 %pack.1 = f32[32,32,128]{2,1,0:T(8,128)} custom-call(s32[64]{0:T(128)} %z_ref.5, s32[64]{0:T(128)} %x_ref.3, s32[64]{0:T(128)} %y_ref.3, f32[64,24,128]{2,1,0:T(8,128)} %bitcast.9, f32[24,128]{1,0:T(8,128)} %bitcast.11), custom_call_target="tpu_custom_call" | custom-call | tf_op jit(solution)/shard_map/pack/pallas_call | solution.py:310
  10.4 30.0 %all_to_all.30.got_ref.ownp_ref = f32[32,32,128]{2,1,0:T(8,128)S(1)} all-to-all(f32[32,32,128]{2,1,0:T(8,128)} %pack.1), channel_id=1, replica_groups={{0,16,32,48,64,80,96,112,128,144,160,176,192,208,224,240,256,272,288,30..., dimensions={0} | all-to-all | bytes 1048576 | tf_op jit(solution)/shard_map/all_to_all | solution.py:536
  40.4 4.3 %collective-permute-start = (f32[32,32,128]{2,1,0:T(8,128)S(1)}, f32[32,32,128]{2,1,0:T(8,128)S(1)}, u32[]{:S(2)}, u32[]{:S(2)}) collective-permute-start(f32[32,32,128]{2,1,0:T(8,128)S(1)} %all_to_all.30.got_ref.ownp_ref), channel_id=1, source_target_pairs={{0,8},{8,0},{16,24},{24,16},{32,40},{40,32},{48,56},{56,48},{64,72... | collective-permute-start | bytes 1572872 | tf_op jit(solution)/shard_map/ppermute | solution.py:523
  44.7 1.0 copy-done.1
  45.7 0.7 copy-done.5
  46.4 0.6 boxes.1
  47.0 23.4 %all_to_all.31.own_ref = f32[32,40,128]{2,1,0:T(8,128)S(1)} all-to-all(f32[32,40,128]{2,1,0:T(8,128)S(1)} %boxes.1), channel_id=1, replica_groups={{0,16,32,48,64,80,96,112,128,144,160,176,192,208,224,240,256,272,288,30..., dimensions={0} | all-to-all | bytes 1310720 | tf_op jit(solution)/shard_map/all_to_all | solution.py:540
  70.4 4.0 %collective-permute-start.1 = (f32[32,40,128]{2,1,0:T(8,128)S(1)}, f32[32,40,128]{2,1,0:T(8,128)S(1)}, u32[]{:S(2)}, u32[]{:S(2)}) collective-permute-start(f32[32,40,128]{2,1,0:T(8,128)S(1)} %all_to_all.31.own_ref), channel_id=1, source_target_pairs={{0,8},{8,0},{16,24},{24,16},{32,40},{40,32},{48,56},{56,48},{64,72... | collective-permute-start | bytes 1966088 | tf_op jit(solution)/shard_map/ppermute | solution.py:523
  74.3 1.7 collective-permute-done.1.oth_ref
  76.1 15.2 %chebyshev.1 = f32[1536,128]{1,0:T(8,128)S(1)} custom-call(s32[64]{0:T(128)S(1)} %copy-done.6, s32[64]{0:T(128)S(1)} %copy-done.7, s32[64]{0:T(128)S(1)} %copy-done.8, f32[64]{0:T(128)S(1)} %copy-done.9, bf16[128,256]{1,0:T(8,128)(2,1)S(1)} %copy-done.2, bf16[96,48]{1,0:T(8,128)(2,1)S(1)} %copy-done.4, bf16[24,96,96]{2,1,0:T(8,128)(2,1)S(1)} %copy-done, ...), custom_call_target="tpu_custom_call" | custom-call | tf_op jit(solution)/shard_map/chebyshev/pallas_call | solution.py:336
  91.3 37.0 %all_to_all.32 = f32[256,3,2,128]{3,2,1,0:T(2,128)S(1)} all-to-all(f32[256,3,2,128]{3,2,1,0:T(2,128)S(1)} %bitcast.6), channel_id=1, replica_groups={{0,16,32,48,64,80,96,112,128,144,160,176,192,208,224,240,256,272,288,30..., dimensions={0} | all-to-all | bytes 1572864 | tf_op jit(solution)/shard_map/all_to_all | solution.py:306
  128.3 1.2 gram.1
  129.4 0.0 all-gather.2.cloned.1.call-update
  129.5 4.6 %collective-permute-start.2 = (f32[16,24,128]{2,1,0:T(8,128)S(1)}, f32[16,24,128]{2,1,0:T(8,128)S(1)}, u32[]{:S(2)}, u32[]{:S(2)}) collective-permute-start(f32[16,24,128]{2,1,0:T(8,128)S(1)} %get-tuple-element.12), channel_id=1, source_target_pairs={{0,8},{8,0},{16,24},{24,16},{32,40},{40,32},{48,56},{56,48},{64,72... | collective-permute-start | bytes 589832 | tf_op jit(solution)/shard_map/ppermute | solution.py:523
  134.1 1.0 collective-permute-done.2
  135.1 12.2 %all_to_all.33 = f32[16,24,128]{2,1,0:T(8,128)S(1)} all-to-all(f32[16,24,128]{2,1,0:T(8,128)S(1)} %add.3), channel_id=1, replica_groups={{0,128,16,144,32,160,48,176,64,192,80,208,96,224,112,240},{1,129,17,145..., dimensions={0} | all-to-all | bytes 393216 | tf_op jit(solution)/shard_map/all_to_all | solution.py:306
  147.4 18.1 %all_to_all.34 = f32[16,24,128]{2,1,0:T(8,128)S(1)} all-to-all(f32[16,24,128]{2,1,0:T(8,128)S(1)} %broadcast_in_dim.4), channel_id=1, replica_groups={{0,1,2,3,4,5,6,7,256,257,258,259,260,261,262,263},{128,129,130,131,132,..., dimensions={0} | all-to-all | bytes 393216 | tf_op jit(solution)/shard_map/all_to_all | solution.py:306
  165.6 13.2 %all_to_all.35.own_ref = f32[16,24,128]{2,1,0:T(8,128)S(1)} all-to-all(f32[16,24,128]{2,1,0:T(8,128)S(1)} %broadcast_in_dim.5), channel_id=1, replica_groups={{0,128,16,144,32,160,48,176,64,192,80,208,96,224,112,240},{1,129,17,145..., dimensions={0} | all-to-all | bytes 393216 | tf_op jit(solution)/shard_map/all_to_all | solution.py:306
  178.7 6.4 %collective-permute-start.3 = (f32[16,24,128]{2,1,0:T(8,128)S(1)}, f32[16,24,128]{2,1,0:T(8,128)S(1)}, u32[]{:S(2)}, u32[]{:S(2)}) collective-permute-start(f32[16,24,128]{2,1,0:T(8,128)S(1)} %all_to_all.35.own_ref), channel_id=1, source_target_pairs={{0,8},{8,0},{16,24},{24,16},{32,40},{40,32},{48,56},{56,48},{64,72... | collective-permute-start | bytes 589832 | tf_op jit(solution)/shard_map/ppermute | solution.py:523
  185.2 1.0 collective-permute-done.3.oth_ref
  186.2 66.8 %ortho.1 = (f32[32,256]{1,0:T(8,128)S(1)}, f32[32,256]{1,0:T(8,128)}) custom-call(f32[16,24,128]{2,1,0:T(8,128)S(1)} %all_to_all.35.own_ref, f32[16,24,128]{2,1,0:T(8,128)S(1)} %collective-permute-done.3.oth_ref), custom_call_target="tpu_custom_call" | custom-call | tf_op jit(solution)/shard_map/ortho/pallas_call | solution.py:496
  253.0 0.6 copy-done.3
  253.6 5.9 %rotate.1 = f32[768,128]{1,0:T(8,128)} custom-call(f32[32,256]{1,0:T(8,128)} %copy-done.3, f32[24,256,128]{2,1,0:T(8,128)} %all-gather.2.cloned.1.call-done.every_ref), custom_call_target="tpu_custom_call" | custom-call | tf_op jit(solution)/shard_map/rotate/pallas_call | solution.py:508
  (24 shorter events, 0.1 us)
Async XLA Ops:
  7.2 68.9 %copy-start = (bf16[24,96,96]{2,1,0:T(8,128)(2,1)S(1)}, bf16[24,96,96]{2,1,0:T(8,128)(2,1)}, u32[]{:S(2)}) copy-start(bf16[24,96,96]{2,1,0:T(8,128)(2,1)} %constant.10.clone.pick_ref) | copy-start | bytes 1327108
  7.2 68.9 %copy-start.2 = (bf16[128,256]{1,0:T(8,128)(2,1)S(1)}, bf16[128,256]{1,0:T(8,128)(2,1)}, u32[]{:S(2)}) copy-start(bf16[128,256]{1,0:T(8,128)(2,1)} %constant.18.tapy_ref) | copy-start | bytes 196612
  7.2 68.9 %copy-start.4 = (bf16[96,48]{1,0:T(8,128)(2,1)S(1)}, bf16[96,48]{1,0:T(8,128)(2,1)}, u32[]{:S(2)}) copy-start(bf16[96,48]{1,0:T(8,128)(2,1)} %constant.23.tapz_ref) | copy-start | bytes 27652
  7.2 68.8 %copy-start.6 = (s32[64]{0:T(128)S(1)}, s32[64]{0:T(128)}, u32[]{:S(2)}) copy-start(s32[64]{0:T(128)} %z_ref.5) | copy-start | bytes 772
  7.2 68.8 %copy-start.7 = (s32[64]{0:T(128)S(1)}, s32[64]{0:T(128)}, u32[]{:S(2)}) copy-start(s32[64]{0:T(128)} %x_ref.3) | copy-start | bytes 772
  7.2 68.8 %copy-start.8 = (s32[64]{0:T(128)S(1)}, s32[64]{0:T(128)}, u32[]{:S(2)}) copy-start(s32[64]{0:T(128)} %y_ref.3) | copy-start | bytes 772
  7.2 68.8 %copy-start.9 = (f32[64]{0:T(128)S(1)}, f32[64]{0:T(128)}, u32[]{:S(2)}) copy-start(f32[64]{0:T(128)} %strength_ref.1) | copy-start | bytes 772
  7.2 246.3 %all-gather.2.cloned.1.call-start = ((), (), s32[]{:S(2)}) async-start(), calls=%async_computation.6 | async-start | bytes 3538944 | tf_op jit(solution)/shard_map/all_gather | solution.py:547
  40.4 6.6 %collective-permute-start = (f32[32,32,128]{2,1,0:T(8,128)S(1)}, f32[32,32,128]{2,1,0:T(8,128)S(1)}, u32[]{:S(2)}, u32[]{:S(2)}) collective-permute-start(f32[32,32,128]{2,1,0:T(8,128)S(1)} %all_to_all.30.got_ref.ownp_ref), channel_id=1, source_target_pairs={{0,8},{8,0},{16,24},{24,16},{32,40},{40,32},{48,56},{56,48},{64,72... | collective-permute-start | bytes 1572872 | tf_op jit(solution)/shard_map/ppermute | solution.py:523
  44.7 1.0 copy-start.1
  45.7 0.7 copy-start.5
  70.4 5.7 %collective-permute-start.1 = (f32[32,40,128]{2,1,0:T(8,128)S(1)}, f32[32,40,128]{2,1,0:T(8,128)S(1)}, u32[]{:S(2)}, u32[]{:S(2)}) collective-permute-start(f32[32,40,128]{2,1,0:T(8,128)S(1)} %all_to_all.31.own_ref), channel_id=1, source_target_pairs={{0,8},{8,0},{16,24},{24,16},{32,40},{40,32},{48,56},{56,48},{64,72... | collective-permute-start | bytes 1966088 | tf_op jit(solution)/shard_map/ppermute | solution.py:523
  129.5 5.6 %collective-permute-start.2 = (f32[16,24,128]{2,1,0:T(8,128)S(1)}, f32[16,24,128]{2,1,0:T(8,128)S(1)}, u32[]{:S(2)}, u32[]{:S(2)}) collective-permute-start(f32[16,24,128]{2,1,0:T(8,128)S(1)} %get-tuple-element.12), channel_id=1, source_target_pairs={{0,8},{8,0},{16,24},{24,16},{32,40},{40,32},{48,56},{56,48},{64,72... | collective-permute-start | bytes 589832 | tf_op jit(solution)/shard_map/ppermute | solution.py:523
  178.7 7.5 %collective-permute-start.3 = (f32[16,24,128]{2,1,0:T(8,128)S(1)}, f32[16,24,128]{2,1,0:T(8,128)S(1)}, u32[]{:S(2)}, u32[]{:S(2)}) collective-permute-start(f32[16,24,128]{2,1,0:T(8,128)S(1)} %all_to_all.35.own_ref), channel_id=1, source_target_pairs={{0,8},{8,0},{16,24},{24,16},{32,40},{40,32},{48,56},{56,48},{64,72... | collective-permute-start | bytes 589832 | tf_op jit(solution)/shard_map/ppermute | solution.py:523
  253.0 0.6 copy-start.3
Sparse Core Ops, SparseCore 0:
  129.6 45.1 all-gather.1

commit v7 on v5

--- a/solution.py
+++ b/solution.py
@@ -313,7 +313,7 @@
         in_specs=[smem()] * 3 + [vmem()] * 2,
         out_specs=vmem(),
         scratch_shapes=[pltpu.VMEM((64, 48, 128), F32)],
-        compiler_params=params(8),
+        compiler_params=params(56),
         name="pack",
     )(*at, proj, pot)
 
@@ -325,7 +325,7 @@
         in_specs=[smem()] + [vmem()] * 2,
         out_specs=vmem(),
         scratch_shapes=[pltpu.VMEM((2, 40, 128), F32)],
-        compiler_params=params(6),
+        compiler_params=params(56),
         name="boxes",
     )(at[0], got, orb)
 
@@ -394,7 +394,9 @@
         ref[0, 16:17, :] = jnp.where(first, diag[:, 0:128], diag[:, 128:256])
 
 
-def ortho_kernel(own_ref, oth_ref, rows_ref, proj_ref, corr, ham, inv, work):
+def ortho_kernel(own_ref, oth_ref, every_ref, rot_ref, proj_ref, corr, ham, inv, work, every, arrived):
+    fetch = pltpu.make_async_copy(every_ref, every, arrived)
+    fetch.start()
     me, block = place()
     core = me & 1
     row = lax.broadcasted_iota(jnp.int32, (256, 256), 0)
@@ -469,17 +471,14 @@
     x = inv[...]
     mine = inv[pl.ds(pl.multiple_of(32 * block, 32), 32), :]
     proj_ref[...] = dot_t(dot(mine, ham[...]), x)
-    rows_ref[...] = mine
-
-
-def rotate_kernel(rows_ref, all_ref, out_ref):
-    rows = parts_of(rows_ref[...])
+    rows = parts_of(mine)
+    fetch.wait()
     for part in range(8):
         j, kh = part // 2, part % 2
-        f = jnp.concatenate([all_ref[3 * part + t] for t in range(3)], axis=1)
+        f = jnp.concatenate([every[3 * part + t] for t in range(3)], axis=1)
         turned = dot_parts(rows, parts_of(f))
         for t in range(3):
-            out_ref[pl.ds((3 * kh + t) * 4 + j, 32, stride=24), :] = turned[:, 128 * t : 128 * t + 128]
+            rot_ref[pl.ds((3 * kh + t) * 4 + j, 32, stride=24), :] = turned[:, 128 * t : 128 * t + 128]
 
 
 def gram(both):
@@ -493,27 +492,17 @@
     )(both)
 
 
-def ortho(own, oth):
+def ortho(own, oth, every):
     return pl.pallas_call(
         ortho_kernel,
-        out_shape=[jax.ShapeDtypeStruct((32, 256), F32)] * 2,
-        in_specs=[vmem()] * 2,
+        out_shape=[jax.ShapeDtypeStruct((768, 128), F32), jax.ShapeDtypeStruct((32, 256), F32)],
+        in_specs=[vmem(), vmem(), pl.BlockSpec(memory_space=pl.ANY)],
         out_specs=[vmem()] * 2,
-        scratch_shapes=[pltpu.VMEM((256, 256), F32)] * 4,
-        compiler_params=params(8),
+        scratch_shapes=[pltpu.VMEM((256, 256), F32)] * 4
+        + [pltpu.VMEM((24, 256, 128), F32), pltpu.SemaphoreType.DMA(())],
+        compiler_params=params(56),
         name="ortho",
-    )(own, oth)
-
-
-def rotate(rows, every):
-    return pl.pallas_call(
-        rotate_kernel,
-        out_shape=jax.ShapeDtypeStruct((768, 128), F32),
-        in_specs=[vmem()] * 2,
-        out_specs=vmem(),
-        compiler_params=params(12),
-        name="rotate",
-    )(rows, every)
+    )(own, oth, every)
 
 
 def swap_cores(values):
@@ -542,8 +531,7 @@
     mine, other, filtered = gram(both)
     every = lax.all_gather(filtered, "band", axis=0, tiled=True)
     mine = sum_everywhere(mine + swap_cores(other))
-    rows, projected = ortho(mine, swap_cores(mine))
-    rotated = rotate(rows, every)
+    rotated, projected = ortho(mine, swap_cores(mine), every)
     return (rotated.reshape(32, 1, 6, 512), projected)
 
 

time: 260 us -> 259 us (level)
  local copies, waits for them, and re-layouts: 6.74 us -> 0.74 us
  Pallas kernels: 87.1 us -> 90.7 us
    unnamed x28 -> x20, local copies, waits for them, and re-layouts: 6.71 us -> 0.71 us
    pallas_call x2 -> x1, Pallas kernels: 68.3 us -> 68.9 us  [ortho(): pl.pallas_call(ortho_kernel, out_shape=[jax.ShapeDtypeStruct((768, 128),...]
  transfers between devices with their start and end apart: 5 -> 5, of which waited for: 3 -> 3; matrix products, arithmetic and copies ran while one was open for 0% -> 0% of each run, Pallas kernels for 26% -> 0%
where the time goes in v7:
time: 259 us; the launch traced here: 258 us
  blocking collectives  131 us (51%)
  Pallas kernels  90.7 us (35%)
  starting transfers between devices  17.1 us (7%)
  between operations  14.2 us (5%)
  waiting for transfers between devices  4.2 us (2%)
    all_to_all x4, blocking collectives, exchange(): lax.all_to_all(values, ('dom', 'band'), 0, 0, tiled=True, axis_index_grou...  78.3 us
    pallas_call x1, Pallas kernels, ortho(): pl.pallas_call(ortho_kernel, out_shape=[jax.ShapeDtypeStruct((768, 128),...  68.9 us
    all_to_all x1, blocking collectives, on_device(): lax.all_to_all(first, 'dom', 0, 0, tiled=True, axis_index_groups=same_cor...  30.1 us
    all_to_all x1, blocking collectives, on_device(): lax.all_to_all(second, 'dom', 0, 0, tiled=True, axis_index_groups=same_co...  22.8 us
    ppermute x4, starting transfers between devices, swap_cores(): return lax.ppermute(values, 'dom', [(i, i ^ 1) for i in range(64)])  17 us
    pallas_call x1, Pallas kernels, chebyshev(): pl.pallas_call(filter_kernel, out_shape=jax.ShapeDtypeStruct((1536, 128),...  15.3 us
  transfers between devices with their start and end apart: 5, of which 3 were waited for; matrix products, arithmetic and copies ran while one was open for 0% of the time, Pallas kernels for 0%

profile of v7, /device:TPU:1, one launch (start us, length us, event | category | flops | bytes accessed | tf_op | source)
XLA Modules:
  0.0 258.2 jit_solution(11079530292118168607)
XLA Ops:
  7.2 0.0 copy-start.3
  7.2 0.0 copy-start.2
  7.2 0.0 copy-start.1
  7.2 0.0 all-gather.2.cloned.1.call-start
  7.3 3.1 %pack.1 = f32[32,32,128]{2,1,0:T(8,128)} custom-call(s32[64]{0:T(128)} %z_ref.5, s32[64]{0:T(128)} %x_ref.3, s32[64]{0:T(128)} %y_ref.3, f32[64,24,128]{2,1,0:T(8,128)} %bitcast.8, f32[24,128]{1,0:T(8,128)} %bitcast.10), custom_call_target="tpu_custom_call" | custom-call | tf_op jit(solution)/shard_map/pack/pallas_call | solution.py:310
  10.4 30.1 %all_to_all.30.got_ref.ownp_ref = f32[32,32,128]{2,1,0:T(8,128)} all-to-all(f32[32,32,128]{2,1,0:T(8,128)} %pack.1), channel_id=1, replica_groups={{0,16,32,48,64,80,96,112,128,144,160,176,192,208,224,240,256,272,288,30..., dimensions={0} | all-to-all | bytes 1048576 | tf_op jit(solution)/shard_map/all_to_all | solution.py:522
  40.5 2.1 boxes.1
  42.7 22.8 %all_to_all.31.own_ref = f32[32,40,128]{2,1,0:T(8,128)S(1)} all-to-all(f32[32,40,128]{2,1,0:T(8,128)} %boxes.1), channel_id=1, replica_groups={{0,16,32,48,64,80,96,112,128,144,160,176,192,208,224,240,256,272,288,30..., dimensions={0} | all-to-all | bytes 1310720 | tf_op jit(solution)/shard_map/all_to_all | solution.py:525
  65.5 5.6 %collective-permute-start = (f32[32,40,128]{2,1,0:T(8,128)S(1)}, f32[32,40,128]{2,1,0:T(8,128)S(1)}, u32[]{:S(2)}, u32[]{:S(2)}) collective-permute-start(f32[32,40,128]{2,1,0:T(8,128)S(1)} %all_to_all.31.own_ref), channel_id=1, source_target_pairs={{0,8},{8,0},{16,24},{24,16},{32,40},{40,32},{48,56},{56,48},{64,72... | collective-permute-start | bytes 1966088 | tf_op jit(solution)/shard_map/ppermute | solution.py:509
  71.1 1.9 collective-permute-start.1
  73.0 2.1 collective-permute-done.1.othp_ref
  75.1 15.3 %chebyshev.1 = f32[1536,128]{1,0:T(8,128)S(1)} custom-call(s32[64]{0:T(128)S(1)} %copy-done.4, s32[64]{0:T(128)S(1)} %copy-done.5, s32[64]{0:T(128)S(1)} %copy-done.6, f32[64]{0:T(128)S(1)} %copy-done.7, bf16[128,256]{1,0:T(8,128)(2,1)S(1)} %copy-done.2, bf16[96,48]{1,0:T(8,128)(2,1)S(1)} %copy-done.3, bf16[24,96,96]{2,1,0:T(8,128)(2,1)S(1)} %copy-done.1, ...), custom_call_target="tpu_custom_call" | custom-call | tf_op jit(solution)/shard_map/chebyshev/pallas_call | solution.py:336
  90.5 37.3 %all_to_all.32 = f32[256,3,2,128]{3,2,1,0:T(2,128)S(1)} all-to-all(f32[256,3,2,128]{3,2,1,0:T(2,128)S(1)} %bitcast.6), channel_id=1, replica_groups={{0,16,32,48,64,80,96,112,128,144,160,176,192,208,224,240,256,272,288,30..., dimensions={0} | all-to-all | bytes 1572864 | tf_op jit(solution)/shard_map/all_to_all | solution.py:306
  127.7 1.2 gram.1
  128.9 0.0 all-gather.2.cloned.1.call-update
  128.9 4.2 %collective-permute-start.2 = (f32[16,24,128]{2,1,0:T(8,128)S(1)}, f32[16,24,128]{2,1,0:T(8,128)S(1)}, u32[]{:S(2)}, u32[]{:S(2)}) collective-permute-start(f32[16,24,128]{2,1,0:T(8,128)S(1)} %get-tuple-element.8), channel_id=1, source_target_pairs={{0,8},{8,0},{16,24},{24,16},{32,40},{40,32},{48,56},{56,48},{64,72... | collective-permute-start | bytes 589832 | tf_op jit(solution)/shard_map/ppermute | solution.py:509
  133.2 1.0 collective-permute-done.2
  134.2 12.5 %all_to_all.33 = f32[16,24,128]{2,1,0:T(8,128)S(1)} all-to-all(f32[16,24,128]{2,1,0:T(8,128)S(1)} %add.3), channel_id=1, replica_groups={{0,1,16,17,32,33,48,49,64,65,80,81,96,97,112,113},{2,3,18,19,34,35,50,5..., dimensions={0} | all-to-all | bytes 393216 | tf_op jit(solution)/shard_map/all_to_all | solution.py:306
  146.8 17.8 %all_to_all.34 = f32[16,24,128]{2,1,0:T(8,128)S(1)} all-to-all(f32[16,24,128]{2,1,0:T(8,128)S(1)} %broadcast_in_dim.4), channel_id=1, replica_groups={{0,2,4,6,128,130,132,134,256,258,260,262,384,386,388,390},{1,3,5,7,129,..., dimensions={0} | all-to-all | bytes 393216 | tf_op jit(solution)/shard_map/all_to_all | solution.py:306
  164.6 10.8 %all_to_all.35.own_ref = f32[16,24,128]{2,1,0:T(8,128)S(1)} all-to-all(f32[16,24,128]{2,1,0:T(8,128)S(1)} %broadcast_in_dim.5), channel_id=1, replica_groups={{0,1,16,17,32,33,48,49,64,65,80,81,96,97,112,113},{2,3,18,19,34,35,50,5..., dimensions={0} | all-to-all | bytes 393216 | tf_op jit(solution)/shard_map/all_to_all | solution.py:306
  175.4 5.3 %collective-permute-start.3 = (f32[16,24,128]{2,1,0:T(8,128)S(1)}, f32[16,24,128]{2,1,0:T(8,128)S(1)}, u32[]{:S(2)}, u32[]{:S(2)}) collective-permute-start(f32[16,24,128]{2,1,0:T(8,128)S(1)} %all_to_all.35.own_ref), channel_id=1, source_target_pairs={{0,8},{8,0},{16,24},{24,16},{32,40},{40,32},{48,56},{56,48},{64,72... | collective-permute-start | bytes 589832 | tf_op jit(solution)/shard_map/ppermute | solution.py:509
  180.7 1.0 collective-permute-done.3.oth_ref
  181.7 0.7 copy-done.9
  182.4 68.9 %ortho.1 = (f32[768,128]{1,0:T(8,128)}, f32[32,256]{1,0:T(8,128)}) custom-call(f32[16,24,128]{2,1,0:T(8,128)} %copy-done.8, f32[16,24,128]{2,1,0:T(8,128)} %copy-done.9, f32[24,256,128]{2,1,0:T(8,128)} %all-gather.2.cloned.1.call-done.every_ref), custom_call_target="tpu_custom_call" | custom-call | tf_op jit(solution)/shard_map/ortho/pallas_call | solution.py:496
  (23 shorter events, 0.1 us)
Async XLA Ops:
  7.2 67.9 %copy-start.3 = (bf16[96,48]{1,0:T(8,128)(2,1)S(1)}, bf16[96,48]{1,0:T(8,128)(2,1)}, u32[]{:S(2)}) copy-start(bf16[96,48]{1,0:T(8,128)(2,1)} %constant.23.tapz_ref) | copy-start | bytes 27652
  7.2 67.9 %copy-start.2 = (bf16[128,256]{1,0:T(8,128)(2,1)S(1)}, bf16[128,256]{1,0:T(8,128)(2,1)}, u32[]{:S(2)}) copy-start(bf16[128,256]{1,0:T(8,128)(2,1)} %constant.18.tapy_ref) | copy-start | bytes 196612
  7.2 67.9 %copy-start.1 = (bf16[24,96,96]{2,1,0:T(8,128)(2,1)S(1)}, bf16[24,96,96]{2,1,0:T(8,128)(2,1)}, u32[]{:S(2)}) copy-start(bf16[24,96,96]{2,1,0:T(8,128)(2,1)} %constant.10.clone.pick_ref) | copy-start | bytes 1327108
  7.2 67.9 %copy-start.4 = (s32[64]{0:T(128)S(1)}, s32[64]{0:T(128)}, u32[]{:S(2)}) copy-start(s32[64]{0:T(128)} %z_ref.5) | copy-start | bytes 772
  7.2 67.9 %copy-start.6 = (s32[64]{0:T(128)S(1)}, s32[64]{0:T(128)}, u32[]{:S(2)}) copy-start(s32[64]{0:T(128)} %y_ref.3) | copy-start | bytes 772
  7.2 67.9 %copy-start.5 = (s32[64]{0:T(128)S(1)}, s32[64]{0:T(128)}, u32[]{:S(2)}) copy-start(s32[64]{0:T(128)} %x_ref.3) | copy-start | bytes 772
  7.2 67.9 %copy-start.7 = (f32[64]{0:T(128)S(1)}, f32[64]{0:T(128)}, u32[]{:S(2)}) copy-start(f32[64]{0:T(128)} %strength_ref.1) | copy-start | bytes 772
  7.2 174.5 %all-gather.2.cloned.1.call-start = ((), (), s32[]{:S(2)}) async-start(), calls=%async_computation.6 | async-start | bytes 3538944 | tf_op jit(solution)/shard_map/all_gather | solution.py:532
  40.5 34.6 %copy-start = (f32[32,32,128]{2,1,0:T(8,128)S(1)}, f32[32,32,128]{2,1,0:T(8,128)}, u32[]{:S(2)}) copy-start(f32[32,32,128]{2,1,0:T(8,128)} %all_to_all.30.got_ref.ownp_ref) | copy-start | bytes 1572868
  65.5 9.6 %collective-permute-start = (f32[32,40,128]{2,1,0:T(8,128)S(1)}, f32[32,40,128]{2,1,0:T(8,128)S(1)}, u32[]{:S(2)}, u32[]{:S(2)}) collective-permute-start(f32[32,40,128]{2,1,0:T(8,128)S(1)} %all_to_all.31.own_ref), channel_id=1, source_target_pairs={{0,8},{8,0},{16,24},{24,16},{32,40},{40,32},{48,56},{56,48},{64,72... | collective-permute-start | bytes 1966088 | tf_op jit(solution)/shard_map/ppermute | solution.py:509
  71.1 4.0 %collective-permute-start.1 = (f32[32,32,128]{2,1,0:T(8,128)}, f32[32,32,128]{2,1,0:T(8,128)S(1)}, u32[]{:S(2)}, u32[]{:S(2)}) collective-permute-start(f32[32,32,128]{2,1,0:T(8,128)} %all_to_all.30.got_ref.ownp_ref), channel_id=1, source_target_pairs={{0,8},{8,0},{16,24},{24,16},{32,40},{40,32},{48,56},{56,48},{64,72... | collective-permute-start | bytes 1572872 | tf_op jit(solution)/shard_map/ppermute | solution.py:509
  128.9 5.3 %collective-permute-start.2 = (f32[16,24,128]{2,1,0:T(8,128)S(1)}, f32[16,24,128]{2,1,0:T(8,128)S(1)}, u32[]{:S(2)}, u32[]{:S(2)}) collective-permute-start(f32[16,24,128]{2,1,0:T(8,128)S(1)} %get-tuple-element.8), channel_id=1, source_target_pairs={{0,8},{8,0},{16,24},{24,16},{32,40},{40,32},{48,56},{56,48},{64,72... | collective-permute-start | bytes 589832 | tf_op jit(solution)/shard_map/ppermute | solution.py:509
  175.4 6.4 %copy-start.8 = (f32[16,24,128]{2,1,0:T(8,128)}, f32[16,24,128]{2,1,0:T(8,128)S(1)}, u32[]{:S(2)}) copy-start(f32[16,24,128]{2,1,0:T(8,128)S(1)} %all_to_all.35.own_ref) | copy-start | bytes 589828
  175.4 6.3 %collective-permute-start.3 = (f32[16,24,128]{2,1,0:T(8,128)S(1)}, f32[16,24,128]{2,1,0:T(8,128)S(1)}, u32[]{:S(2)}, u32[]{:S(2)}) collective-permute-start(f32[16,24,128]{2,1,0:T(8,128)S(1)} %all_to_all.35.own_ref), channel_id=1, source_target_pairs={{0,8},{8,0},{16,24},{24,16},{32,40},{40,32},{48,56},{56,48},{64,72... | collective-permute-start | bytes 589832 | tf_op jit(solution)/shard_map/ppermute | solution.py:509
  181.7 0.7 copy-start.9
Sparse Core Ops, SparseCore 0:
  129.0 47.9 all-gather.1

commit v8 on v7

--- a/solution.py
+++ b/solution.py
@@ -216,7 +216,7 @@
                 here = after
             return carry
 
-        lax.fori_loop(0, 6, along_x, 0, unroll=2)
+        lax.fori_loop(0, 6, along_x, 0, unroll=3)
 
         def outer(a, carry):
             xs = jnp.minimum(x_ref[a] >> 1, 26)

time: 259 us -> 259 us (level)
  no operation moved by 1% of the time
where the time goes in v8:
time: 259 us; the launch traced here: 258 us
  blocking collectives  131 us (51%)
  Pallas kernels  90.6 us (35%)
  starting transfers between devices  17.1 us (7%)
  between operations  14.2 us (5%)
  waiting for transfers between devices  4.2 us (2%)
    all_to_all x4, blocking collectives, exchange(): lax.all_to_all(values, ('dom', 'band'), 0, 0, tiled=True, axis_index_grou...  78.3 us
    pallas_call x1, Pallas kernels, ortho(): pl.pallas_call(ortho_kernel, out_shape=[jax.ShapeDtypeStruct((768, 128),...  68.9 us
    all_to_all x1, blocking collectives, on_device(): lax.all_to_all(first, 'dom', 0, 0, tiled=True, axis_index_groups=same_cor...  30.1 us
    all_to_all x1, blocking collectives, on_device(): lax.all_to_all(second, 'dom', 0, 0, tiled=True, axis_index_groups=same_co...  22.8 us
    ppermute x4, starting transfers between devices, swap_cores(): return lax.ppermute(values, 'dom', [(i, i ^ 1) for i in range(64)])  17 us
    pallas_call x1, Pallas kernels, chebyshev(): pl.pallas_call(filter_kernel, out_shape=jax.ShapeDtypeStruct((1536, 128),...  15.3 us
  transfers between devices with their start and end apart: 5, of which 3 were waited for; matrix products, arithmetic and copies ran while one was open for 0% of the time, Pallas kernels for 0%

profile of v8, /device:TPU:1, one launch (start us, length us, event | category | flops | bytes accessed | tf_op | source)
XLA Modules:
  0.0 258.1 jit_solution(8671841854904559880)
XLA Ops:
  7.2 0.0 copy-start.3
  7.2 0.0 copy-start.2
  7.2 0.0 copy-start.1
  7.2 0.0 all-gather.2.cloned.1.call-start
  7.3 3.1 %pack.1 = f32[32,32,128]{2,1,0:T(8,128)} custom-call(s32[64]{0:T(128)} %z_ref.5, s32[64]{0:T(128)} %x_ref.3, s32[64]{0:T(128)} %y_ref.3, f32[64,24,128]{2,1,0:T(8,128)} %bitcast.8, f32[24,128]{1,0:T(8,128)} %bitcast.10), custom_call_target="tpu_custom_call" | custom-call | tf_op jit(solution)/shard_map/pack/pallas_call | solution.py:310
  10.4 30.1 %all_to_all.30.got_ref.ownp_ref = f32[32,32,128]{2,1,0:T(8,128)} all-to-all(f32[32,32,128]{2,1,0:T(8,128)} %pack.1), channel_id=1, replica_groups={{0,16,32,48,64,80,96,112,128,144,160,176,192,208,224,240,256,272,288,30..., dimensions={0} | all-to-all | bytes 1048576 | tf_op jit(solution)/shard_map/all_to_all | solution.py:522
  40.5 2.1 boxes.1
  42.7 22.8 %all_to_all.31.own_ref = f32[32,40,128]{2,1,0:T(8,128)S(1)} all-to-all(f32[32,40,128]{2,1,0:T(8,128)} %boxes.1), channel_id=1, replica_groups={{0,16,32,48,64,80,96,112,128,144,160,176,192,208,224,240,256,272,288,30..., dimensions={0} | all-to-all | bytes 1310720 | tf_op jit(solution)/shard_map/all_to_all | solution.py:525
  65.5 5.6 %collective-permute-start = (f32[32,40,128]{2,1,0:T(8,128)S(1)}, f32[32,40,128]{2,1,0:T(8,128)S(1)}, u32[]{:S(2)}, u32[]{:S(2)}) collective-permute-start(f32[32,40,128]{2,1,0:T(8,128)S(1)} %all_to_all.31.own_ref), channel_id=1, source_target_pairs={{0,8},{8,0},{16,24},{24,16},{32,40},{40,32},{48,56},{56,48},{64,72... | collective-permute-start | bytes 1966088 | tf_op jit(solution)/shard_map/ppermute | solution.py:509
  71.1 1.9 collective-permute-start.1
  73.0 2.1 collective-permute-done.1.othp_ref
  75.1 15.3 %chebyshev.1 = f32[1536,128]{1,0:T(8,128)S(1)} custom-call(s32[64]{0:T(128)S(1)} %copy-done.4, s32[64]{0:T(128)S(1)} %copy-done.5, s32[64]{0:T(128)S(1)} %copy-done.6, f32[64]{0:T(128)S(1)} %copy-done.7, bf16[128,256]{1,0:T(8,128)(2,1)S(1)} %copy-done.2, bf16[96,48]{1,0:T(8,128)(2,1)S(1)} %copy-done.3, bf16[24,96,96]{2,1,0:T(8,128)(2,1)S(1)} %copy-done.1, ...), custom_call_target="tpu_custom_call" | custom-call | tf_op jit(solution)/shard_map/chebyshev/pallas_call | solution.py:336
  90.4 37.3 %all_to_all.32 = f32[256,3,2,128]{3,2,1,0:T(2,128)S(1)} all-to-all(f32[256,3,2,128]{3,2,1,0:T(2,128)S(1)} %bitcast.6), channel_id=1, replica_groups={{0,16,32,48,64,80,96,112,128,144,160,176,192,208,224,240,256,272,288,30..., dimensions={0} | all-to-all | bytes 1572864 | tf_op jit(solution)/shard_map/all_to_all | solution.py:306
  127.7 1.2 gram.1
  128.9 0.0 all-gather.2.cloned.1.call-update
  128.9 4.2 %collective-permute-start.2 = (f32[16,24,128]{2,1,0:T(8,128)S(1)}, f32[16,24,128]{2,1,0:T(8,128)S(1)}, u32[]{:S(2)}, u32[]{:S(2)}) collective-permute-start(f32[16,24,128]{2,1,0:T(8,128)S(1)} %get-tuple-element.8), channel_id=1, source_target_pairs={{0,8},{8,0},{16,24},{24,16},{32,40},{40,32},{48,56},{56,48},{64,72... | collective-permute-start | bytes 589832 | tf_op jit(solution)/shard_map/ppermute | solution.py:509
  133.1 1.0 collective-permute-done.2
  134.2 12.5 %all_to_all.33 = f32[16,24,128]{2,1,0:T(8,128)S(1)} all-to-all(f32[16,24,128]{2,1,0:T(8,128)S(1)} %add.3), channel_id=1, replica_groups={{0,1,16,17,32,33,48,49,64,65,80,81,96,97,112,113},{2,3,18,19,34,35,50,5..., dimensions={0} | all-to-all | bytes 393216 | tf_op jit(solution)/shard_map/all_to_all | solution.py:306
  146.7 17.8 %all_to_all.34 = f32[16,24,128]{2,1,0:T(8,128)S(1)} all-to-all(f32[16,24,128]{2,1,0:T(8,128)S(1)} %broadcast_in_dim.4), channel_id=1, replica_groups={{0,2,4,6,128,130,132,134,256,258,260,262,384,386,388,390},{1,3,5,7,129,..., dimensions={0} | all-to-all | bytes 393216 | tf_op jit(solution)/shard_map/all_to_all | solution.py:306
  164.6 10.8 %all_to_all.35.own_ref = f32[16,24,128]{2,1,0:T(8,128)S(1)} all-to-all(f32[16,24,128]{2,1,0:T(8,128)S(1)} %broadcast_in_dim.5), channel_id=1, replica_groups={{0,1,16,17,32,33,48,49,64,65,80,81,96,97,112,113},{2,3,18,19,34,35,50,5..., dimensions={0} | all-to-all | bytes 393216 | tf_op jit(solution)/shard_map/all_to_all | solution.py:306
  175.3 5.3 %collective-permute-start.3 = (f32[16,24,128]{2,1,0:T(8,128)S(1)}, f32[16,24,128]{2,1,0:T(8,128)S(1)}, u32[]{:S(2)}, u32[]{:S(2)}) collective-permute-start(f32[16,24,128]{2,1,0:T(8,128)S(1)} %all_to_all.35.own_ref), channel_id=1, source_target_pairs={{0,8},{8,0},{16,24},{24,16},{32,40},{40,32},{48,56},{56,48},{64,72... | collective-permute-start | bytes 589832 | tf_op jit(solution)/shard_map/ppermute | solution.py:509
  180.7 1.0 collective-permute-done.3.oth_ref
  181.7 0.7 copy-done.9
  182.4 68.9 %ortho.1 = (f32[768,128]{1,0:T(8,128)}, f32[32,256]{1,0:T(8,128)}) custom-call(f32[16,24,128]{2,1,0:T(8,128)} %copy-done.8, f32[16,24,128]{2,1,0:T(8,128)} %copy-done.9, f32[24,256,128]{2,1,0:T(8,128)} %all-gather.2.cloned.1.call-done.every_ref), custom_call_target="tpu_custom_call" | custom-call | tf_op jit(solution)/shard_map/ortho/pallas_call | solution.py:496
  (23 shorter events, 0.1 us)
Async XLA Ops:
  7.2 67.9 %copy-start.3 = (bf16[96,48]{1,0:T(8,128)(2,1)S(1)}, bf16[96,48]{1,0:T(8,128)(2,1)}, u32[]{:S(2)}) copy-start(bf16[96,48]{1,0:T(8,128)(2,1)} %constant.23.tapz_ref) | copy-start | bytes 27652
  7.2 67.9 %copy-start.2 = (bf16[128,256]{1,0:T(8,128)(2,1)S(1)}, bf16[128,256]{1,0:T(8,128)(2,1)}, u32[]{:S(2)}) copy-start(bf16[128,256]{1,0:T(8,128)(2,1)} %constant.18.tapy_ref) | copy-start | bytes 196612
  7.2 67.9 %copy-start.1 = (bf16[24,96,96]{2,1,0:T(8,128)(2,1)S(1)}, bf16[24,96,96]{2,1,0:T(8,128)(2,1)}, u32[]{:S(2)}) copy-start(bf16[24,96,96]{2,1,0:T(8,128)(2,1)} %constant.10.clone.pick_ref) | copy-start | bytes 1327108
  7.2 67.9 %copy-start.4 = (s32[64]{0:T(128)S(1)}, s32[64]{0:T(128)}, u32[]{:S(2)}) copy-start(s32[64]{0:T(128)} %z_ref.5) | copy-start | bytes 772
  7.2 67.9 %copy-start.6 = (s32[64]{0:T(128)S(1)}, s32[64]{0:T(128)}, u32[]{:S(2)}) copy-start(s32[64]{0:T(128)} %y_ref.3) | copy-start | bytes 772
  7.2 67.9 %copy-start.5 = (s32[64]{0:T(128)S(1)}, s32[64]{0:T(128)}, u32[]{:S(2)}) copy-start(s32[64]{0:T(128)} %x_ref.3) | copy-start | bytes 772
  7.2 67.9 %copy-start.7 = (f32[64]{0:T(128)S(1)}, f32[64]{0:T(128)}, u32[]{:S(2)}) copy-start(f32[64]{0:T(128)} %strength_ref.1) | copy-start | bytes 772
  7.2 174.5 %all-gather.2.cloned.1.call-start = ((), (), s32[]{:S(2)}) async-start(), calls=%async_computation.6 | async-start | bytes 3538944 | tf_op jit(solution)/shard_map/all_gather | solution.py:532
  40.5 34.6 %copy-start = (f32[32,32,128]{2,1,0:T(8,128)S(1)}, f32[32,32,128]{2,1,0:T(8,128)}, u32[]{:S(2)}) copy-start(f32[32,32,128]{2,1,0:T(8,128)} %all_to_all.30.got_ref.ownp_ref) | copy-start | bytes 1572868
  65.5 9.6 %collective-permute-start = (f32[32,40,128]{2,1,0:T(8,128)S(1)}, f32[32,40,128]{2,1,0:T(8,128)S(1)}, u32[]{:S(2)}, u32[]{:S(2)}) collective-permute-start(f32[32,40,128]{2,1,0:T(8,128)S(1)} %all_to_all.31.own_ref), channel_id=1, source_target_pairs={{0,8},{8,0},{16,24},{24,16},{32,40},{40,32},{48,56},{56,48},{64,72... | collective-permute-start | bytes 1966088 | tf_op jit(solution)/shard_map/ppermute | solution.py:509
  71.1 4.0 %collective-permute-start.1 = (f32[32,32,128]{2,1,0:T(8,128)}, f32[32,32,128]{2,1,0:T(8,128)S(1)}, u32[]{:S(2)}, u32[]{:S(2)}) collective-permute-start(f32[32,32,128]{2,1,0:T(8,128)} %all_to_all.30.got_ref.ownp_ref), channel_id=1, source_target_pairs={{0,8},{8,0},{16,24},{24,16},{32,40},{40,32},{48,56},{56,48},{64,72... | collective-permute-start | bytes 1572872 | tf_op jit(solution)/shard_map/ppermute | solution.py:509
  128.9 5.3 %collective-permute-start.2 = (f32[16,24,128]{2,1,0:T(8,128)S(1)}, f32[16,24,128]{2,1,0:T(8,128)S(1)}, u32[]{:S(2)}, u32[]{:S(2)}) collective-permute-start(f32[16,24,128]{2,1,0:T(8,128)S(1)} %get-tuple-element.8), channel_id=1, source_target_pairs={{0,8},{8,0},{16,24},{24,16},{32,40},{40,32},{48,56},{56,48},{64,72... | collective-permute-start | bytes 589832 | tf_op jit(solution)/shard_map/ppermute | solution.py:509
  175.3 6.4 %copy-start.8 = (f32[16,24,128]{2,1,0:T(8,128)}, f32[16,24,128]{2,1,0:T(8,128)S(1)}, u32[]{:S(2)}) copy-start(f32[16,24,128]{2,1,0:T(8,128)S(1)} %all_to_all.35.own_ref) | copy-start | bytes 589828
  175.3 6.4 %collective-permute-start.3 = (f32[16,24,128]{2,1,0:T(8,128)S(1)}, f32[16,24,128]{2,1,0:T(8,128)S(1)}, u32[]{:S(2)}, u32[]{:S(2)}) collective-permute-start(f32[16,24,128]{2,1,0:T(8,128)S(1)} %all_to_all.35.own_ref), channel_id=1, source_target_pairs={{0,8},{8,0},{16,24},{24,16},{32,40},{40,32},{48,56},{56,48},{64,72... | collective-permute-start | bytes 589832 | tf_op jit(solution)/shard_map/ppermute | solution.py:509
  181.7 0.7 copy-start.9
Sparse Core Ops, SparseCore 0:
  129.0 47.9 all-gather.1
